TPU v7x, 32 devices: a whole 2x2x4 slice. The times are simulated.
32 devices in a mesh: shard: 4 (over z), ctx: 2 (over x), tensor: 4 (over y, core).
Axes of the slice: x: 2, y: 2, z: 4, core: 2. Of those that a mesh axis runs over, the one named last changes fastest.
Arguments:
- tokens: bfloat16 [8192, 2048], P(('shard', 'ctx')), may hold values from -6 to 6
- cotangent: bfloat16 [8192, 2048], P(('shard', 'ctx')), may hold values from -6 to 6
- seq_len: int32 [4], P('shard'), may hold values from 1024 to 2048
- block_slot: int32 [4, 16], P('shard'), may hold values from 0 to 15, each once within a row
- attn_gain: bfloat16 [2048], P(('shard', 'ctx')), may hold values from 0.099609375 to 1.8984375
- w_query: bfloat16 [2048, 2048], P(('shard', 'ctx'), 'tensor'), may hold values from -0.125 to 0.125
- w_key: bfloat16 [2048, 2048], P(('shard', 'ctx'), 'tensor'), may hold values from -0.125 to 0.125
- w_value: bfloat16 [2048, 2048], P(('shard', 'ctx'), 'tensor'), may hold values from -0.125 to 0.125
- w_out: bfloat16 [2048, 2048], P('tensor', ('shard', 'ctx')), may hold values from -1.5 to 1.5
- mlp_gain: bfloat16 [2048], P(('shard', 'ctx')), may hold values from 0.099609375 to 1.8984375
- w_gate: bfloat16 [2048, 8192], P(('shard', 'ctx'), 'tensor'), may hold values from -0.125 to 0.125
- w_up: bfloat16 [2048, 8192], P(('shard', 'ctx'), 'tensor'), may hold values from -0.125 to 0.125
- w_down: bfloat16 [8192, 2048], P('tensor', ('shard', 'ctx')), may hold values from -0.0625 to 0.0625
Outputs:
- out: bfloat16 [8192, 2048], P(('shard', 'ctx'))
- grad_x: bfloat16 [8192, 2048], P(('shard', 'ctx'))
- grad_attn_gain: float32 [2048], P(('shard', 'ctx'))
- grad_w_query: float32 [2048, 2048], P(('shard', 'ctx'), 'tensor')
- grad_w_key: float32 [2048, 2048], P(('shard', 'ctx'), 'tensor')
- grad_w_value: float32 [2048, 2048], P(('shard', 'ctx'), 'tensor')
- grad_w_out: float32 [2048, 2048], P('tensor', ('shard', 'ctx'))
- grad_mlp_gain: float32 [2048], P(('shard', 'ctx'))
- grad_w_gate: float32 [2048, 8192], P(('shard', 'ctx'), 'tensor')
- grad_w_up: float32 [2048, 8192], P(('shard', 'ctx'), 'tensor')
- grad_w_down: float32 [8192, 2048], P('tensor', ('shard', 'ctx'))
Inputs may be any that keep to these rules, and one draw needn't show every extreme that they name: Rows of a sequence at positions from seq_len on are padding. `block_slot`: each row is a permutation of the sequence's 16 slots; slot j holds rows j * 128 to (j + 1) * 128 - 1 of the sequence.
All inputs are finite; a program needn't handle non-finite values.
Results may differ from a plain program's by a relative error of at most 0.024.
Values may be sent and summed in bfloat16 or wider, within the bound.
A program may use at most 256 MiB of HBM per device.

v0:
```python
import jax
import jax.numpy as jnp
from jax import lax
from jax.sharding import PartitionSpec as P

HDIM = 64
BLK = 128


EPS = 1e-05
THETA = 130000.0
NEG = -1e30


def block_layout(live_len, block_slot, block_len):
    slot_count = block_slot.shape[0]
    order = jnp.arange(slot_count, dtype=jnp.int32)
    placed = (block_slot[:, None] == order[None, :]).astype(jnp.int32)
    slot_within = jnp.sum(placed * order[:, None], axis=0)
    offsets = jnp.arange(block_len, dtype=jnp.int32)
    row_pos = (slot_within[:, None] * block_len + offsets[None, :]).reshape(-1)
    row_live = row_pos < live_len
    return (row_pos, row_live)


def rope_tables(positions, half_dim):
    freqs = THETA ** (-jnp.arange(half_dim, dtype=jnp.float32) / half_dim)
    angles = positions.astype(jnp.float32)[:, None] * freqs[None, :]
    return (jnp.cos(angles), jnp.sin(angles))


def rotate(values, cosines, sines, head_count):
    row_count = values.shape[0]
    paired = values.reshape(row_count, head_count, 2, -1)
    first = paired[:, :, 0]
    second = paired[:, :, 1]
    cos_wide = cosines[:, None]
    sin_wide = sines[:, None]
    turned = jnp.stack(
        [first * cos_wide - second * sin_wide, second * cos_wide + first * sin_wide], axis=2
    )
    return turned.reshape(row_count, -1)


def matmul(left, right):
    return jnp.dot(left, right, preferred_element_type=jnp.float32)


def rms_parts(values):
    scale = lax.rsqrt(jnp.mean(values * values, axis=-1, keepdims=True) + EPS)
    return (scale, values * scale)


def rms_back(grad_out, gain, scale, normed):
    scaled = grad_out * gain
    inner = jnp.mean(scaled * normed, axis=-1, keepdims=True)
    return (scale * (scaled - normed * inner), jnp.sum(grad_out * normed, axis=0))


def tensor_total(partial_value):
    return lax.psum(partial_value.astype(jnp.bfloat16), "tensor").astype(jnp.float32)


def per_device(
    tokens,
    cotangent,
    seq_len,
    block_slot,
    attn_gain,
    w_query,
    w_key,
    w_value,
    w_out,
    mlp_gain,
    w_gate,
    w_up,
    w_down,
):
    row_count = tokens.shape[0]
    head_local = w_query.shape[1] // HDIM
    col_local = head_local * HDIM
    row_pos, row_live = block_layout(seq_len[0], block_slot[0], BLK)
    group_rows = row_pos.shape[0]
    begin = lax.axis_index("ctx") * row_count
    local_pos = lax.dynamic_slice_in_dim(row_pos, begin, row_count)
    cosines, sines = rope_tables(local_pos, HDIM // 2)
    q_rows = min(512, row_count)
    q_blocks = row_count // q_rows
    attn_set = (
        lax.all_gather(attn_gain, ("shard", "ctx"), axis=0, tiled=True),
        lax.all_gather(w_query, ("shard", "ctx"), axis=0, tiled=True),
        lax.all_gather(w_key, ("shard", "ctx"), axis=0, tiled=True),
        lax.all_gather(w_value, ("shard", "ctx"), axis=0, tiled=True),
        lax.all_gather(w_out, ("shard", "ctx"), axis=1, tiled=True),
    )
    inputs = tokens.astype(jnp.float32)
    scale_one, normed_one = rms_parts(inputs)
    n_one = (normed_one * attn_set[0].astype(jnp.float32)).astype(jnp.bfloat16)
    queries = rotate(matmul(n_one, attn_set[1]), cosines, sines, head_local).astype(jnp.bfloat16)
    keys_own = rotate(matmul(n_one, attn_set[2]), cosines, sines, head_local).astype(jnp.bfloat16)
    values_own = matmul(n_one, attn_set[3]).astype(jnp.bfloat16)
    keys_all, values_all = (
        lax.all_gather(keys_own, "ctx", axis=0, tiled=True),
        lax.all_gather(values_own, "ctx", axis=0, tiled=True),
    )
    key_heads = keys_all.reshape(group_rows, head_local, HDIM)
    value_heads = values_all.reshape(group_rows, head_local, HDIM)
    query_heads = queries.reshape(q_blocks, q_rows, head_local, HDIM)
    pos_parts = local_pos.reshape(q_blocks, q_rows)

    def masked_scores(query_part, pos_part):
        raw = (
            jnp.einsum("qhd,khd->hqk", query_part, key_heads, preferred_element_type=jnp.float32)
            * 0.125
        )
        allowed = (row_pos[None, :] <= pos_part[:, None]) & row_live[None, :]
        return jnp.where(allowed[None], raw, NEG)

    def attend(packed):
        query_part, pos_part = packed
        scores = masked_scores(query_part, pos_part)
        row_max = jnp.max(scores, axis=-1, keepdims=True)
        powers = jnp.exp(scores - row_max)
        totals = jnp.sum(powers, axis=-1, keepdims=True)
        attn_prob = (powers / totals).astype(jnp.bfloat16)
        mixed = jnp.einsum(
            "hqk,khd->qhd", attn_prob, value_heads, preferred_element_type=jnp.float32
        )
        return (mixed.astype(jnp.bfloat16).reshape(q_rows, col_local), row_max, totals)

    attn_blocks, maxima, sums_kept = lax.map(attend, (query_heads, pos_parts))
    attn_out = attn_blocks.reshape(row_count, col_local)
    attn_partial = matmul(attn_out, attn_set[4])
    mlp_set = (
        lax.all_gather(mlp_gain, ("shard", "ctx"), axis=0, tiled=True),
        lax.all_gather(w_gate, ("shard", "ctx"), axis=0, tiled=True),
        lax.all_gather(w_up, ("shard", "ctx"), axis=0, tiled=True),
        lax.all_gather(w_down, ("shard", "ctx"), axis=1, tiled=True),
    )
    gain_two_w = mlp_set[0].astype(jnp.float32)
    hidden_res = inputs + tensor_total(attn_partial)
    scale_two, normed_two = rms_parts(hidden_res)
    n_two = (normed_two * gain_two_w).astype(jnp.bfloat16)
    gate_pre = matmul(n_two, mlp_set[1])
    up_proj = matmul(n_two, mlp_set[2])
    gate_sig = jax.nn.sigmoid(gate_pre)
    gate_act = gate_pre * gate_sig
    activated = (gate_act * up_proj).astype(jnp.bfloat16)
    mlp_partial = matmul(activated, mlp_set[3])
    result = (hidden_res + tensor_total(mlp_partial)).astype(jnp.bfloat16)
    grad_top = cotangent.astype(jnp.float32)
    mlp_back = (
        lax.all_gather(mlp_gain, ("shard", "ctx"), axis=0, tiled=True),
        lax.all_gather(w_gate, ("shard", "ctx"), axis=0, tiled=True),
        lax.all_gather(w_up, ("shard", "ctx"), axis=0, tiled=True),
        lax.all_gather(w_down, ("shard", "ctx"), axis=1, tiled=True),
    )
    grad_down = jnp.einsum("tf,td->fd", activated, cotangent, preferred_element_type=jnp.float32)
    grad_act = jnp.einsum("td,fd->tf", cotangent, mlp_back[3], preferred_element_type=jnp.float32)
    grad_gate = (grad_act * up_proj * gate_sig * (1.0 + gate_pre * (1.0 - gate_sig))).astype(
        jnp.bfloat16
    )
    grad_upper = (grad_act * gate_act).astype(jnp.bfloat16)
    grad_wgate = jnp.einsum("td,tf->df", n_two, grad_gate, preferred_element_type=jnp.float32)
    grad_wup = jnp.einsum("td,tf->df", n_two, grad_upper, preferred_element_type=jnp.float32)
    partial_two = jnp.einsum(
        "tf,df->td", grad_gate, mlp_back[1], preferred_element_type=jnp.float32
    ) + jnp.einsum("tf,df->td", grad_upper, mlp_back[2], preferred_element_type=jnp.float32)
    back_gain_two = mlp_back[0].astype(jnp.float32)
    grad_n_two = tensor_total(partial_two)
    grad_res_part, gain_two_part = rms_back(grad_n_two, back_gain_two, scale_two, normed_two)
    grad_res = grad_top + grad_res_part
    grad_res_low = grad_res.astype(jnp.bfloat16)
    attn_back = (
        lax.all_gather(attn_gain, ("shard", "ctx"), axis=0, tiled=True),
        lax.all_gather(w_query, ("shard", "ctx"), axis=0, tiled=True),
        lax.all_gather(w_key, ("shard", "ctx"), axis=0, tiled=True),
        lax.all_gather(w_value, ("shard", "ctx"), axis=0, tiled=True),
        lax.all_gather(w_out, ("shard", "ctx"), axis=1, tiled=True),
    )
    grad_wout = jnp.einsum("tc,td->cd", attn_out, grad_res_low, preferred_element_type=jnp.float32)
    grad_attn = jnp.einsum(
        "td,cd->tc", grad_res_low, attn_back[4], preferred_element_type=jnp.float32
    ).astype(jnp.bfloat16)
    grad_heads = grad_attn.reshape(q_blocks, q_rows, head_local, HDIM)

    def attend_back(carry, packed):
        key_acc, value_acc = carry
        query_part, pos_part, grad_part, row_max, totals = packed
        scores = masked_scores(query_part, pos_part)
        prob_full = jnp.exp(scores - row_max) / totals
        attn_prob = prob_full.astype(jnp.bfloat16)
        grad_prob = jnp.einsum(
            "qhd,khd->hqk", grad_part, value_heads, preferred_element_type=jnp.float32
        )
        delta = jnp.sum(prob_full * grad_prob, axis=-1, keepdims=True)
        grad_scores = (prob_full * grad_prob - prob_full * delta).astype(jnp.bfloat16)
        grad_query = (
            jnp.einsum("hqk,khd->qhd", grad_scores, key_heads, preferred_element_type=jnp.float32)
            * 0.125
        )
        key_term = (
            jnp.einsum("hqk,qhd->khd", grad_scores, query_part, preferred_element_type=jnp.float32)
            * 0.125
        )
        value_term = jnp.einsum(
            "hqk,qhd->khd", attn_prob, grad_part, preferred_element_type=jnp.float32
        )
        key_acc = key_acc + key_term.reshape(group_rows, col_local)
        value_acc = value_acc + value_term.reshape(group_rows, col_local)
        return ((key_acc, value_acc), grad_query.reshape(q_rows, col_local))

    zero_acc = jnp.zeros((group_rows, col_local), jnp.float32)
    (key_grad, value_grad), query_grads = lax.scan(
        attend_back, (zero_acc, zero_acc), (query_heads, pos_parts, grad_heads, maxima, sums_kept)
    )
    key_mine, value_mine = (
        lax.psum_scatter(
            key_grad.astype(jnp.bfloat16), "ctx", scatter_dimension=0, tiled=True
        ).astype(jnp.float32),
        lax.psum_scatter(
            value_grad.astype(jnp.bfloat16), "ctx", scatter_dimension=0, tiled=True
        ).astype(jnp.float32),
    )
    grad_q = rotate(query_grads.reshape(row_count, col_local), cosines, -sines, head_local).astype(
        jnp.bfloat16
    )
    grad_k = rotate(key_mine, cosines, -sines, head_local).astype(jnp.bfloat16)
    grad_v = value_mine.astype(jnp.bfloat16)
    grad_wq = jnp.einsum("td,tc->dc", n_one, grad_q, preferred_element_type=jnp.float32)
    grad_wk = jnp.einsum("td,tc->dc", n_one, grad_k, preferred_element_type=jnp.float32)
    grad_wv = jnp.einsum("td,tc->dc", n_one, grad_v, preferred_element_type=jnp.float32)
    partial_one = jnp.einsum("tc,dc->td", grad_q, attn_back[1], preferred_element_type=jnp.float32)
    partial_one = partial_one + jnp.einsum(
        "tc,dc->td", grad_k, attn_back[2], preferred_element_type=jnp.float32
    )
    partial_one = partial_one + jnp.einsum(
        "tc,dc->td", grad_v, attn_back[3], preferred_element_type=jnp.float32
    )
    back_gain_one = attn_back[0].astype(jnp.float32)
    grad_n_one = tensor_total(partial_one)
    grad_in_part, gain_one_part = rms_back(grad_n_one, back_gain_one, scale_one, normed_one)
    grad_input = (grad_res + grad_in_part).astype(jnp.bfloat16)
    mlp_grads = (
        lax.psum_scatter(
            gain_two_part.astype(jnp.bfloat16), ("shard", "ctx"), scatter_dimension=0, tiled=True
        ).astype(jnp.float32),
        lax.psum_scatter(
            grad_wgate.astype(jnp.bfloat16), ("shard", "ctx"), scatter_dimension=0, tiled=True
        ).astype(jnp.float32),
        lax.psum_scatter(
            grad_wup.astype(jnp.bfloat16), ("shard", "ctx"), scatter_dimension=0, tiled=True
        ).astype(jnp.float32),
        lax.psum_scatter(
            grad_down.astype(jnp.bfloat16), ("shard", "ctx"), scatter_dimension=1, tiled=True
        ).astype(jnp.float32),
    )
    attn_grads = (
        lax.psum_scatter(
            gain_one_part.astype(jnp.bfloat16), ("shard", "ctx"), scatter_dimension=0, tiled=True
        ).astype(jnp.float32),
        lax.psum_scatter(
            grad_wq.astype(jnp.bfloat16), ("shard", "ctx"), scatter_dimension=0, tiled=True
        ).astype(jnp.float32),
        lax.psum_scatter(
            grad_wk.astype(jnp.bfloat16), ("shard", "ctx"), scatter_dimension=0, tiled=True
        ).astype(jnp.float32),
        lax.psum_scatter(
            grad_wv.astype(jnp.bfloat16), ("shard", "ctx"), scatter_dimension=0, tiled=True
        ).astype(jnp.float32),
        lax.psum_scatter(
            grad_wout.astype(jnp.bfloat16), ("shard", "ctx"), scatter_dimension=1, tiled=True
        ).astype(jnp.float32),
    )
    return (
        result,
        grad_input,
        attn_grads[0],
        attn_grads[1],
        attn_grads[2],
        attn_grads[3],
        attn_grads[4],
        mlp_grads[0],
        mlp_grads[1],
        mlp_grads[2],
        mlp_grads[3],
    )


def solution(mesh):
    placed = (
        P(("shard", "ctx"), None),
        P(("shard", "ctx"), None),
        P("shard"),
        P("shard", None),
        P(("shard", "ctx")),
        P(("shard", "ctx"), "tensor"),
        P(("shard", "ctx"), "tensor"),
        P(("shard", "ctx"), "tensor"),
        P("tensor", ("shard", "ctx")),
        P(("shard", "ctx")),
        P(("shard", "ctx"), "tensor"),
        P(("shard", "ctx"), "tensor"),
        P("tensor", ("shard", "ctx")),
    )
    return jax.shard_map(
        per_device,
        mesh=mesh,
        in_specs=placed,
        out_specs=(
            P(("shard", "ctx"), None),
            P(("shard", "ctx"), None),
            P(("shard", "ctx")),
            P(("shard", "ctx"), "tensor"),
            P(("shard", "ctx"), "tensor"),
            P(("shard", "ctx"), "tensor"),
            P("tensor", ("shard", "ctx")),
            P(("shard", "ctx")),
            P(("shard", "ctx"), "tensor"),
            P(("shard", "ctx"), "tensor"),
            P("tensor", ("shard", "ctx")),
        ),
        check_vma=False,
    )
```

profile of v0, /device:TPU:0, one launch (start us, length us, event | category | flops | bytes accessed | tf_op | source)
XLA Modules:
  0.0 2186.3 jit_solution(15445810402795696454)
XLA Ops:
  10.1 22.2 %all-gather = bf16[8,1,256]{2,1,0:T(2,128)(2,1)S(1)} all-gather(bf16[1,1,256]{2,1,0:T(2,128)(2,1)S(1)} %reshape.292), channel_id=1, replica_groups=mesh['shard'=4,'ctx'=2,'tensor'=4] {'shard','ctx'}, dimensions={0}, use_global_device_ids=true | all-gather | bytes 4608 | tf_op jit(solution)/shard_map/all_gather | solution.py:90
  36.3 26.1 %all-gather.18.cloned.1.call-done = bf16[2048,512]{1,0:T(8,128)(2,1)} async-done(((bf16[256,512]{1,0:T(8,128)(2,1)}), bf16[2048,512]{1,0:T(8,128)(2,1)}) %all-gather.18.cloned.1.call-update) | async-done | bytes 2097168 | tf_op jit(solution)/shard_map/all_gather | solution.py:93
  70.0 42.4 %all-gather.14.cloned.1.call-done = bf16[2048,512]{1,0:T(8,128)(2,1)} async-done(((bf16[256,512]{1,0:T(8,128)(2,1)}), bf16[2048,512]{1,0:T(8,128)(2,1)}) %all-gather.14.cloned.1.call-update) | async-done | bytes 2097168 | tf_op jit(solution)/shard_map/all_gather | solution.py:92
  117.7 44.6 %all-gather.12.cloned.1.call-done = bf16[2048,512]{1,0:T(8,128)(2,1)} async-done(((bf16[256,512]{1,0:T(8,128)(2,1)}), bf16[2048,512]{1,0:T(8,128)(2,1)}) %all-gather.12.cloned.1.call-update) | async-done | bytes 2097168 | tf_op jit(solution)/shard_map/all_gather | solution.py:91
  173.5 22.4 %all-gather.20.cloned.1.call-done = bf16[2048,512]{1,0:T(8,128)(2,1)} async-done(((bf16[1024,512]{1,0:T(8,128)(2,1)}), bf16[2048,512]{1,0:T(8,128)(2,1)}) %all-gather.20.cloned.1.call-update) | async-done | bytes 2097168 | tf_op jit(solution)/shard_map/all_gather | solution.py:104
  199.8 31.2 %all-gather.16.cloned.1.call-done = bf16[2048,512]{0,1:T(8,128)(2,1)} async-done(((bf16[1024,512]{0,1:T(8,128)(2,1)}), bf16[2048,512]{0,1:T(8,128)(2,1)}) %all-gather.16.cloned.1.call-update) | async-done | bytes 2097168 | tf_op jit(solution)/shard_map/all_gather | solution.py:103
  231.0 96.1 %while.33 = (s32[]{:T(128)}, bf16[2,512,512]{2,1,0:T(8,128)(2,1)}, f32[2,8,512,1]{2,1,3,0:T(8,128)S(1)}, f32[2,8,512,1]{2,1,3,0:T(8,128)S(1)}, s32[2,512]{1,0:T(...) while((s32[]{:T(128)}, bf16[2,512,512]{2,1,0:T(8,128)(2,1)}, ...), condition=%wide.region_5.6_spmd.clone.clone, body=%wide.region_2.5_spmd.clone.clone.sunk | while | flops 2250504192 | bytes 112371968 | solution.py:131
  336.0 20.1 all-gather.1
  356.1 63.5 %all-reduce.8.cloned.1.call-done = bf16[1024,2048]{1,0:T(8,128)(2,1)} async-done(((bf16[1024,2048]{1,0:T(8,128)(2,1)}), bf16[1024,2048]{1,0:T(8,128)(2,1)}) %all-reduce.8.cloned.1.call-update) | async-done | bytes 4194320 | tf_op jit(solution)/shard_map/psum | solution.py:61
  429.6 117.5 %all-gather.26.cloned.1.call-done = bf16[2048,2048]{1,0:T(8,128)(2,1)} async-done(((bf16[256,2048]{1,0:T(8,128)(2,1)}), bf16[2048,2048]{1,0:T(8,128)(2,1)}) %all-gather.26.cloned.1.call-update) | async-done | bytes 8388624 | tf_op jit(solution)/shard_map/all_gather | solution.py:137
  561.5 111.1 %all-gather.24.cloned.1.call-done = bf16[2048,2048]{1,0:T(8,128)(2,1)} async-done(((bf16[256,2048]{1,0:T(8,128)(2,1)}), bf16[2048,2048]{1,0:T(8,128)(2,1)}) %all-gather.24.cloned.1.call-update) | async-done | bytes 8388624 | tf_op jit(solution)/shard_map/all_gather | solution.py:136
  687.0 111.3 %all-gather.28.cloned.1.call-done = bf16[2048,2048]{1,0:T(8,128)(2,1)} async-done(((bf16[2048,256]{1,0:T(8,128)(2,1)}), bf16[2048,2048]{1,0:T(8,128)(2,1)}) %all-gather.28.cloned.1.call-update) | async-done | bytes 8388624 | tf_op jit(solution)/shard_map/all_gather | solution.py:138
  798.3 22.1 %multiply_convert_fusion = (bf16[1024,2048]{1,0:T(8,128)(2,1)}, bf16[1024,2048]{1,0:T(8,128)(2,1)}, bf16[1024,2048]{1,0:T(8,128)(2,1)}) fusion(f32[1024,2048]{1,0:T(8,128)} %fusion.75, f32[1024,2048]{1,0:T(8,128)} %fusion.76, bf16[1024,2048]{1,0:T(8,128)(2,1)} %param.18, bf16[2048,2048]{1,0:T(8,128)(2,1)} %all-gather.28.cloned.1.call-done), kind=kOutput, calls=%fused_computation.78 | convolution fusion | flops 8621391872 | bytes 41943040 | tf_op jit(solution)/shard_map/td,fd->tf/dot_general | solution.py:159
  846.3 83.5 %all-reduce.10.cloned.1.call-done = bf16[1024,2048]{1,0:T(8,128)(2,1)} async-done(((bf16[1024,2048]{1,0:T(8,128)(2,1)}), bf16[1024,2048]{1,0:T(8,128)(2,1)}) %all-reduce.10.cloned.1.call-update) | async-done | bytes 4194320 | tf_op jit(solution)/shard_map/psum | solution.py:61
  955.2 255.5 %while.34 = (s32[]{:T(128)}, f32[2048,512]{0,1:T(8,128)}, f32[2048,512]{0,1:T(8,128)}, f32[2,512,512]{1,0,2:T(2,128)}, bf16[2,512,8,64]{1,3,2,0:T(8,128)(2,1)}, ...) while((s32[]{:T(128)}, f32[2048,512]{0,1:T(8,128)}, ...), condition=%wide.region_13.14_spmd.clone.clone.clone, body=%wide.region_11.13_spmd.clone.clone.clone.sunk | while | flops 6559123456 | bytes 261746032 | solution.py:214
  957.2 16.8 exponential_divide_fusion.2
  974.1 30.7 %convolution_multiply_fusion.6 = f32[8,512,64]{1,2,0:T(8,128)} fusion(bf16[2048,8,64]{0,2,1:T(8,128)(2,1)S(1)} %get-tuple-element.705, f32[8,512,2048]{2,1,0:T(8,128)} %exponential_divide_fusion.2, bf16[2048,8,64]{0,2,1:T(8,128)(2,1)} %get-tuple-element.709, bf16[2,512,8,64]{1,3,2,0:T(8,128)(2,1)S(1)} %get-tuple-element.708, s32[]{:T(128)S(6)} %copy.86), kind=kOutput, calls=%fused_computation.34.clone.1 | convolution fusion | flops 2181306368 | bytes 72876032 | tf_op jit(solution)/shard_map/while/body/eval_jaxpr/hqk,khd->qhd/dot_general | solution.py:199
  1007.1 19.5 dynamic_update_slice.32
  1026.6 30.2 %convolution_multiply_fusion.5 = f32[8,64,2048]{2,1,0:T(8,128)} fusion(bf16[2,512,8,64]{1,3,2,0:T(8,128)(2,1)} %get-tuple-element.703, s32[]{:T(128)S(6)} %copy.86, f32[8,512,2048]{2,1,0:T(8,128)} %exponential_divide_fusion.2, bf16[2048,8,64]{0,2,1:T(8,128)(2,1)} %get-tuple-element.709, bf16[2,512,8,64]{1,3,2,0:T(8,128)(2,1)} %copy-done.8), kind=kOutput, calls=%fused_computation.33.clone.1 | convolution fusion | flops 2182092800 | bytes 74449920 | tf_op jit(solution)/shard_map/while/body/eval_jaxpr/hqk,qhd->khd/dot_general | solution.py:203
  1100.3 30.7 %convolution_multiply_fusion.6 = f32[8,512,64]{1,2,0:T(8,128)} fusion(bf16[2048,8,64]{0,2,1:T(8,128)(2,1)S(1)} %get-tuple-element.705, f32[8,512,2048]{2,1,0:T(8,128)} %exponential_divide_fusion.2, bf16[2048,8,64]{0,2,1:T(8,128)(2,1)} %get-tuple-element.709, bf16[2,512,8,64]{1,3,2,0:T(8,128)(2,1)S(1)} %get-tuple-element.708, s32[]{:T(128)S(6)} %copy.86), kind=kOutput, calls=%fused_computation.34.clone.1 | convolution fusion | flops 2181306368 | bytes 72876032 | tf_op jit(solution)/shard_map/while/body/eval_jaxpr/hqk,khd->qhd/dot_general | solution.py:199
  1133.4 19.5 dynamic_update_slice.32
  1152.9 30.3 %convolution_multiply_fusion.5 = f32[8,64,2048]{2,1,0:T(8,128)} fusion(bf16[2,512,8,64]{1,3,2,0:T(8,128)(2,1)} %get-tuple-element.703, s32[]{:T(128)S(6)} %copy.86, f32[8,512,2048]{2,1,0:T(8,128)} %exponential_divide_fusion.2, bf16[2048,8,64]{0,2,1:T(8,128)(2,1)} %get-tuple-element.709, bf16[2,512,8,64]{1,3,2,0:T(8,128)(2,1)} %copy-done.8), kind=kOutput, calls=%fused_computation.33.clone.1 | convolution fusion | flops 2182092800 | bytes 74449920 | tf_op jit(solution)/shard_map/while/body/eval_jaxpr/hqk,qhd->khd/dot_general | solution.py:203
  1229.7 17.1 reduce-scatter.10.cloned.1.call-done
  1262.0 19.6 reduce-scatter.12.cloned.1.call-done
  1359.7 64.1 %reduce-scatter.16.cloned.1.call-done = bf16[256,512]{1,0:T(8,128)(2,1)} async-done(((bf16[2048,512]{1,0:T(8,128)(2,1)}), bf16[256,512]{1,0:T(8,128)(2,1)}) %reduce-scatter.16.cloned.1.call-update) | async-done | bytes 262160 | tf_op jit(solution)/shard_map/reduce_scatter | solution.py:265
  1425.6 69.1 %reduce-scatter.14.cloned.1.call-done = bf16[256,512]{1,0:T(8,128)(2,1)} async-done(((bf16[2048,512]{1,0:T(8,128)(2,1)}), bf16[256,512]{1,0:T(8,128)(2,1)}) %reduce-scatter.14.cloned.1.call-update) | async-done | bytes 262160 | tf_op jit(solution)/shard_map/reduce_scatter | solution.py:262
  1496.6 69.0 %reduce-scatter.18.cloned.1.call-done = bf16[256,512]{1,0:T(8,128)(2,1)} async-done(((bf16[2048,512]{1,0:T(8,128)(2,1)}), bf16[256,512]{1,0:T(8,128)(2,1)}) %reduce-scatter.18.cloned.1.call-update) | async-done | bytes 262160 | tf_op jit(solution)/shard_map/reduce_scatter | solution.py:268
  1567.3 152.9 %all-reduce.12.cloned.1.call-done = (bf16[1024,2048]{1,0:T(8,128)(2,1)}, bf16[1024,2048]{1,0:T(8,128)(2,1)}) async-done(((bf16[1024,2048]{1,0:T(8,128)(2,1)}, bf16[1024,2048]{1,0:T(8,128)(2,1)}), (bf16[1024,2048]{1,0:T(8,128)(2,1)}, bf16[1024,2048]{1,0:T(8,128)(2,1)})) %all-reduce.12.cloned.1.call-update) | async-done | bytes 8388624 | tf_op jit(solution)/shard_map/psum | solution.py:61
  1725.2 22.6 %all-reduce.2 = (bf16[2048]{0:T(1024)(128)(2,1)S(1)}, bf16[2048]{0:T(1024)(128)(2,1)S(1)}) all-reduce(bf16[2048]{0:T(1024)(128)(2,1)S(1)} %get-tuple-element.402, bf16[2048]{0:T(1024)(128)(2,1)S(1)} %copy-done.22), channel_id=4, replica_groups=mesh['shard'=4,'ctx'=2,'tensor'=4] {'shard','ctx'}, use_global_device_ids=true, to_apply=%region_19.20.clone | all-reduce | flops 4096 | bytes 16384
  1762.7 110.2 %reduce-scatter.26.cloned.1.call-done = bf16[2048,256]{1,0:T(8,128)(2,1)} async-done(((bf16[2048,2048]{1,0:T(8,128)(2,1)}), bf16[2048,256]{1,0:T(8,128)(2,1)}) %reduce-scatter.26.cloned.1.call-update) | async-done | bytes 1048592 | tf_op jit(solution)/shard_map/reduce_scatter | solution.py:254
  1875.6 149.2 %reduce-scatter.24.cloned.1.call-done = bf16[256,2048]{1,0:T(8,128)(2,1)} async-done(((bf16[2048,2048]{1,0:T(8,128)(2,1)}), bf16[256,2048]{1,0:T(8,128)(2,1)}) %reduce-scatter.24.cloned.1.call-update) | async-done | bytes 1048592 | tf_op jit(solution)/shard_map/reduce_scatter | solution.py:251
  2027.6 148.9 %reduce-scatter.22.cloned.1.call-done = bf16[256,2048]{1,0:T(8,128)(2,1)} async-done(((bf16[2048,2048]{1,0:T(8,128)(2,1)}), bf16[256,2048]{1,0:T(8,128)(2,1)}) %reduce-scatter.22.cloned.1.call-update) | async-done | bytes 1048592 | tf_op jit(solution)/shard_map/reduce_scatter | solution.py:248
  (217 shorter events, 451.3 us)
Async XLA Ops:
  7.2 55.3 %all-gather.18.cloned.1.call-start = ((), (), s32[]{:S(2)}) async-start(), calls=%async_computation.12 | async-start | bytes 2359296 | tf_op jit(solution)/shard_map/all_gather | solution.py:93
  7.9 104.5 %all-gather.14.cloned.1.call-start = ((), (), s32[]{:S(2)}) async-start(), calls=%async_computation.10 | async-start | bytes 2359296 | tf_op jit(solution)/shard_map/all_gather | solution.py:92
  8.7 153.7 %all-gather.12.cloned.1.call-start = ((), (), s32[]{:S(2)}) async-start(), calls=%async_computation.9 | async-start | bytes 2359296 | tf_op jit(solution)/shard_map/all_gather | solution.py:91
  9.4 186.5 %all-gather.20.cloned.1.call-start = ((), (), s32[]{:S(2)}) async-start(), calls=%async_computation.13 | async-start | bytes 3145728 | tf_op jit(solution)/shard_map/all_gather | solution.py:104
  32.4 130.0 %copy-start.18 = (f32[8,1,256]{2,1,0:T(1,128)}, f32[8,1,256]{2,1,0:T(1,128)S(1)}, u32[]{:S(2)}) copy-start(f32[8,1,256]{2,1,0:T(1,128)S(1)} %convert_element_type.214) | copy-start | bytes 24580
  36.3 126.0 %copy-start.20 = (f32[1024]{0:T(1024)}, f32[1024]{0:T(1024)S(1)}, u32[]{:S(2)}) copy-start(f32[1024]{0:T(1024)S(1)} %add_rsqrt_fusion.1) | copy-start | bytes 12292
  68.7 162.4 %all-gather.16.cloned.1.call-start = ((), (), s32[]{:S(2)}) async-start(), calls=%async_computation.11 | async-start | bytes 3145728 | tf_op jit(solution)/shard_map/all_gather | solution.py:103
  70.0 97.7 %copy-start.12 = (f32[1024,32]{0,1:T(8,128)}, f32[1024,32]{0,1:T(8,128)S(1)}, u32[]{:S(2)}) copy-start(f32[1024,32]{0,1:T(8,128)S(1)} %get-tuple-element.481) | copy-start | bytes 393220
  169.4 157.8 %all-gather.22.cloned.1.call-start = ((), (), s32[]{:S(2)}) async-start(), calls=%async_computation.14 | async-start | bytes 2359296 | tf_op jit(solution)/shard_map/all_gather | solution.py:94
  170.0 249.6 %all-reduce.8.cloned.1.call-start = ((), (), s32[]{:S(2)}) async-start(), calls=%async_computation.15 | async-start | bytes 8388608 | tf_op jit(solution)/shard_map/psum | solution.py:61
  333.9 213.2 %all-gather.26.cloned.1.call-start = ((), (), s32[]{:S(2)}) async-start(), calls=%async_computation.17 | async-start | bytes 9437184 | tf_op jit(solution)/shard_map/all_gather | solution.py:137
  334.6 337.9 %all-gather.24.cloned.1.call-start = ((), (), s32[]{:S(2)}) async-start(), calls=%async_computation.16 | async-start | bytes 9437184 | tf_op jit(solution)/shard_map/all_gather | solution.py:136
  335.4 462.9 %all-gather.28.cloned.1.call-start = ((), (), s32[]{:S(2)}) async-start(), calls=%async_computation.18 | async-start | bytes 9437184 | tf_op jit(solution)/shard_map/all_gather | solution.py:138
  335.9 593.9 %all-reduce.10.cloned.1.call-start = ((), (), s32[]{:S(2)}) async-start(), calls=%async_computation.19 | async-start | bytes 8388608 | tf_op jit(solution)/shard_map/psum | solution.py:61
  846.0 400.8 %reduce-scatter.10.cloned.1.call-start = ((), (), s32[]{:S(2)}) async-start(), calls=%async_computation.20 | async-start | bytes 3145728 | tf_op jit(solution)/shard_map/reduce_scatter | solution.py:218
  955.6 18.4 copy-start.8
  1026.6 30.2 %copy-start.9 = (bf16[2,512,8,64]{1,3,2,0:T(8,128)(2,1)S(1)}, bf16[2,512,8,64]{1,3,2,0:T(8,128)(2,1)}, u32[]{:S(2)}) copy-start(bf16[2,512,8,64]{1,3,2,0:T(8,128)(2,1)} %copy-done.8) | copy-start | bytes 3145732 | tf_op jit(solution)/shard_map/while
  1152.9 30.3 %copy-start.9 = (bf16[2,512,8,64]{1,3,2,0:T(8,128)(2,1)S(1)}, bf16[2,512,8,64]{1,3,2,0:T(8,128)(2,1)}, u32[]{:S(2)}) copy-start(bf16[2,512,8,64]{1,3,2,0:T(8,128)(2,1)} %copy-done.8) | copy-start | bytes 3145732 | tf_op jit(solution)/shard_map/while
  1214.7 66.9 %reduce-scatter.12.cloned.1.call-start = ((), (), s32[]{:S(2)}) async-start(), calls=%async_computation.21 | async-start | bytes 3145728 | tf_op jit(solution)/shard_map/reduce_scatter | solution.py:221
  1218.6 29.8 %copy-start.13 = (f32[1024,32]{0,1:T(8,128)S(1)}, f32[1024,32]{0,1:T(8,128)}, u32[]{:S(2)}) copy-start(f32[1024,32]{0,1:T(8,128)} %copy-done.12) | copy-start | bytes 393220
  1218.6 29.8 %copy-start.17 = (f32[1024,32]{0,1:T(8,128)S(1)}, f32[1024,32]{0,1:T(8,128)}, u32[]{:S(2)}) copy-start(f32[1024,32]{0,1:T(8,128)} %get-tuple-element.479) | copy-start | bytes 393220
  1218.6 139.3 %reduce-scatter.20.cloned.1.call-start = ((), (), s32[]{:S(2)}) async-start(), calls=%async_computation.25 | async-start | bytes 2359296 | tf_op jit(solution)/shard_map/reduce_scatter | solution.py:271
  1226.5 197.3 %reduce-scatter.16.cloned.1.call-start = ((), (), s32[]{:S(2)}) async-start(), calls=%async_computation.23 | async-start | bytes 2359296 | tf_op jit(solution)/shard_map/reduce_scatter | solution.py:265
  1226.6 23.8 %copy-start.19 = (f32[8,1,256]{2,1,0:T(1,128)S(1)}, f32[8,1,256]{2,1,0:T(1,128)}, u32[]{:S(2)}) copy-start(f32[8,1,256]{2,1,0:T(1,128)} %copy-done.18) | copy-start | bytes 24580
  1226.6 23.8 %copy-start.21 = (f32[1024]{0:T(1024)S(1)}, f32[1024]{0:T(1024)}, u32[]{:S(2)}) copy-start(f32[1024]{0:T(1024)} %copy-done.20) | copy-start | bytes 12292
  1254.6 240.2 %reduce-scatter.14.cloned.1.call-start = ((), (), s32[]{:S(2)}) async-start(), calls=%async_computation.22 | async-start | bytes 2359296 | tf_op jit(solution)/shard_map/reduce_scatter | solution.py:262
  1261.7 303.8 %reduce-scatter.18.cloned.1.call-start = ((), (), s32[]{:S(2)}) async-start(), calls=%async_computation.24 | async-start | bytes 2359296 | tf_op jit(solution)/shard_map/reduce_scatter | solution.py:268
  1288.3 431.9 %all-reduce.12.cloned.1.call-start = ((), (), s32[]{:S(2)}) async-start(), calls=%async_computation.29 | async-start | bytes 16777216 | tf_op jit(solution)/shard_map/psum | solution.py:61
  1312.9 560.0 %reduce-scatter.26.cloned.1.call-start = ((), (), s32[]{:S(2)}) async-start(), calls=%async_computation.28 | async-start | bytes 9437184 | tf_op jit(solution)/shard_map/reduce_scatter | solution.py:254
  1327.6 697.3 %reduce-scatter.24.cloned.1.call-start = ((), (), s32[]{:S(2)}) async-start(), calls=%async_computation.27 | async-start | bytes 9437184 | tf_op jit(solution)/shard_map/reduce_scatter | solution.py:251
  1341.8 834.7 %reduce-scatter.22.cloned.1.call-start = ((), (), s32[]{:S(2)}) async-start(), calls=%async_computation.26 | async-start | bytes 9437184 | tf_op jit(solution)/shard_map/reduce_scatter | solution.py:248
  1356.0 369.2 %copy-start.22 = (bf16[2048]{0:T(1024)(128)(2,1)S(1)}, bf16[2048]{0:T(1024)(128)(2,1)}, u32[]{:S(2)}) copy-start(bf16[2048]{0:T(1024)(128)(2,1)} %get-tuple-element.400) | copy-start | bytes 12292
  (20 other events, 137.9 us)
Sparse Core Ops, SparseCore 0:
  10.1 52.2 all-gather.17
  64.6 47.7 all-gather.13
  114.5 47.7 all-gather.11
  164.3 31.5 all-gather.19
  197.9 33.1 all-gather.15
  232.9 51.0 all-gather.21
  334.0 85.6 all-reduce.7
  422.0 125.0 all-gather.25
  549.4 123.1 all-gather.23
  674.7 123.5 all-gather.27
  846.1 83.6 all-reduce.9
  1214.8 31.9 reduce-scatter.9
  1249.7 31.8 reduce-scatter.11
  1285.0 67.9 reduce-scatter.19
  1357.0 66.8 reduce-scatter.15
  1427.8 66.9 reduce-scatter.13
  1498.7 66.7 reduce-scatter.17
  1568.0 152.2 all-reduce.11
  1723.9 149.0 reduce-scatter.25
  1876.8 147.9 reduce-scatter.23
  2028.5 147.9 reduce-scatter.21
where the time goes:
time: 2200 us; the launch traced here: 2190 us
  waiting for transfers between devices  1460 us (66%)
  matrix products  443 us (20%)
  other arithmetic  134 us (6%)
  local copies, waits for them, and re-layouts  67.5 us (3%)
  blocking collectives  64.9 us (3%)
    psum x3, waiting for transfers between devices, tensor_total(): lax.psum(partial_value.astype(jnp.bfloat16), 'tensor').astype(jnp.float32)  300 us
    reduce_scatter x1, waiting for transfers between devices, per_device(): lax.psum_scatter(grad_wup.astype(jnp.bfloat16), ('shard', 'ctx'), scatter...  149 us
    reduce_scatter x1, waiting for transfers between devices, per_device(): lax.psum_scatter(grad_wgate.astype(jnp.bfloat16), ('shard', 'ctx'), scatt...  149 us
    all_gather x1, waiting for transfers between devices, per_device(): lax.all_gather(w_up, ('shard', 'ctx'), axis=0, tiled=True)  118 us
    all_gather x1, waiting for transfers between devices, per_device(): lax.all_gather(w_down, ('shard', 'ctx'), axis=1, tiled=True)  111 us
    all_gather x1, waiting for transfers between devices, per_device(): lax.all_gather(w_gate, ('shard', 'ctx'), axis=0, tiled=True)  111 us
    reduce_scatter x1, waiting for transfers between devices, per_device(): lax.psum_scatter(grad_down.astype(jnp.bfloat16), ('shard', 'ctx'), scatte...  110 us
    reduce_scatter x1, waiting for transfers between devices, per_device(): lax.psum_scatter(grad_wq.astype(jnp.bfloat16), ('shard', 'ctx'), scatter_...  69.1 us
  transfers between devices with their start and end apart: 21, of which 19 were waited for; matrix products, arithmetic and copies ran while one was open for 14% of the time, Pallas kernels for 0%

commit v1 on v0

v1 whole, which is shorter than its diff:
```python
import functools

import jax
import jax.numpy as jnp
from jax import lax
from jax.experimental import pallas as pl
from jax.experimental.pallas import tpu as pltpu
from jax.sharding import PartitionSpec as P

HDIM = 64
BLK = 128
EPS = 1e-05
THETA = 130000.0
NEG = -1e30
LEVEL = ("ctx", "tensor")
BF = jnp.bfloat16
F32 = jnp.float32
QT = 512

NT = (((1,), (1,)), ((), ()))
TN = (((0,), (0,)), ((), ()))


def mm(left, right, dims=None):
    if dims is None:
        return jnp.dot(left, right, preferred_element_type=F32)
    return lax.dot_general(left, right, dims, preferred_element_type=F32)


def swap(value, group, bit):
    return lax.ppermute(value, LEVEL, [(i, i ^ bit) for i in range(group)])


def level_bits(ctx, tensor):
    bits_y = []
    bit = 2
    while bit < tensor:
        bits_y.append(bit)
        bit *= 2
    bits_x = []
    bit = tensor
    while bit < ctx * tensor:
        bits_x.append(bit)
        bit *= 2
    return bits_y, bits_x


def level_gather(block, ctx, tensor, axis=0):
    group = ctx * tensor
    bits_y, bits_x = level_bits(ctx, tensor)
    half = block.shape[axis] // 2
    whole = {0: block, 1: swap(block, group, 1)}
    parts = [lax.slice_in_dim(block, 0, half, axis=axis), lax.slice_in_dim(block, half, 2 * half, axis=axis)]
    found = [{0: parts[0]}, {0: parts[1]}]
    for which, order in enumerate((bits_x + bits_y, bits_y + bits_x)):
        have = [(0, parts[which])]
        for bit in order:
            sent = jnp.concatenate([v for _, v in have], axis=axis) if len(have) > 1 else have[0][1]
            got = swap(sent, group, bit)
            core = swap(got, group, 1)
            new = []
            for i, (k, _) in enumerate(have):
                piece = lax.slice_in_dim(got, i * half, (i + 1) * half, axis=axis)
                new.append((k | bit, piece))
                found[which][k | bit] = piece
                found[which][k | bit | 1] = lax.slice_in_dim(core, i * half, (i + 1) * half, axis=axis)
            have = have + new
    out = []
    for k in range(group):
        if k in whole:
            out.append(whole[k])
        else:
            out.append(jnp.concatenate([found[0][k], found[1][k]], axis=axis))
    return out


def plus(a, b):
    return (a.astype(F32) + b.astype(F32)).astype(BF)


def level_sum(blocks, ctx, tensor):
    group = ctx * tensor
    bits_y, bits_x = level_bits(ctx, tensor)
    rows = blocks[0].shape[0]
    half = rows // 2
    evens = list(range(0, group, 2))
    got = swap(jnp.concatenate([blocks[k | 1] for k in evens], axis=0), group, 1)
    chip = {k: plus(blocks[k], got[i * rows : (i + 1) * rows]) for i, k in enumerate(evens)}
    done = []
    for which, order in enumerate((bits_x + bits_y, bits_y + bits_x)):
        have = {k: v[which * half : (which + 1) * half] for k, v in chip.items()}
        for bit in order:
            leave = sorted(k for k in have if k & bit)
            got = swap(jnp.concatenate([have[k] for k in leave], axis=0), group, bit)
            for i, k in enumerate(leave):
                piece = got[i * half : (i + 1) * half]
                own = have[k ^ bit]
                have[k ^ bit] = plus(own, piece) if len(leave) > 1 else own.astype(F32) + piece.astype(F32)
                del have[k]
        done.append(have[0])
    return jnp.concatenate(done, axis=0)


def level_exchange(blocks, group):
    return [blocks[0]] + [swap(blocks[k], group, k) for k in range(1, group)]


def chain_gather(own, shards):
    here = lax.axis_index("shard")
    ups, downs = [], []
    up = down = own
    for k in range(1, shards):
        up = lax.ppermute(up, "shard", [(i, i + 1) for i in range(k - 1, shards - 1)])
        down = lax.ppermute(down, "shard", [(i, i - 1) for i in range(1, shards - k + 1)])
        ups.append(up)
        downs.append(down)
    rel = [own]
    for k in range(1, shards):
        rel.append(jnp.where(here >= k, ups[k - 1], downs[shards - k - 1]))
    return rel


def in_order(rel, shards):
    here = lax.axis_index("shard")
    order = (here - jnp.arange(shards)) % shards
    return jnp.take(jnp.stack(rel, axis=0), order, axis=0)


def chain_sum(terms, shards):
    here = lax.axis_index("shard")

    def term(index):
        return lax.dynamic_index_in_dim(terms, jnp.clip(index, 0, shards - 1), 0, keepdims=False)

    up = down = None
    for k in range(1, shards):
        send = term(here + shards - k)
        send = send if up is None else plus(send, up)
        up = lax.ppermute(send, "shard", [(i, i + 1) for i in range(0, k)])
        send = term(here - (shards - k))
        send = send if down is None else plus(send, down)
        down = lax.ppermute(send, "shard", [(i, i - 1) for i in range(shards - k, shards)])
    return term(here).astype(F32) + up.astype(F32) + down.astype(F32)


def qkv_kernel(tok_ref, gain_ref, w_ref, n_ref, out_ref):
    x = tok_ref[...].astype(F32)
    scale = lax.rsqrt(jnp.mean(x * x, axis=-1, keepdims=True) + EPS)
    n = (x * scale * gain_ref[...]).astype(BF)
    n_ref[...] = n
    out_ref[...] = mm(n, w_ref[...])


def qkv_call(tok, gain, weights):
    rows, width = tok.shape
    cols = weights.shape[1]
    tile = 256
    return pl.pallas_call(
        qkv_kernel,
        grid=(rows // tile,),
        in_specs=[
            pl.BlockSpec((tile, width), lambda i: (i, 0)),
            pl.BlockSpec((1, width), lambda i: (0, 0)),
            pl.BlockSpec((width, cols), lambda i: (0, 0)),
        ],
        out_specs=[
            pl.BlockSpec((tile, width), lambda i: (i, 0)),
            pl.BlockSpec((tile, cols), lambda i: (i, 0)),
        ],
        out_shape=[
            jax.ShapeDtypeStruct((rows, width), BF),
            jax.ShapeDtypeStruct((rows, cols), F32),
        ],
        compiler_params=pltpu.CompilerParams(vmem_limit_bytes=48 * 1024 * 1024),
        cost_estimate=pl.CostEstimate(
            flops=2 * rows * width * cols, bytes_accessed=rows * width * 4 + rows * cols * 4 + width * cols * 2, transcendentals=0
        ),
        name="norm_qkv",
    )(tok, gain, weights)


def turn(u, cos, sin):
    lane = lax.broadcasted_iota(jnp.int32, u.shape, 1)
    width = u.shape[1]
    ahead = pltpu.roll(u, width - HDIM // 2, axis=1)
    behind = pltpu.roll(u, HDIM // 2, axis=1)
    other = jnp.where(lane % HDIM < HDIM // 2, ahead, behind)
    return u * cos + other * sin


def wide(table, cols):
    reps = cols // table.shape[1]
    return jnp.concatenate([table] * reps, axis=1) if reps > 1 else table


def attend_kernel(slots, lin_ref, cos_ref, sin_ref, o_slot, qs, ks, vs, os, stats):
    rows, cols = qs.shape
    heads = cols // HDIM

    def fill(b, carry):
        src = pl.ds(pl.multiple_of(slots[b] * BLK, BLK), BLK)
        dst = pl.ds(pl.multiple_of(b * BLK, BLK), BLK)
        cos = wide(cos_ref[dst, :], cols)
        sin = wide(sin_ref[dst, :], cols)
        qs[dst, :] = turn(lin_ref[src, 0:cols], cos, sin).astype(BF)
        ks[dst, :] = turn(lin_ref[src, cols : 2 * cols], cos, sin).astype(BF)
        vs[dst, :] = lin_ref[src, 2 * cols : 3 * cols].astype(BF)
        return carry

    lax.fori_loop(0, rows // BLK, fill, 0)
    live = slots[rows // BLK]
    tiles = rows // QT
    for t in range(tiles):
        ext = (t + 1) * QT
        lane = lax.broadcasted_iota(jnp.int32, (QT, cols), 1) // HDIM
        qpos = lax.broadcasted_iota(jnp.int32, (QT, QT), 0)
        kpos = lax.broadcasted_iota(jnp.int32, (QT, QT), 1)
        diag = jnp.where(kpos <= qpos, 0.0, NEG)
        dead = jnp.where(lax.broadcasted_iota(jnp.int32, (1, ext), 1) < live, 0.0, NEG)

        def head(h, acc):
            q = jnp.where(lane == h, qs[t * QT : ext, :] * BF(0.125), BF(0))
            s = mm(q, ks[0:ext, :], NT) + dead
            last = s[:, t * QT :] + diag
            s = jnp.concatenate([s[:, : t * QT], last], axis=1) if t else last
            top = jnp.max(s, axis=1, keepdims=True)
            p = jnp.exp(s - top)
            total = jnp.sum(p, axis=1, keepdims=True)
            mixed = mm(p.astype(BF), vs[0:ext, :]) / total
            note = jnp.broadcast_to(top + jnp.log(total), (QT, 128))
            stats[pl.ds(h, 1), t * QT : ext] = jnp.transpose(note)[0:1, :]
            return jnp.where(lane == h, mixed, acc)

        acc = lax.fori_loop(0, heads, head, jnp.zeros((QT, cols), F32))
        out = acc.astype(BF)
        os[t * QT : ext, :] = out
        for i in range(QT // BLK):
            dst = pl.ds(pl.multiple_of(slots[t * (QT // BLK) + i] * BLK, BLK), BLK)
            o_slot[dst, :] = out[i * BLK : (i + 1) * BLK, :]


def full_spec(shape):
    return pl.BlockSpec(shape, lambda *_: (0,) * len(shape))


def attend_call(slots, lin, cos, sin):
    rows = lin.shape[0]
    cols = lin.shape[1] // 3
    heads = cols // HDIM
    piece = jax.ShapeDtypeStruct((rows, cols), BF)
    return pl.pallas_call(
        attend_kernel,
        grid_spec=pltpu.PrefetchScalarGridSpec(
            num_scalar_prefetch=1,
            grid=(1,),
            in_specs=[full_spec(lin.shape), full_spec(cos.shape), full_spec(sin.shape)],
            out_specs=[full_spec((rows, cols))] * 5 + [full_spec((8, rows))],
        ),
        out_shape=[piece] * 5 + [jax.ShapeDtypeStruct((8, rows), F32)],
        compiler_params=pltpu.CompilerParams(vmem_limit_bytes=56 * 1024 * 1024),
        cost_estimate=pl.CostEstimate(
            flops=heads * rows * rows * HDIM * 8, bytes_accessed=rows * cols * 22, transcendentals=heads * rows * rows // 2
        ),
        name="attend",
    )(slots, lin, cos, sin)


def attend_back_kernel(slots, qs, ks, vs, os, stats, go_ref, cos_ref, sin_ref, out_ref, go, delta, dq):
    rows, cols = qs.shape
    heads = cols // HDIM

    def fill(b, carry):
        src = pl.ds(pl.multiple_of(slots[b] * BLK, BLK), BLK)
        dst = pl.ds(pl.multiple_of(b * BLK, BLK), BLK)
        go[dst, :] = go_ref[src, :]
        return carry

    lax.fori_loop(0, rows // BLK, fill, 0)
    pick = (
        lax.broadcasted_iota(jnp.int32, (8, cols), 0) == lax.broadcasted_iota(jnp.int32, (8, cols), 1) // HDIM
    ).astype(F32)
    for t in range(rows // QT):
        part = slice(t * QT, (t + 1) * QT)
        both = go[part, :].astype(F32) * os[part, :].astype(F32)
        delta[:, part] = lax.dot_general(
            pick, both, NT, precision=lax.Precision.HIGHEST, preferred_element_type=F32
        )
    dq[...] = jnp.zeros_like(dq)
    live = slots[rows // BLK]
    tiles = rows // QT

    def store(t, column, value, sign):
        cos = wide(cos_ref[t * QT : (t + 1) * QT, :], cols)
        sin = wide(sin_ref[t * QT : (t + 1) * QT, :], cols)
        done = (turn(value, cos, -sin) if sign else value).astype(BF)
        for i in range(QT // BLK):
            dst = pl.ds(pl.multiple_of(slots[t * (QT // BLK) + i] * BLK, BLK), BLK)
            out_ref[dst, column * cols : (column + 1) * cols] = done[i * BLK : (i + 1) * BLK, :]

    for t in range(tiles):
        begin = t * QT
        count = rows - begin
        lane_k = lax.broadcasted_iota(jnp.int32, (QT, cols), 1) // HDIM
        lane_q = lax.broadcasted_iota(jnp.int32, (count, cols), 1) // HDIM
        kpos = lax.broadcasted_iota(jnp.int32, (QT, QT), 0)
        qpos = lax.broadcasted_iota(jnp.int32, (QT, QT), 1)
        diag = jnp.where(kpos <= qpos, 0.0, NEG)
        dead = jnp.where(lax.broadcasted_iota(jnp.int32, (QT, 1), 0) + begin < live, 0.0, NEG)

        def head(h, carry):
            dk, dv = carry
            kt = ks[begin : begin + QT, :]
            qm = jnp.where(lane_q == h, qs[begin:, :] * BF(0.125), BF(0))
            gm = jnp.where(lane_q == h, go[begin:, :], BF(0))
            s = mm(kt, qm, NT) + dead
            first = s[:, :QT] + diag
            s = jnp.concatenate([first, s[:, QT:]], axis=1) if count > QT else first
            p = jnp.exp(s - stats[pl.ds(h, 1), begin:])
            dp = mm(vs[begin : begin + QT, :], gm, NT)
            ds = (p * (dp - delta[pl.ds(h, 1), begin:])).astype(BF)
            km = jnp.where(lane_k == h, kt * BF(0.125), BF(0))
            dq[begin:, :] += mm(ds, km, TN)
            return dk + mm(ds, qm), dv + mm(p.astype(BF), gm)

        zero = jnp.zeros((QT, cols), F32)
        dk, dv = lax.fori_loop(0, heads, head, (zero, zero))
        store(t, 1, dk, True)
        store(t, 2, dv, False)
    for t in range(tiles):
        store(t, 0, dq[t * QT : (t + 1) * QT, :], True)


def attend_back_call(slots, qs, ks, vs, os, stats, go, cos, sin):
    rows, cols = qs.shape
    heads = cols // HDIM
    return pl.pallas_call(
        attend_back_kernel,
        grid_spec=pltpu.PrefetchScalarGridSpec(
            num_scalar_prefetch=1,
            grid=(1,),
            in_specs=[full_spec(qs.shape)] * 4
            + [full_spec(stats.shape), full_spec(go.shape), full_spec(cos.shape), full_spec(sin.shape)],
            out_specs=full_spec((rows, 3 * cols)),
            scratch_shapes=[
                pltpu.VMEM((rows, cols), BF),
                pltpu.VMEM((8, rows), F32),
                pltpu.VMEM((rows, cols), F32),
            ],
        ),
        out_shape=jax.ShapeDtypeStruct((rows, 3 * cols), BF),
        compiler_params=pltpu.CompilerParams(vmem_limit_bytes=60 * 1024 * 1024),
        cost_estimate=pl.CostEstimate(
            flops=heads * rows * rows * HDIM * 20, bytes_accessed=rows * cols * 18, transcendentals=heads * rows * rows // 2
        ),
        name="attend_back",
    )(slots, qs, ks, vs, os, stats, go, cos, sin)


def per_device(
    shards, ctx, tensor, tokens, cotangent, seq_len, block_slot, attn_gain, w_query, w_key, w_value, w_out, mlp_gain, w_gate, w_up, w_down
):
    group = ctx * tensor
    my_x = lax.axis_index("ctx")
    my_t = lax.axis_index("tensor")
    my_z = lax.axis_index("shard")
    me = my_x * tensor + my_t
    width = tokens.shape[1]
    own_rows = tokens.shape[0] // tensor
    level_rows = own_rows * group
    slots_each = own_rows // BLK
    d_own = w_query.shape[0]
    cols = w_query.shape[1] // ctx
    ff = w_gate.shape[1] // ctx
    rel = jnp.arange(group, dtype=jnp.int32)
    swap_x = [(i, i ^ 1) for i in range(ctx)]

    slot = block_slot[0]
    place = ((slot // slots_each) ^ me) * slots_each + slot % slots_each
    slots = jnp.concatenate([place, seq_len]).astype(jnp.int32)

    def level_rows_of(array):
        local = jnp.take(array.reshape(tensor, own_rows, width), my_t ^ jnp.arange(tensor), axis=0)
        blocks = [local[k] for k in range(tensor)]
        half = own_rows // 2
        have = [(0, blocks[0])]
        got = swap(blocks[0], group, tensor)
        far = {tensor: got}
        bit = tensor // 2
        while bit >= 1:
            keys = sorted(far)
            sent = jnp.concatenate([far[k] for k in keys], axis=0) if len(keys) > 1 else far[keys[0]]
            got = swap(sent, group, bit)
            for i, k in enumerate(keys):
                far[k | bit] = got[i * own_rows : (i + 1) * own_rows]
            bit //= 2
        return jnp.concatenate([local.reshape(tensor * own_rows, width)] + [far[tensor + k] for k in range(tensor)], axis=0), blocks[0]

    def x_halves(array, axis):
        size = array.shape[axis] // ctx
        mine = lax.dynamic_slice_in_dim(array, my_x * size, size, axis=axis)
        other = lax.dynamic_slice_in_dim(array, (1 - my_x) * size, size, axis=axis)
        return mine, other

    def x_join(mine, got, axis):
        return jnp.where(
            my_x == 0, jnp.concatenate([mine, got], axis=axis), jnp.concatenate([got, mine], axis=axis)
        )

    gains = jnp.stack([attn_gain, mlp_gain], axis=0)
    gains = x_join(gains, lax.ppermute(gains, "ctx", swap_x), 1)
    gains = in_order(chain_gather(gains, shards), shards)
    gains = jnp.transpose(gains, (1, 0, 2)).reshape(2, width).astype(F32)
    gain_one, gain_two = gains[0:1], gains[1:2]

    halves = [x_halves(w, 1) for w in (w_query, w_key, w_value)]
    mine = jnp.concatenate([a for a, _ in halves], axis=1)
    got = lax.ppermute(jnp.concatenate([b for _, b in halves], axis=1), "ctx", swap_x)
    w_qkv = in_order(chain_gather(x_join(mine, got, 0), shards), shards).reshape(width, 3 * cols)

    tok, tok_own = level_rows_of(tokens)

    angle_at = jnp.arange(level_rows, dtype=F32)
    lane = jnp.arange(128)
    freqs = THETA ** (-(lane % (HDIM // 2)).astype(F32) / (HDIM // 2))
    angles = angle_at[:, None] * freqs[None, :]
    cos = jnp.cos(angles)
    sin = jnp.sin(angles) * jnp.where(lane % HDIM < HDIM // 2, -1.0, 1.0)
    n_one, lin = qkv_call(tok, gain_one, w_qkv)
    o_slot, qs, ks, vs, os, stats = attend_call(slots, lin, cos, sin)

    head_order = jnp.arange(group)
    head_owner = (head_order % ctx) * tensor + head_order // ctx
    got = level_exchange([o_slot[k * own_rows : (k + 1) * own_rows] for k in range(group)], group)
    attn_rows = jnp.take(jnp.stack(got, axis=0), head_owner ^ me, axis=0)
    attn_rows = jnp.transpose(attn_rows, (1, 0, 2)).reshape(own_rows, width)

    pieces = jnp.stack(chain_gather(w_out, shards), axis=0)
    every = jnp.stack(level_gather(pieces, ctx, tensor, axis=1), axis=0)
    every = jnp.take(every, rel ^ me, axis=0)
    every = jnp.take(every, (my_z - jnp.arange(shards)) % shards, axis=1)
    every = every.reshape(ctx, tensor, shards, w_out.shape[0], d_own)
    w_out_all = jnp.transpose(every, (1, 3, 2, 0, 4)).reshape(width, width)

    x_own = tok_own.astype(F32)
    hidden_res = x_own + mm(attn_rows, w_out_all)
    scale_two = lax.rsqrt(jnp.mean(hidden_res * hidden_res, axis=-1, keepdims=True) + EPS)
    normed_two = hidden_res * scale_two
    n_two_own = (normed_two * gain_two).astype(BF)
    n_two = jnp.concatenate(level_gather(n_two_own, ctx, tensor), axis=0)
    cot, cot_own = level_rows_of(cotangent)

    chunks = 2
    fc = ff // chunks
    w_down_t = w_down.T
    chunk_grads = []
    gu_all, hid_all, w_gu_all, w_dt_all = [], [], [], []
    for c in range(chunks):
        mine_parts, other_parts = [], []
        for w in (w_gate, w_up, w_down_t):
            mine_parts.append(lax.dynamic_slice_in_dim(w, my_x * ff + c * fc, fc, axis=1))
            other_parts.append(lax.dynamic_slice_in_dim(w, (1 - my_x) * ff + c * fc, fc, axis=1))
        mine = jnp.concatenate(mine_parts, axis=1)
        got = lax.ppermute(jnp.concatenate(other_parts, axis=1), "ctx", swap_x)
        weights = in_order(chain_gather(x_join(mine, got, 0), shards), shards).reshape(width, 3 * fc)
        w_gu, w_dt = weights[:, : 2 * fc], weights[:, 2 * fc :]
        gate_up = mm(n_two, w_gu)
        gate, up = gate_up[:, :fc], gate_up[:, fc:]
        sig = jax.nn.sigmoid(gate)
        act = gate * sig
        hidden = (act * up).astype(BF)
        d_hidden = mm(cot, w_dt)
        d_gate = (d_hidden * up * sig * (1.0 + gate * (1.0 - sig))).astype(BF)
        d_up = (d_hidden * act).astype(BF)
        d_gu = jnp.concatenate([d_gate, d_up], axis=1)
        grad_gu = mm(n_two, d_gu, TN).astype(BF)
        grad_dt = mm(cot, hidden, TN).astype(BF)
        chunk_grads.append(jnp.concatenate([grad_gu, grad_dt], axis=1))
        gu_all.append(d_gu)
        hid_all.append(hidden)
        w_gu_all.append(w_gu)
        w_dt_all.append(w_dt)
    d_gu = jnp.concatenate(gu_all, axis=1)
    hidden = jnp.concatenate(hid_all, axis=1)
    w_gu = jnp.concatenate(w_gu_all, axis=1)
    w_dt = jnp.concatenate(w_dt_all, axis=1)

    def row_blocks(array):
        return [array[k * own_rows : (k + 1) * own_rows] for k in range(group)]

    d_n_two = level_sum(row_blocks(mm(d_gu, w_gu, NT).astype(BF)), ctx, tensor)
    out_own = hidden_res + level_sum(row_blocks(mm(hidden, w_dt, NT).astype(BF)), ctx, tensor)

    def tensor_rows(own):
        have = [(0, own)]
        bit = tensor // 2
        while bit >= 1:
            sent = jnp.concatenate([v for _, v in have], axis=0) if len(have) > 1 else have[0][1]
            got = swap(sent, group, bit)
            have = have + [(k | bit, got[i * own_rows : (i + 1) * own_rows]) for i, (k, _) in enumerate(have)]
            bit //= 2
        have = [v for _, v in sorted(have, key=lambda e: e[0])]
        ordered = jnp.take(jnp.stack(have, axis=0), my_t ^ jnp.arange(tensor), axis=0)
        return ordered.reshape(tensor * own_rows, width)

    result = tensor_rows(out_own.astype(BF))

    def mlp_sums(chunk):
        total = chain_sum(chunk.reshape(shards, ctx * d_own, 3 * fc), shards)
        mine, other = x_halves(total, 0)
        got = lax.ppermute(other.astype(BF), "ctx", swap_x).astype(F32)
        return mine, got

    cot_f = cot_own.astype(F32)
    scaled = d_n_two * gain_two
    inner = jnp.mean(scaled * normed_two, axis=-1, keepdims=True)
    d_h = cot_f + scale_two * (scaled - normed_two * inner)
    gain_two_part = jnp.sum(d_n_two * normed_two, axis=0)
    d_h_low = d_h.astype(BF)
    d_attn = mm(d_h_low, w_out_all, NT).astype(BF)
    blocks = jnp.transpose(d_attn.reshape(own_rows, group, cols), (1, 0, 2))
    owner_rel = rel ^ me
    col_of = (owner_rel % tensor) * ctx + owner_rel // tensor
    blocks = jnp.take(blocks, col_of, axis=0)
    go = jnp.concatenate(level_exchange([blocks[k] for k in range(group)], group), axis=0)
    d_qkv = attend_back_call(slots, qs, ks, vs, os, stats, go, cos, sin)

    d_h_all = jnp.concatenate(level_gather(d_h_low, ctx, tensor), axis=0)
    grad_wo = mm(d_h_all, o_slot, TN).astype(BF)
    grad_wqkv = mm(n_one, d_qkv, TN).astype(BF)
    d_n_one = level_sum(row_blocks(mm(d_qkv, w_qkv, NT).astype(BF)), ctx, tensor)
    x_scale = lax.rsqrt(jnp.mean(x_own * x_own, axis=-1, keepdims=True) + EPS)
    x_normed = x_own * x_scale
    scaled = d_n_one * gain_one
    inner = jnp.mean(scaled * x_normed, axis=-1, keepdims=True)
    d_x = d_h + x_scale * (scaled - x_normed * inner)
    gain_one_part = jnp.sum(d_n_one * x_normed, axis=0)
    grad_x = tensor_rows(d_x.astype(BF))

    def spread(parts, axis):
        mine = jnp.concatenate([m for m, _ in parts], axis=axis) if len(parts) > 1 else parts[0][0]
        got = jnp.concatenate([g for _, g in parts], axis=axis) if len(parts) > 1 else parts[0][1]
        return x_join(mine, got, axis)

    sums = [mlp_sums(g) for g in chunk_grads]
    grad_gate = spread([(m[:, :fc], g[:, :fc]) for m, g in sums], 1)
    grad_up = spread([(m[:, fc : 2 * fc], g[:, fc : 2 * fc]) for m, g in sums], 1)
    grad_down = spread([(m[:, 2 * fc :], g[:, 2 * fc :]) for m, g in sums], 1).T

    def attn_sums(array):
        total = chain_sum(array.reshape(shards, ctx * d_own, array.shape[1]), shards)
        mine, other = x_halves(total, 0)
        got = lax.ppermute(other.astype(BF), "ctx", swap_x).astype(F32)
        return mine, got

    mine, got = attn_sums(grad_wo)
    grad_out = x_join(mine, got, 1).T
    mine, got = attn_sums(grad_wqkv)
    grad_q = x_join(mine[:, :cols], got[:, :cols], 1)
    grad_k = x_join(mine[:, cols : 2 * cols], got[:, cols : 2 * cols], 1)
    grad_v = x_join(mine[:, 2 * cols :], got[:, 2 * cols :], 1)

    def gain_sum(part):
        total = lax.psum(part, ("shard", "ctx", "tensor"))
        return lax.dynamic_slice_in_dim(total, (my_z * ctx + my_x) * d_own, d_own)

    grad_gain_two = gain_sum(gain_two_part)
    grad_gain_one = gain_sum(gain_one_part)
    return (
        result,
        grad_x,
        grad_gain_one,
        grad_q,
        grad_k,
        grad_v,
        grad_out,
        grad_gain_two,
        grad_gate,
        grad_up,
        grad_down,
    )


def solution(mesh):
    rows = P(("shard", "ctx"), None)
    gain = P(("shard", "ctx"))
    into = P(("shard", "ctx"), "tensor")
    back = P("tensor", ("shard", "ctx"))
    sizes = mesh.shape
    return jax.shard_map(
        functools.partial(per_device, sizes["shard"], sizes["ctx"], sizes["tensor"]),
        mesh=mesh,
        in_specs=(rows, rows, P("shard"), P("shard", None), gain, into, into, into, back, gain, into, into, back),
        out_specs=(rows, rows, gain, into, into, into, back, gain, into, into, back),
        check_vma=False,
    )
```

time: 2200 us -> 1370 us (0.62)
  waiting for transfers between devices: 1460 us -> 352 us
  matrix products: 443 us -> 157 us
  local copies, waits for them, and re-layouts: 67.5 us -> 268 us
  starting transfers between devices: 2.06 us -> 198 us
  other arithmetic: 134 us -> 242 us
  Pallas kernels: 0 us -> 102 us
  blocking collectives: 64.9 us -> 39.3 us
    reduce_scatter x9 -> x0, waiting for transfers between devices: 647 us -> none  [the longest x1 149 us: per_device(): lax.psum_scatter(grad_wup.astype(jnp.bfloat16), ('shard', 'ctx'), scatter...]
    all_gather x9 -> x0, waiting for transfers between devices: 507 us -> none  [the longest x1 118 us: per_device(): lax.all_gather(w_up, ('shard', 'ctx'), axis=0, tiled=True)]
    ppermute x0 -> x128, waiting for transfers between devices: none -> 352 us  [the longest x66 169 us: swap(): return lax.ppermute(value, LEVEL, [(i, i ^ bit) for i in range(group)])]
    psum x3 -> x0, waiting for transfers between devices: 300 us -> none  [tensor_total(): lax.psum(partial_value.astype(jnp.bfloat16), 'tensor').astype(jnp.float32)]
    dot_general x33 -> x15, matrix products: 443 us -> 157 us  [the longest x10 97.9 us: mm(): return lax.dot_general(left, right, dims, preferred_element_type=F32)]
    ppermute x0 -> x128, starting transfers between devices: none -> 198 us  [the longest x12 60.9 us: chain_sum(): up = lax.ppermute(send, 'shard', [(i, i + 1) for i in range(0, k)])]
    pallas_call x0 -> x3, Pallas kernels: none -> 102 us  [the longest x1 48.3 us: attend_back_call(): pl.pallas_call(attend_back_kernel, grid_spec=pltpu.PrefetchScalarGridSpec...]
    unnamed x59 -> x289, local copies, waits for them, and re-layouts: 11.1 us -> 100 us
  transfers between devices with their start and end apart: 21 -> 128, of which waited for: 19 -> 47; matrix products, arithmetic and copies ran while one was open for 14% -> 41% of each run, Pallas kernels for 0% -> 7%
where the time goes in v1:
time: 1370 us; the launch traced here: 1360 us
  waiting for transfers between devices  352 us (26%)
  local copies, waits for them, and re-layouts  268 us (20%)
  other arithmetic  242 us (18%)
  starting transfers between devices  198 us (14%)
  matrix products  157 us (11%)
  Pallas kernels  102 us (7%)
  blocking collectives  39.3 us (3%)
    ppermute x66, waiting for transfers between devices, swap(): return lax.ppermute(value, LEVEL, [(i, i ^ bit) for i in range(group)])  169 us
    unnamed x289, local copies, waits for them, and re-layouts  100 us
    dot_general x10, matrix products, mm(): return lax.dot_general(left, right, dims, preferred_element_type=F32)  97.9 us
    ppermute x15, waiting for transfers between devices, chain_gather(): lax.ppermute(down, 'shard', [(i, i - 1) for i in range(1, shards - k + 1)])  86.3 us
    ppermute x12, starting transfers between devices, chain_sum(): up = lax.ppermute(send, 'shard', [(i, i + 1) for i in range(0, k)])  60.9 us
    dot_general x5, matrix products, mm(): return jnp.dot(left, right, preferred_element_type=F32)  59.2 us
    ppermute x66, starting transfers between devices, swap(): return lax.ppermute(value, LEVEL, [(i, i ^ bit) for i in range(group)])  51.3 us
    ppermute x12, waiting for transfers between devices, chain_sum(): up = lax.ppermute(send, 'shard', [(i, i + 1) for i in range(0, k)])  49.7 us
  transfers between devices with their start and end apart: 128, of which 47 were waited for; matrix products, arithmetic and copies ran while one was open for 41% of the time, Pallas kernels for 7%

profile of v1, /device:TPU:0, one launch (start us, length us, event | category | flops | bytes accessed | tf_op | source)
XLA Modules:
  0.0 1361.7 jit_solution(5572455975714755257)
XLA Ops:
  115.7 9.1 maximum_select_fusion.4
  131.0 9.3 maximum_select_fusion.6
  144.0 9.5 collective-permute-done.69
  193.0 20.2 %collective-permute-done.70 = bf16[256,2048]{1,0:T(8,128)(2,1)S(1)} collective-permute-done((bf16[256,2048]{1,0:T(8,128)(2,1)S(1)}, bf16[256,2048]{1,0:T(8,128)(2,1)S(1)}, u32[]{:S(2)}, u32[]{:S(2)}) %collective-permute-start.70) | collective-permute-done | bytes 1048608 | tf_op jit(solution)/shard_map/ppermute | solution.py:31
  216.5 10.8 collective-permute-done.32
  254.9 15.8 %collective-permute-done.50 = bf16[512,1536]{1,0:T(8,128)(2,1)} collective-permute-done((bf16[512,1536]{1,0:T(8,128)(2,1)}, bf16[512,1536]{1,0:T(8,128)(2,1)}, u32[]{:S(2)}, u32[]{:S(2)}) %collective-permute-start.50) | collective-permute-done | bytes 1572896 | tf_op jit(solution)/shard_map/ppermute | solution.py:114
  275.8 28.6 %collective-permute-done.57 = bf16[512,1536]{1,0:T(8,128)(2,1)} collective-permute-done((bf16[512,1536]{1,0:T(8,128)(2,1)}, bf16[512,1536]{1,0:T(8,128)(2,1)}, u32[]{:S(2)}, u32[]{:S(2)}) %collective-permute-start.57) | collective-permute-done | bytes 1572896 | tf_op jit(solution)/shard_map/ppermute | solution.py:114
  348.3 17.7 %fusion.11 = bf16[4,512,4,2,256]{4,3,2,1,0:T(2,128)(2,1)} fusion(bf16[2,4,4,512,256]{4,3,1,0,2:T(8,128)(2,1)} %bitcast.304, pred[4]{0:T(512)(128)(4,1)S(1)} %copy-done.77), kind=kLoop, calls=%fused_computation.26 | loop fusion | flops 4194304 | bytes 16777220 | tf_op jit(solution)/shard_map/transpose | solution.py:442
  366.0 14.5 %reshape.479 = bf16[2048,2048]{1,0:T(8,128)(2,1)} reshape(bf16[4,512,4,2,256]{4,3,2,1,0:T(2,128)(2,1)} %fusion.11) | data formatting | bytes 16777216 | tf_op jit(solution)/shard_map/reshape | solution.py:442
  395.1 13.2 norm_qkv.1
  408.3 40.4 %attend.1 = (bf16[2048,256]{1,0:T(8,128)(2,1)}, bf16[2048,256]{1,0:T(8,128)(2,1)}, bf16[2048,256]{1,0:T(8,128)(2,1)}, bf16[2048,256]{1,0:T(8,128)(2,1)}, bf16[2048,256]{1,0:T(8,128)(2,1)}, /*index=5*/f32[8,2048]{1,0:T(8,128)}) custom-call(s32[17]{0:T(128)} %pad_add_fusion.slots, f32[2048,768]{1,0:T(8,128)} %get-tuple-element.22.lin_ref, ...), custom_call_target="tpu_custom_call" | custom-call | flops 8589934592 | bytes 11534336 | tf_op jit(solution)/shard_map/attend/pallas_call | solution.py:251
  491.1 9.6 collective-permute-done.42
  520.6 22.2 %collective-permute-done.59 = bf16[512,1536]{1,0:T(8,128)(2,1)S(1)} collective-permute-done((bf16[512,1536]{1,0:T(8,128)(2,1)}, bf16[512,1536]{1,0:T(8,128)(2,1)S(1)}, u32[]{:S(2)}, u32[]{:S(2)}) %collective-permute-start.59) | collective-permute-done | bytes 1572896 | tf_op jit(solution)/shard_map/ppermute | solution.py:114
  563.7 10.4 broadcast_select_fusion.3
  607.5 13.4 fusion.108
  620.9 13.8 %fusion.106 = f32[2048,1024]{0,1:T(8,128)} fusion(bf16[2048,2048]{1,0:T(8,128)(2,1)} %slice_dynamic-update-slice_fusion.12, bf16[2048,1536]{1,0:T(8,128)(2,1)S(1)} %bitcast.311), kind=kOutput, calls=%fused_computation.438 | convolution fusion | flops 8589934592 | bytes 20971520 | tf_op jit(solution)/shard_map/dot_general | solution.py:26
  634.7 12.6 multiply_convert_fusion.3
  656.3 11.5 fusion.36
  689.6 13.1 multiply_convert_fusion.1
  707.5 11.3 fusion.33
  737.4 10.8 convolution_convert_fusion.1
  753.6 26.1 %fusion.12 = bf16[2048,2048]{1,0:T(8,128)(2,1)} fusion(bf16[2048,1024]{1,0:T(8,128)(2,1)} %slice.683, bf16[2048,1024]{1,0:T(8,128)(2,1)} %slice.680, bf16[2048,512]{0,1:T(8,128)(2,1)} %get-tuple-element.85, bf16[2048,512]{0,1:T(8,128)(2,1)} %get-tuple-element.84, bf16[2048,512]{0,1:T(8,128)(2,1)} %get-tuple-element.83, bf16[2048,512]{0,1:T(8,128)(2,1)} %get-tuple-element.82), kind=kOutput, calls=%fused_computation.28 | convolution fusion | flops 17234395136 | bytes 25165824 | tf_op jit(solution)/shard_map/dot_general | solution.py:27
  804.7 17.6 %collective-permute-done.115 = bf16[512,1536]{1,0:T(8,128)(2,1)} collective-permute-done((bf16[512,1536]{1,0:T(8,128)(2,1)}, bf16[512,1536]{1,0:T(8,128)(2,1)}, u32[]{:S(2)}, u32[]{:S(2)}) %collective-permute-start.115) | collective-permute-done | bytes 1572896 | tf_op jit(solution)/shard_map/ppermute | solution.py:139
  836.7 19.2 %collective-permute-done.121 = bf16[512,1536]{1,0:T(8,128)(2,1)} collective-permute-done((bf16[512,1536]{1,0:T(8,128)(2,1)}, bf16[512,1536]{1,0:T(8,128)(2,1)}, u32[]{:S(2)}, u32[]{:S(2)}) %collective-permute-start.121) | collective-permute-done | bytes 1572896 | tf_op jit(solution)/shard_map/ppermute | solution.py:139
  885.9 13.6 collective-permute-done.65
  905.0 14.2 %collective-permute-done.75 = bf16[256,2048]{1,0:T(8,128)(2,1)S(1)} collective-permute-done((bf16[256,2048]{1,0:T(8,128)(2,1)S(1)}, bf16[256,2048]{1,0:T(8,128)(2,1)S(1)}, u32[]{:S(2)}, u32[]{:S(2)}) %collective-permute-start.75) | collective-permute-done | bytes 1048608 | tf_op jit(solution)/shard_map/ppermute | solution.py:31
  985.9 48.3 %attend_back.1 = bf16[2048,768]{1,0:T(8,128)(2,1)} custom-call(s32[17]{0:T(128)} %pad_add_fusion.slots, bf16[2048,256]{1,0:T(8,128)(2,1)} %get-tuple-element.24.qs, bf16[2048,256]{1,0:T(8,128)(2,1)} %get-tuple-element.25.ks, bf16[2048,256]{1,0:T(8,128)(2,1)} %get-tuple-element.26.vs, bf16[2048,256]{1,0:T(8,128)(2,1)} %get-tuple-element.27.os, ...), custom_call_target="tpu_custom_call" | custom-call | flops 21474836480 | bytes 9437184 | tf_op jit(solution)/shard_map/attend_back/pallas_call | solution.py:336
  1034.2 11.2 convolution_convert_fusion.2
  1133.7 12.2 collective-permute-done.127
  1168.2 14.1 %collective-permute-done.96 = bf16[512,768]{0,1:T(8,128)(2,1)} collective-permute-done((bf16[512,768]{0,1:T(8,128)(2,1)}, bf16[512,768]{0,1:T(8,128)(2,1)}, u32[]{:S(2)}, u32[]{:S(2)}) %collective-permute-start.96) | collective-permute-done | bytes 786464 | tf_op jit(solution)/shard_map/ppermute | solution.py:142
  1202.2 22.1 %collective-permute-done.87 = bf16[256,2048]{1,0:T(8,128)(2,1)S(1)} collective-permute-done((bf16[256,2048]{1,0:T(8,128)(2,1)S(1)}, bf16[256,2048]{1,0:T(8,128)(2,1)S(1)}, u32[]{:S(2)}, u32[]{:S(2)}) %collective-permute-start.87) | collective-permute-done | bytes 1048608 | tf_op jit(solution)/shard_map/ppermute | solution.py:31
  1303.9 39.3 %all-reduce = (f32[2048]{0:T(1024)S(1)}, f32[2048]{0:T(1024)S(1)}) all-reduce(f32[2048]{0:T(1024)S(1)} %get-tuple-element.63, f32[2048]{0:T(1024)S(1)} %copy-done.72), channel_id=1, replica_groups=mesh['shard'=4,'ctx'=2,'tensor'=4] {'shard','ctx','tensor'}, use_global_device_ids=true, to_apply=%region_5.9 | all-reduce | flops 4096 | bytes 32768 | tf_op jit(solution)/shard_map/psum | solution.py:563
  (763 shorter events, 802.3 us)
Async XLA Ops:
  0.6 81.0 %collective-permute-start.25 = (bf16[512,256]{1,0:T(8,128)(2,1)}, bf16[512,256]{1,0:T(8,128)(2,1)}, u32[]{:S(2)}, u32[]{:S(2)}) collective-permute-start(bf16[512,256]{1,0:T(8,128)(2,1)} %param.27), channel_id=1, source_target_pairs={{8,0},{16,8},{24,16},{9,1},{17,9},{25,17},{10,2},{18,10},{26,18},{... | collective-permute-start | bytes 786440 | tf_op jit(solution)/shard_map/ppermute | solution.py:114
  1.9 79.0 %collective-permute-start.24 = (bf16[512,256]{1,0:T(8,128)(2,1)}, bf16[512,256]{1,0:T(8,128)(2,1)}, u32[]{:S(2)}, u32[]{:S(2)}) collective-permute-start(bf16[512,256]{1,0:T(8,128)(2,1)} %param.27), channel_id=1, source_target_pairs={{0,8},{8,16},{16,24},{1,9},{9,17},{17,25},{2,10},{10,18},{18,26},{... | collective-permute-start | bytes 786440 | tf_op jit(solution)/shard_map/ppermute | solution.py:113
  11.2 77.1 %collective-permute-start.10 = (bf16[256,768]{1,0:T(8,128)(2,1)}, bf16[256,768]{1,0:T(8,128)(2,1)}, u32[]{:S(2)}, u32[]{:S(2)}) collective-permute-start(bf16[256,768]{1,0:T(8,128)(2,1)} %pad_maximum_fusion.33), channel_id=1, source_target_pairs={{0,4},{4,0},{1,5},{5,1},{2,6},{6,2},{3,7},{7,3},{8,12},{12,8},{9,1... | collective-permute-start | bytes 1179656 | tf_op jit(solution)/shard_map/ppermute | solution.py:417
  71.0 71.1 %collective-permute-start = (bf16[256,2048]{1,0:T(8,128)(2,1)}, bf16[256,2048]{1,0:T(8,128)(2,1)S(1)}, u32[]{:S(2)}, u32[]{:S(2)}) collective-permute-start(bf16[256,2048]{1,0:T(8,128)(2,1)} %slice_bitcast_fusion.5), channel_id=1, source_target_pairs={{0,4},{1,5},{2,6},{3,7},{4,0},{5,1},{6,2},{7,3},{8,12},{9,13},{10,... | collective-permute-start | bytes 3145736 | tf_op jit(solution)/shard_map/ppermute | solution.py:31
  171.6 81.4 %collective-permute-start.49 = (bf16[512,1536]{1,0:T(8,128)(2,1)}, bf16[512,1536]{1,0:T(8,128)(2,1)}, u32[]{:S(2)}, u32[]{:S(2)}) collective-permute-start(bf16[512,1536]{1,0:T(8,128)(2,1)} %maximum_select_fusion.4), channel_id=1, source_target_pairs={{0,8},{8,16},{16,24},{1,9},{9,17},{17,25},{2,10},{10,18},{18,26},{... | collective-permute-start | bytes 4718600 | tf_op jit(solution)/shard_map/ppermute | solution.py:113
  241.2 63.2 %collective-permute-start.57 = (bf16[512,1536]{1,0:T(8,128)(2,1)}, bf16[512,1536]{1,0:T(8,128)(2,1)}, u32[]{:S(2)}, u32[]{:S(2)}) collective-permute-start(bf16[512,1536]{1,0:T(8,128)(2,1)} %maximum_select_fusion.6), channel_id=1, source_target_pairs={{8,0},{16,8},{24,16},{9,1},{17,9},{25,17},{10,2},{18,10},{26,18},{... | collective-permute-start | bytes 4718600 | tf_op jit(solution)/shard_map/ppermute | solution.py:114
  252.9 136.5 %collective-permute-start.2 = (bf16[512,2048]{1,0:T(8,128)(2,1)}, bf16[512,2048]{1,0:T(8,128)(2,1)}, u32[]{:S(2)}, u32[]{:S(2)}) collective-permute-start(bf16[512,2048]{1,0:T(8,128)(2,1)} %pad_maximum_fusion.11), channel_id=1, source_target_pairs={{0,1},{1,0},{2,3},{3,2},{4,5},{5,4},{6,7},{7,6},{8,9},{9,8},{10,11... | collective-permute-start | bytes 6291464 | tf_op jit(solution)/shard_map/ppermute | solution.py:31
  253.0 127.5 %collective-permute-start.53 = (bf16[512,1536]{1,0:T(8,128)(2,1)}, bf16[512,1536]{1,0:T(8,128)(2,1)}, u32[]{:S(2)}, u32[]{:S(2)}) collective-permute-start(bf16[512,1536]{1,0:T(8,128)(2,1)} %collective-permute-done.49), channel_id=1, source_target_pairs={{8,16},{16,24},{9,17},{17,25},{10,18},{18,26},{11,19},{19,27},{12,... | collective-permute-start | bytes 4718600 | tf_op jit(solution)/shard_map/ppermute | solution.py:113
  270.7 109.8 %collective-permute-start.51 = (bf16[512,1536]{1,0:T(8,128)(2,1)}, bf16[512,1536]{1,0:T(8,128)(2,1)}, u32[]{:S(2)}, u32[]{:S(2)}) collective-permute-start(bf16[512,1536]{1,0:T(8,128)(2,1)} %collective-permute-done.50), channel_id=1, source_target_pairs={{8,0},{16,8},{9,1},{17,9},{10,2},{18,10},{11,3},{19,11},{12,4},{20... | collective-permute-start | bytes 4718600 | tf_op jit(solution)/shard_map/ppermute | solution.py:114
  274.0 111.0 %collective-permute-start.60 = (bf16[512,1536]{1,0:T(8,128)(2,1)}, bf16[512,1536]{1,0:T(8,128)(2,1)}, u32[]{:S(2)}, u32[]{:S(2)}) collective-permute-start(bf16[512,1536]{1,0:T(8,128)(2,1)} %collective-permute-done.56), channel_id=1, source_target_pairs={{8,16},{16,24},{9,17},{17,25},{10,18},{18,26},{11,19},{19,27},{12,... | collective-permute-start | bytes 4718600 | tf_op jit(solution)/shard_map/ppermute | solution.py:113
  304.4 82.3 %collective-permute-start.58 = (bf16[512,1536]{1,0:T(8,128)(2,1)}, bf16[512,1536]{1,0:T(8,128)(2,1)}, u32[]{:S(2)}, u32[]{:S(2)}) collective-permute-start(bf16[512,1536]{1,0:T(8,128)(2,1)} %collective-permute-done.57), channel_id=1, source_target_pairs={{8,0},{16,8},{9,1},{17,9},{10,2},{18,10},{11,3},{19,11},{12,4},{20... | collective-permute-start | bytes 4718600 | tf_op jit(solution)/shard_map/ppermute | solution.py:114
  380.5 71.6 %collective-permute-start.71 = (bf16[512,2048]{1,0:T(8,128)(2,1)}, bf16[512,2048]{1,0:T(8,128)(2,1)S(1)}, u32[]{:S(2)}, u32[]{:S(2)}) collective-permute-start(bf16[512,2048]{1,0:T(8,128)(2,1)} %pad_maximum_fusion.13), channel_id=1, source_target_pairs={{0,1},{1,0},{2,3},{3,2},{4,5},{5,4},{6,7},{7,6},{8,9},{9,8},{10,11... | collective-permute-start | bytes 6291464 | tf_op jit(solution)/shard_map/ppermute | solution.py:31
  380.5 129.1 %collective-permute-start.54 = (bf16[512,1536]{1,0:T(8,128)(2,1)}, bf16[512,1536]{1,0:T(8,128)(2,1)}, u32[]{:S(2)}, u32[]{:S(2)}) collective-permute-start(bf16[512,1536]{1,0:T(8,128)(2,1)} %collective-permute-done.53), channel_id=1, source_target_pairs={{16,24},{17,25},{18,26},{19,27},{20,28},{21,29},{22,30},{23,31}} | collective-permute-start | bytes 4718600 | tf_op jit(solution)/shard_map/ppermute | solution.py:113
  385.1 127.1 %collective-permute-start.52 = (bf16[512,1536]{1,0:T(8,128)(2,1)}, bf16[512,1536]{1,0:T(8,128)(2,1)}, u32[]{:S(2)}, u32[]{:S(2)}) collective-permute-start(bf16[512,1536]{1,0:T(8,128)(2,1)} %collective-permute-done.51), channel_id=1, source_target_pairs={{8,0},{9,1},{10,2},{11,3},{12,4},{13,5},{14,6},{15,7}} | collective-permute-start | bytes 4718600 | tf_op jit(solution)/shard_map/ppermute | solution.py:114
  507.1 83.0 %collective-permute-start.45 = (bf16[256,2048]{1,0:T(8,128)(2,1)}, bf16[256,2048]{1,0:T(8,128)(2,1)}, u32[]{:S(2)}, u32[]{:S(2)}) collective-permute-start(bf16[256,2048]{1,0:T(8,128)(2,1)} %pad_maximum_fusion.22), channel_id=1, source_target_pairs={{0,4},{1,5},{2,6},{3,7},{4,0},{5,1},{6,2},{7,3},{8,12},{9,13},{10,... | collective-permute-start | bytes 3145736 | tf_op jit(solution)/shard_map/ppermute | solution.py:31
  512.1 80.5 %collective-permute-start.44 = (bf16[128,2048]{1,0:T(8,128)(2,1)}, bf16[128,2048]{1,0:T(8,128)(2,1)}, u32[]{:S(2)}, u32[]{:S(2)}) collective-permute-start(bf16[128,2048]{1,0:T(8,128)(2,1)} %collective-permute-done.42), channel_id=1, source_target_pairs={{0,1},{1,0},{2,3},{3,2},{4,5},{5,4},{6,7},{7,6},{8,9},{9,8},{10,11... | collective-permute-start | bytes 1572872 | tf_op jit(solution)/shard_map/ppermute | solution.py:31
  513.8 84.4 %collective-permute-start.46 = (bf16[128,2048]{1,0:T(8,128)(2,1)}, bf16[128,2048]{1,0:T(8,128)(2,1)}, u32[]{:S(2)}, u32[]{:S(2)}) collective-permute-start(bf16[128,2048]{1,0:T(8,128)(2,1)} %collective-permute-done.40), channel_id=1, source_target_pairs={{0,1},{1,0},{2,3},{3,2},{4,5},{5,4},{6,7},{7,6},{8,9},{9,8},{10,11... | collective-permute-start | bytes 1572872 | tf_op jit(solution)/shard_map/ppermute | solution.py:31
  683.5 98.9 %collective-permute-start.114 = (bf16[512,1536]{1,0:T(8,128)(2,1)}, bf16[512,1536]{1,0:T(8,128)(2,1)}, u32[]{:S(2)}, u32[]{:S(2)}) collective-permute-start(bf16[512,1536]{1,0:T(8,128)(2,1)} %get-tuple-element.108), channel_id=1, source_target_pairs={{0,8},{1,9},{2,10},{3,11},{4,12},{5,13},{6,14},{7,15}} | collective-permute-start | bytes 4718600 | tf_op jit(solution)/shard_map/ppermute | solution.py:139
  687.7 108.7 %collective-permute-start.117 = (bf16[512,1536]{1,0:T(8,128)(2,1)}, bf16[512,1536]{1,0:T(8,128)(2,1)}, u32[]{:S(2)}, u32[]{:S(2)}) collective-permute-start(bf16[512,1536]{1,0:T(8,128)(2,1)} %get-tuple-element.109), channel_id=1, source_target_pairs={{24,16},{25,17},{26,18},{27,19},{28,20},{29,21},{30,22},{31,23}} | collective-permute-start | bytes 4718600 | tf_op jit(solution)/shard_map/ppermute | solution.py:142
  753.6 107.9 %collective-permute-start.62 = (bf16[1024,2048]{1,0:T(8,128)(2,1)}, bf16[1024,2048]{1,0:T(8,128)(2,1)}, u32[]{:S(2)}, u32[]{:S(2)}) collective-permute-start(bf16[1024,2048]{1,0:T(8,128)(2,1)} %pad_maximum_fusion.5), channel_id=1, source_target_pairs={{0,1},{1,0},{2,3},{3,2},{4,5},{5,4},{6,7},{7,6},{8,9},{9,8},{10,11... | collective-permute-start | bytes 12582920 | tf_op jit(solution)/shard_map/ppermute | solution.py:31
  790.6 82.7 %collective-permute-start.72 = (bf16[1024,2048]{1,0:T(8,128)(2,1)}, bf16[1024,2048]{1,0:T(8,128)(2,1)}, u32[]{:S(2)}, u32[]{:S(2)}) collective-permute-start(bf16[1024,2048]{1,0:T(8,128)(2,1)} %pad_maximum_fusion.7), channel_id=1, source_target_pairs={{0,1},{1,0},{2,3},{3,2},{4,5},{5,4},{6,7},{7,6},{8,9},{9,8},{10,11... | collective-permute-start | bytes 12582920 | tf_op jit(solution)/shard_map/ppermute | solution.py:31
  796.3 59.6 %collective-permute-start.121 = (bf16[512,1536]{1,0:T(8,128)(2,1)}, bf16[512,1536]{1,0:T(8,128)(2,1)}, u32[]{:S(2)}, u32[]{:S(2)}) collective-permute-start(bf16[512,1536]{1,0:T(8,128)(2,1)} %fusion.41), channel_id=1, source_target_pairs={{0,8},{8,16},{1,9},{9,17},{2,10},{10,18},{3,11},{11,19},{4,12},{12... | collective-permute-start | bytes 4718600 | tf_op jit(solution)/shard_map/ppermute | solution.py:139
  828.0 250.2 %collective-permute-start.116 = (bf16[512,1536]{1,0:T(8,128)(2,1)}, bf16[512,1536]{1,0:T(8,128)(2,1)}, u32[]{:S(2)}, u32[]{:S(2)}) collective-permute-start(bf16[512,1536]{1,0:T(8,128)(2,1)} %get-tuple-element.106), channel_id=1, source_target_pairs={{0,8},{8,16},{16,24},{1,9},{9,17},{17,25},{2,10},{10,18},{18,26},{... | collective-permute-start | bytes 4718600 | tf_op jit(solution)/shard_map/ppermute | solution.py:139
  861.6 221.7 %collective-permute-start.122 = (bf16[512,1536]{1,0:T(8,128)(2,1)}, bf16[512,1536]{1,0:T(8,128)(2,1)}, u32[]{:S(2)}, u32[]{:S(2)}) collective-permute-start(bf16[512,1536]{1,0:T(8,128)(2,1)} %get-tuple-element.110), channel_id=1, source_target_pairs={{0,8},{8,16},{16,24},{1,9},{9,17},{17,25},{2,10},{10,18},{18,26},{... | collective-permute-start | bytes 4718600 | tf_op jit(solution)/shard_map/ppermute | solution.py:139
  927.1 151.9 %collective-permute-start.119 = (bf16[512,1536]{1,0:T(8,128)(2,1)}, bf16[512,1536]{1,0:T(8,128)(2,1)}, u32[]{:S(2)}, u32[]{:S(2)}) collective-permute-start(bf16[512,1536]{1,0:T(8,128)(2,1)} %fusion.45), channel_id=1, source_target_pairs={{8,0},{16,8},{24,16},{9,1},{17,9},{25,17},{10,2},{18,10},{26,18},{... | collective-permute-start | bytes 4718600 | tf_op jit(solution)/shard_map/ppermute | solution.py:142
  981.7 110.1 %collective-permute-start.125 = (bf16[512,1536]{1,0:T(8,128)(2,1)}, bf16[512,1536]{1,0:T(8,128)(2,1)}, u32[]{:S(2)}, u32[]{:S(2)}) collective-permute-start(bf16[512,1536]{1,0:T(8,128)(2,1)} %fusion.40), channel_id=1, source_target_pairs={{8,0},{16,8},{24,16},{9,1},{17,9},{25,17},{10,2},{18,10},{26,18},{... | collective-permute-start | bytes 4718600 | tf_op jit(solution)/shard_map/ppermute | solution.py:142
  984.5 126.7 %collective-permute-start.98 = (bf16[256,2048]{1,0:T(8,128)(2,1)}, bf16[256,2048]{1,0:T(8,128)(2,1)}, u32[]{:S(2)}, u32[]{:S(2)}) collective-permute-start(bf16[256,2048]{1,0:T(8,128)(2,1)} %get-tuple-element.70), channel_id=1, source_target_pairs={{0,1},{1,0},{2,3},{3,2},{4,5},{5,4},{6,7},{7,6},{8,9},{9,8},{10,11... | collective-permute-start | bytes 3145736 | tf_op jit(solution)/shard_map/ppermute | solution.py:31
  1099.5 96.4 %collective-permute-start.84 = (bf16[1024,2048]{1,0:T(8,128)(2,1)}, bf16[1024,2048]{1,0:T(8,128)(2,1)}, u32[]{:S(2)}, u32[]{:S(2)}) collective-permute-start(bf16[1024,2048]{1,0:T(8,128)(2,1)} %pad_maximum_fusion.8), channel_id=1, source_target_pairs={{0,1},{1,0},{2,3},{3,2},{4,5},{5,4},{6,7},{7,6},{8,9},{9,8},{10,11... | collective-permute-start | bytes 12582920 | tf_op jit(solution)/shard_map/ppermute | solution.py:31
  1111.2 74.0 %collective-permute-start.104 = (bf16[256,2048]{1,0:T(8,128)(2,1)}, bf16[256,2048]{1,0:T(8,128)(2,1)}, u32[]{:S(2)}, u32[]{:S(2)}) collective-permute-start(bf16[256,2048]{1,0:T(8,128)(2,1)} %pad_maximum_fusion.30), channel_id=1, source_target_pairs={{0,4},{1,5},{2,6},{3,7},{4,0},{5,1},{6,2},{7,3},{8,12},{9,13},{10,... | collective-permute-start | bytes 3145736 | tf_op jit(solution)/shard_map/ppermute | solution.py:31
  1185.1 99.3 %collective-permute-start.68 = (bf16[512,2048]{1,0:T(8,128)(2,1)}, bf16[512,2048]{1,0:T(8,128)(2,1)}, u32[]{:S(2)}, u32[]{:S(2)}) collective-permute-start(bf16[512,2048]{1,0:T(8,128)(2,1)} %pad_maximum_fusion.12), channel_id=1, source_target_pairs={{0,1},{1,0},{2,3},{3,2},{4,5},{5,4},{6,7},{7,6},{8,9},{9,8},{10,11... | collective-permute-start | bytes 6291464 | tf_op jit(solution)/shard_map/ppermute | solution.py:31
  1186.6 78.9 %collective-permute-start.97 = (bf16[256,768]{0,1:T(8,128)(2,1)}, bf16[256,768]{0,1:T(8,128)(2,1)S(1)}, u32[]{:S(2)}, u32[]{:S(2)}) collective-permute-start(bf16[256,768]{0,1:T(8,128)(2,1)} %dynamic-slice_convert_fusion.2), channel_id=1, source_target_pairs={{0,4},{4,0},{1,5},{5,1},{2,6},{6,2},{3,7},{7,3},{8,12},{12,8},{9,1... | collective-permute-start | bytes 1179656 | tf_op jit(solution)/shard_map/ppermute | solution.py:552
  1271.6 72.9 %collective-permute-start.90 = (bf16[512,2048]{1,0:T(8,128)(2,1)}, bf16[512,2048]{1,0:T(8,128)(2,1)}, u32[]{:S(2)}, u32[]{:S(2)}) collective-permute-start(bf16[512,2048]{1,0:T(8,128)(2,1)} %pad_maximum_fusion.16), channel_id=1, source_target_pairs={{0,1},{1,0},{2,3},{3,2},{4,5},{5,4},{6,7},{7,6},{8,9},{9,8},{10,11... | collective-permute-start | bytes 6291464 | tf_op jit(solution)/shard_map/ppermute | solution.py:31
  (207 other events, 3625.6 us)

commit v2 on v1

--- a/solution.py
+++ b/solution.py
@@ -356,6 +356,514 @@
     )(slots, qs, ks, vs, os, stats, go, cos, sin)
 
 
+def flip(index, bit):
+    return index + bit - 2 * bit * ((index // bit) % 2)
+
+
+def mlp_kernel(
+    dims, n_own, cot_in, wg, wu, wd,
+    dn_out, out_out, mine_out, got_out, g_hbm, r_hbm,
+    n2, cot, wgu_v, wd_v, hid, dgu, left_t, gt, st, ost, fin, away,
+    lev_send, lev_recv, x_own, x_send, x_recv, a_send, a_recv, g_sem, s_sem, rs_send, rs_recv, fx_send, fx_recv, o_sem, c_sem,
+):
+    shards, ctx, tensor, chunks, fc, rows_own, d_own = dims
+    group = ctx * tensor
+    rows, width = n2.shape
+    dz = ctx * d_own
+    ff = chunks * fc
+    z = lax.axis_index("shard")
+    x = lax.axis_index("ctx")
+    t = lax.axis_index("tensor")
+    bits_y, bits_x = level_bits(ctx, tensor)
+
+    def mesh_id(bit):
+        return (z, x, flip(t, bit)) if bit < tensor else (z, 1 - x, t)
+
+    def above():
+        return (z + 1, x, t)
+
+    def below():
+        return (z - 1, x, t)
+
+    barrier = pltpu.get_barrier_semaphore()
+    partners = [1] + bits_y + bits_x
+    for bit in partners:
+        pl.semaphore_signal(barrier, inc=1, device_id=mesh_id(bit), device_id_type=pl.DeviceIdType.MESH)
+
+    @pl.when(z < shards - 1)
+    def _():
+        pl.semaphore_signal(barrier, inc=1, device_id=above(), device_id_type=pl.DeviceIdType.MESH)
+
+    @pl.when(z > 0)
+    def _():
+        pl.semaphore_signal(barrier, inc=1, device_id=below(), device_id_type=pl.DeviceIdType.MESH)
+
+    peers = len(partners) + (z + shards - 1) // shards + (2 * shards - 2 - z) // shards
+    pl.semaphore_wait(barrier, peers)
+
+    here_too = (z, x, flip(t, 1))
+
+    def remote(src, dst, send, recv, where):
+        return pltpu.make_async_remote_copy(
+            src_ref=src, dst_ref=dst, send_sem=send, recv_sem=recv, device_id=where, device_id_type=pl.DeviceIdType.MESH
+        )
+
+    def x_copies(c, own):
+        half = x if own else 1 - x
+        low_c = pl.multiple_of(half * ff + c * fc, fc)
+        d_at = pl.ds(pl.multiple_of((z * ctx + x) * d_own, d_own), d_own)
+        pairs = [
+            (wg.at[:, pl.ds(low_c, fc)], wgu_v.at[c, d_at, pl.ds(0, fc)]),
+            (wu.at[:, pl.ds(low_c, fc)], wgu_v.at[c, d_at, pl.ds(fc, fc)]),
+            (wd.at[pl.ds(low_c, fc), :], wd_v.at[pl.ds(pl.multiple_of(c * fc, fc), fc), d_at]),
+        ]
+        if own:
+            return [pltpu.make_async_copy(a, b, x_own.at[c, i]) for i, (a, b) in enumerate(pairs)]
+        return [remote(a, b, x_send.at[c, i], x_recv.at[c, i], (z, 1 - x, t)) for i, (a, b) in enumerate(pairs)]
+
+    def x_landed(c):
+        d_at = pl.ds(pl.multiple_of((z * ctx + 1 - x) * d_own, d_own), d_own)
+        lands = [
+            wgu_v.at[c, d_at, pl.ds(0, fc)],
+            wgu_v.at[c, d_at, pl.ds(fc, fc)],
+            wd_v.at[pl.ds(pl.multiple_of(c * fc, fc), fc), d_at],
+        ]
+        return [remote(a, a, x_send.at[c, i], x_recv.at[c, i], here_too) for i, a in enumerate(lands)]
+
+    def hop(c, way, k, b, wait=False):
+        at = pl.ds(pl.multiple_of(b * dz, dz), dz)
+        parts = [wgu_v.at[c, at, :], wd_v.at[pl.ds(pl.multiple_of(c * fc, fc), fc), at]]
+        where = here_too if wait else above() if way == 0 else below()
+        return [remote(p, p, a_send.at[c, way, k, i], a_recv.at[c, way, k, i], where) for i, p in enumerate(parts)]
+
+    def hop_start(c, k):
+        @pl.when((z >= k - 1) & (z < shards - 1))
+        def _():
+            for d in hop(c, 0, k - 1, z - (k - 1)):
+                d.start()
+
+        @pl.when((z + k - 1 <= shards - 1) & (z > 0))
+        def _():
+            for d in hop(c, 1, k - 1, z + (k - 1)):
+                d.start()
+
+    def hop_sent(c, k):
+        @pl.when((z >= k - 1) & (z < shards - 1))
+        def _():
+            for d in hop(c, 0, k - 1, z - (k - 1)):
+                d.wait_send()
+
+        @pl.when((z + k - 1 <= shards - 1) & (z > 0))
+        def _():
+            for d in hop(c, 1, k - 1, z + (k - 1)):
+                d.wait_send()
+
+    def hop_wait(c, k):
+        @pl.when(z >= k)
+        def _():
+            for d in hop(c, 0, k - 1, z - k, True):
+                d.wait_recv()
+
+        @pl.when(z + k <= shards - 1)
+        def _():
+            for d in hop(c, 1, k - 1, z + k, True):
+                d.wait_recv()
+
+    def x_start(c):
+        for d in x_copies(c, False):
+            d.start()
+        for d in x_copies(c, True):
+            d.start()
+
+    x_start(0)
+
+    half = rows_own // 2
+
+    def lev(src_k, dst_k, part, sem, bit):
+        if part is None:
+            s = pl.ds(src_k * rows_own, rows_own)
+            e = pl.ds(dst_k * rows_own, rows_own)
+        else:
+            s = pl.ds(src_k * rows_own + part * half, half)
+            e = pl.ds(dst_k * rows_own + part * half, half)
+        return remote(n2.at[s, :], n2.at[e, :], lev_send.at[sem], lev_recv.at[sem], mesh_id(bit))
+
+    cot_copy = pltpu.make_async_copy(cot_in, cot, c_sem.at[0])
+    own_copy = pltpu.make_async_copy(n_own, n2.at[pl.ds(0, rows_own), :], c_sem.at[1])
+    own_copy.start()
+    cot_copy.start()
+    own_copy.wait()
+    sem = 0
+    started = []
+
+    def go(src_k, dst_k, part, bit):
+        nonlocal sem
+        d = lev(src_k, dst_k, part, sem, bit)
+        d.start()
+        sem += 1
+        started.append(d)
+        return d
+
+    first = go(0, 1, None, 1)
+    have = [[0], [0]]
+    orders = [bits_x + bits_y, bits_y + bits_x]
+    core_moves = [first]
+    arrived = {}
+    stages = len(orders[0])
+    pending = []
+    for stage in range(stages):
+        now = []
+        for part in (0, 1):
+            bit = orders[part][stage]
+            for k in have[part]:
+                now.append((part, k | bit, go(k, k | bit, part, bit)))
+        for part in (0, 1):
+            bit = orders[part][stage]
+            have[part] = have[part] + [k | bit for k in have[part]]
+        pending.append(now)
+        if stage == 0:
+            for c in range(1, chunks):
+                x_start(c)
+            for d in x_copies(0, True):
+                d.wait()
+            for d in x_landed(0):
+                d.wait_recv()
+            hop_start(0, 1)
+        for part, k, d in now:
+            d.wait_recv()
+            arrived[k] = arrived.get(k, 0) + 1
+            if arrived[k] == 2:
+                core_moves.append(go(k, k | 1, None, 1))
+
+    def ag_round(r, top):
+        for k in range(shards - 1, 0, -1):
+            if k > top:
+                continue
+            c = r - k + 1
+
+            @pl.when((c >= 0) & (c < chunks))
+            def _(c=c, k=k):
+                if k == 1:
+                    for d in x_copies(c, True):
+                        d.wait()
+                    for d in x_landed(c):
+                        d.wait_recv()
+                else:
+                    hop_wait(c, k - 1)
+                hop_start(c, k)
+
+    for r in range(1, shards - 1):
+        ag_round(jnp.int32(r), shards - 1)
+    for d in core_moves:
+        d.wait_recv()
+    cot_copy.wait()
+
+    def block_of(i):
+        down = shards - 1 - i
+        down = down - jnp.where(down <= z, 1, 0)
+        up = i + jnp.where(i >= z, 1, 0)
+        return jnp.where(i == shards - 1, z, jnp.where(2 * z < shards, down, up))
+
+    def g_copy(c, d, slot):
+        return pltpu.make_async_copy(gt.at[slot], g_hbm.at[c, d], g_sem.at[slot])
+
+    def rs_send_copy(src, c, way, d, wait=False):
+        where = here_too if wait else above() if way == 0 else below()
+        return remote(src, r_hbm.at[c, way, d], rs_send.at[c, way, d], rs_recv.at[c, way, d], where)
+
+    combos = [(way, k) for k in range(2, shards) for way in (0, 1)]
+
+    def target(way, k):
+        return z + shards - k if way == 0 else z - (shards - k)
+
+    def sends(way, k):
+        if way == 0:
+            return z < k
+        return z >= shards - k
+
+    def starts(way):
+        return z == 0 if way == 0 else z == shards - 1
+
+    def runs(way):
+        return z != 0 if way == 0 else z != shards - 1
+
+    def rs_step(s):
+        for way in (0, 1):
+            for k in range(1, shards):
+                c = s - (k - 1)
+
+                @pl.when((c >= 0) & (c < chunks) & starts(way))
+                def _(c=c, way=way, k=k):
+                    d = target(way, k)
+                    rs_send_copy(g_hbm.at[c, d], c, way, d).start()
+
+        for i, (way, k) in enumerate(combos):
+            c = s - (k - 1)
+
+            @pl.when((c >= 0) & (c < chunks) & sends(way, k) & runs(way))
+            def _(c=c, way=way, k=k, i=i):
+                d = target(way, k)
+
+                @pl.when(c >= 1)
+                def _():
+                    rs_send_copy(st.at[2 * i], c - 1, way, d).wait_send()
+
+                rs_send_copy(st.at[2 * i], c, way, d, True).wait_recv()
+                pltpu.make_async_copy(g_hbm.at[c, d], st.at[2 * i], s_sem.at[2 * i]).start()
+                pltpu.make_async_copy(r_hbm.at[c, way, d], st.at[2 * i + 1], s_sem.at[2 * i + 1]).start()
+
+        last = 2 * len(combos)
+        c_fin = s - (shards - 1)
+
+        @pl.when((c_fin >= 0) & (c_fin < chunks))
+        def _():
+            pltpu.make_async_copy(g_hbm.at[c_fin, z], st.at[last], s_sem.at[last]).start()
+            for way in (0, 1):
+                slot = last + 1 + way
+
+                @pl.when(runs(way))
+                def _(way=way, slot=slot):
+                    rs_send_copy(st.at[slot], c_fin, way, z, True).wait_recv()
+                    pltpu.make_async_copy(r_hbm.at[c_fin, way, z], st.at[slot], s_sem.at[slot]).start()
+
+                @pl.when(starts(way))
+                def _(slot=slot):
+                    st[slot] = jnp.zeros(st.shape[1:], BF)
+
+        for i, (way, k) in enumerate(combos):
+            c = s - (k - 1)
+
+            @pl.when((c >= 0) & (c < chunks) & sends(way, k) & runs(way))
+            def _(c=c, way=way, k=k, i=i):
+                d = target(way, k)
+                pltpu.make_async_copy(g_hbm.at[c, d], st.at[2 * i], s_sem.at[2 * i]).wait()
+                pltpu.make_async_copy(r_hbm.at[c, way, d], st.at[2 * i + 1], s_sem.at[2 * i + 1]).wait()
+                st[2 * i] = (st[2 * i].astype(F32) + st[2 * i + 1].astype(F32)).astype(BF)
+                rs_send_copy(st.at[2 * i], c, way, d).start()
+
+        @pl.when((c_fin >= 0) & (c_fin < chunks))
+        def _():
+            pltpu.make_async_copy(g_hbm.at[c_fin, z], st.at[last], s_sem.at[last]).wait()
+            for way in (0, 1):
+                slot = last + 1 + way
+
+                @pl.when(runs(way))
+                def _(way=way, slot=slot):
+                    pltpu.make_async_copy(r_hbm.at[c_fin, way, z], st.at[slot], s_sem.at[slot]).wait()
+
+            @pl.when(c_fin >= 1)
+            def _():
+                pltpu.make_async_copy(fin, mine_out.at[c_fin - 1], c_sem.at[2]).wait()
+                fin_copy(c_fin - 1).wait_send()
+
+            total = st[last].astype(F32) + st[last + 1].astype(F32) + st[last + 2].astype(F32)
+            low, high = total[:, :d_own], total[:, d_own:]
+            fin[...] = jnp.where(x == 0, low, high)
+            away[...] = jnp.where(x == 0, high, low).astype(BF)
+            pltpu.make_async_copy(fin, mine_out.at[c_fin], c_sem.at[2]).start()
+            fin_copy(c_fin).start()
+
+    def fin_copy(c):
+        return remote(away, got_out.at[c], fx_send.at[c], fx_recv.at[c], (z, 1 - x, t))
+
+    tile = 512
+
+    def phase_one(c):
+        def body(r, carry):
+            at = pl.ds(pl.multiple_of(r * tile, tile), tile)
+            gu = mm(n2[at, :], wgu_v[c])
+            dh = mm(cot[at, :], wd_v[pl.ds(pl.multiple_of(c * fc, fc), fc), :], NT)
+            gate, up = gu[:, :fc], gu[:, fc:]
+            sig = 1.0 / (1.0 + jnp.exp(-gate))
+            act = gate * sig
+            h = (act * up).astype(BF)
+            dg = (dh * up * sig * (1.0 + gate * (1.0 - sig))).astype(BF)
+            du = (dh * act).astype(BF)
+            hid[c, at, :] = h
+            dgu[c, at, 0:fc] = dg
+            dgu[c, at, fc : 2 * fc] = du
+            left_t[0:fc, at] = h.T
+            left_t[fc : 2 * fc, at] = dg.T
+            left_t[2 * fc : 3 * fc, at] = du.T
+            return carry
+
+        lax.fori_loop(0, rows // tile, body, 0)
+
+    def phase_two(c):
+        def body(i, carry):
+            d = block_of(i)
+            slot = i % 2
+            at = pl.ds(pl.multiple_of(d * dz, dz), dz)
+
+            @pl.when(i >= 2)
+            def _():
+                g_copy(c, block_of(i - 2), slot).wait()
+
+            gt[slot, 0:fc, :] = mm(left_t[0:fc, :], cot[:, at]).astype(BF)
+            gt[slot, fc : 3 * fc, :] = mm(left_t[fc : 3 * fc, :], n2[:, at]).astype(BF)
+            g_copy(c, d, slot).start()
+            return carry
+
+        lax.fori_loop(0, shards, body, 0)
+        for i in (shards - 2, shards - 1):
+            g_copy(c, block_of(jnp.int32(i)), i % 2).wait()
+
+    ot = 256
+    units = rows // ot
+
+    def tail_unit(u):
+        at = pl.ds(pl.multiple_of((u % units) * ot, ot), ot)
+        slot = u % 2
+
+        @pl.when(u >= 2)
+        def _():
+            pltpu.make_async_copy(ost.at[slot], dn_out.at[at, :], o_sem.at[slot]).wait()
+
+        @pl.when(u < units)
+        def _():
+            for n in range(width // 512):
+                cols = slice(n * 512, (n + 1) * 512)
+                acc = jnp.zeros((ot, 512), F32)
+                for c in range(chunks):
+                    acc = acc + mm(dgu[c, at, :], wgu_v[c, cols, :], NT)
+                ost[slot, :, cols] = acc.astype(BF)
+            pltpu.make_async_copy(ost.at[slot], dn_out.at[at, :], o_sem.at[slot]).start()
+
+        @pl.when(u >= units)
+        def _():
+            for n in range(width // 512):
+                cols = slice(n * 512, (n + 1) * 512)
+                acc = jnp.zeros((ot, 512), F32)
+                for c in range(chunks):
+                    acc = acc + mm(hid[c, at, :], wd_v[c * fc : (c + 1) * fc, cols])
+                ost[slot, :, cols] = acc.astype(BF)
+            pltpu.make_async_copy(ost.at[slot], out_out.at[at, :], o_sem.at[slot]).start()
+
+    tail_slots = shards - 1
+    per_slot = -(-2 * units // tail_slots)
+
+    def slot_body(s, carry):
+        @pl.when(s < chunks)
+        def _():
+            hop_wait(s, shards - 1)
+            phase_one(s)
+            ag_round(s + shards - 1, shards - 1)
+            phase_two(s)
+
+        @pl.when(s >= chunks)
+        def _():
+            first_u = (s - chunks) * per_slot
+            last_u = jnp.minimum(first_u + per_slot, 2 * units)
+
+            def body(u, carry):
+                tail_unit(u)
+                return carry
+
+            lax.fori_loop(first_u, last_u, body, 0)
+
+        rs_step(s)
+        return carry
+
+    lax.fori_loop(0, chunks + tail_slots, slot_body, 0)
+
+    for u in (2 * units - 2, 2 * units - 1):
+        at = pl.ds((u % units) * ot, ot)
+        pltpu.make_async_copy(ost.at[u % 2], out_out.at[at, :], o_sem.at[u % 2]).wait()
+    for d in started:
+        d.wait_send()
+    for c in range(chunks):
+        for d in x_copies(c, False):
+            d.wait_send()
+        for k in range(1, shards):
+            hop_sent(c, k)
+    for way in (0, 1):
+        for k in range(1, shards):
+
+            @pl.when(starts(way))
+            def _(way=way, k=k):
+                d = target(way, k)
+                for c in range(chunks):
+                    rs_send_copy(g_hbm.at[c, d], c, way, d).wait_send()
+
+    for i, (way, k) in enumerate(combos):
+
+        @pl.when(sends(way, k) & runs(way))
+        def _(way=way, k=k, i=i):
+            rs_send_copy(st.at[2 * i], chunks - 1, way, target(way, k)).wait_send()
+
+    pltpu.make_async_copy(fin, mine_out.at[chunks - 1], c_sem.at[2]).wait()
+    fin_copy(chunks - 1).wait_send()
+    for c in range(chunks):
+        fin_copy(c).wait_recv()
+
+
+def mlp_call(shards, ctx, tensor, n_own, cot, wg, wu, wd):
+    rows_own, width = n_own.shape
+    group = ctx * tensor
+    rows = rows_own * group
+    d_own = wg.shape[0]
+    ff = wg.shape[1] // ctx
+    fc = 256
+    chunks = ff // fc
+    dz = ctx * d_own
+    any_spec = pl.BlockSpec(memory_space=pl.ANY)
+    bits_y, bits_x = level_bits(ctx, tensor)
+    halves = 2 ** (len(bits_y) + len(bits_x)) - 1
+    moves = 2 * halves + halves + 1
+    stage = 4 * (shards - 2) + 3
+    dims = (shards, ctx, tensor, chunks, fc, rows_own, d_own)
+    dma = pltpu.SemaphoreType.DMA
+    return pl.pallas_call(
+        functools.partial(mlp_kernel, dims),
+        in_specs=[any_spec] * 5,
+        out_specs=[any_spec] * 6,
+        out_shape=[
+            jax.ShapeDtypeStruct((rows, width), BF),
+            jax.ShapeDtypeStruct((rows, width), BF),
+            jax.ShapeDtypeStruct((chunks, 3 * fc, d_own), F32),
+            jax.ShapeDtypeStruct((chunks, 3 * fc, d_own), BF),
+            jax.ShapeDtypeStruct((chunks, shards, 3 * fc, dz), BF),
+            jax.ShapeDtypeStruct((chunks, 2, shards, 3 * fc, dz), BF),
+        ],
+        scratch_shapes=[
+            pltpu.VMEM((rows, width), BF),
+            pltpu.VMEM((rows, width), BF),
+            pltpu.VMEM((chunks, width, 2 * fc), BF),
+            pltpu.VMEM((ff, width), BF),
+            pltpu.VMEM((chunks, rows, fc), BF),
+            pltpu.VMEM((chunks, rows, 2 * fc), BF),
+            pltpu.VMEM((3 * fc, rows), BF),
+            pltpu.VMEM((2, 3 * fc, dz), BF),
+            pltpu.VMEM((stage, 3 * fc, dz), BF),
+            pltpu.VMEM((2, 256, width), BF),
+            pltpu.VMEM((3 * fc, d_own), F32),
+            pltpu.VMEM((3 * fc, d_own), BF),
+            dma((moves,)),
+            dma((moves,)),
+            dma((chunks, 3)),
+            dma((chunks, 3)),
+            dma((chunks, 3)),
+            dma((chunks, 2, shards - 1, 2)),
+            dma((chunks, 2, shards - 1, 2)),
+            dma((2,)),
+            dma((stage,)),
+            dma((chunks, 2, shards)),
+            dma((chunks, 2, shards)),
+            dma((chunks,)),
+            dma((chunks,)),
+            dma((2,)),
+            dma((3,)),
+        ],
+        compiler_params=pltpu.CompilerParams(
+            collective_id=1, has_side_effects=True, vmem_limit_bytes=63 * 1024 * 1024
+        ),
+        cost_estimate=pl.CostEstimate(
+            flops=18 * rows * width * ff, bytes_accessed=100 * 1024 * 1024, transcendentals=rows * ff
+        ),
+        name="feed_forward",
+    )(n_own, cot, wg, wu, wd)
+
+
 def per_device(
     shards, ctx, tensor, tokens, cotangent, seq_len, block_slot, attn_gain, w_query, w_key, w_value, w_out, mlp_gain, w_gate, w_up, w_down
 ):
@@ -446,49 +954,14 @@
     scale_two = lax.rsqrt(jnp.mean(hidden_res * hidden_res, axis=-1, keepdims=True) + EPS)
     normed_two = hidden_res * scale_two
     n_two_own = (normed_two * gain_two).astype(BF)
-    n_two = jnp.concatenate(level_gather(n_two_own, ctx, tensor), axis=0)
     cot, cot_own = level_rows_of(cotangent)
-
-    chunks = 2
-    fc = ff // chunks
-    w_down_t = w_down.T
-    chunk_grads = []
-    gu_all, hid_all, w_gu_all, w_dt_all = [], [], [], []
-    for c in range(chunks):
-        mine_parts, other_parts = [], []
-        for w in (w_gate, w_up, w_down_t):
-            mine_parts.append(lax.dynamic_slice_in_dim(w, my_x * ff + c * fc, fc, axis=1))
-            other_parts.append(lax.dynamic_slice_in_dim(w, (1 - my_x) * ff + c * fc, fc, axis=1))
-        mine = jnp.concatenate(mine_parts, axis=1)
-        got = lax.ppermute(jnp.concatenate(other_parts, axis=1), "ctx", swap_x)
-        weights = in_order(chain_gather(x_join(mine, got, 0), shards), shards).reshape(width, 3 * fc)
-        w_gu, w_dt = weights[:, : 2 * fc], weights[:, 2 * fc :]
-        gate_up = mm(n_two, w_gu)
-        gate, up = gate_up[:, :fc], gate_up[:, fc:]
-        sig = jax.nn.sigmoid(gate)
-        act = gate * sig
-        hidden = (act * up).astype(BF)
-        d_hidden = mm(cot, w_dt)
-        d_gate = (d_hidden * up * sig * (1.0 + gate * (1.0 - sig))).astype(BF)
-        d_up = (d_hidden * act).astype(BF)
-        d_gu = jnp.concatenate([d_gate, d_up], axis=1)
-        grad_gu = mm(n_two, d_gu, TN).astype(BF)
-        grad_dt = mm(cot, hidden, TN).astype(BF)
-        chunk_grads.append(jnp.concatenate([grad_gu, grad_dt], axis=1))
-        gu_all.append(d_gu)
-        hid_all.append(hidden)
-        w_gu_all.append(w_gu)
-        w_dt_all.append(w_dt)
-    d_gu = jnp.concatenate(gu_all, axis=1)
-    hidden = jnp.concatenate(hid_all, axis=1)
-    w_gu = jnp.concatenate(w_gu_all, axis=1)
-    w_dt = jnp.concatenate(w_dt_all, axis=1)
+    dn_part, out_part, ff_mine, ff_got, _, _ = mlp_call(shards, ctx, tensor, n_two_own, cot, w_gate, w_up, w_down)
 
     def row_blocks(array):
         return [array[k * own_rows : (k + 1) * own_rows] for k in range(group)]
 
-    d_n_two = level_sum(row_blocks(mm(d_gu, w_gu, NT).astype(BF)), ctx, tensor)
-    out_own = hidden_res + level_sum(row_blocks(mm(hidden, w_dt, NT).astype(BF)), ctx, tensor)
+    d_n_two = level_sum(row_blocks(dn_part), ctx, tensor)
+    out_own = hidden_res + level_sum(row_blocks(out_part), ctx, tensor)
 
     def tensor_rows(own):
         have = [(0, own)]
@@ -503,12 +976,6 @@
         return ordered.reshape(tensor * own_rows, width)
 
     result = tensor_rows(out_own.astype(BF))
-
-    def mlp_sums(chunk):
-        total = chain_sum(chunk.reshape(shards, ctx * d_own, 3 * fc), shards)
-        mine, other = x_halves(total, 0)
-        got = lax.ppermute(other.astype(BF), "ctx", swap_x).astype(F32)
-        return mine, got
 
     cot_f = cot_own.astype(F32)
     scaled = d_n_two * gain_two
@@ -536,15 +1003,17 @@
     gain_one_part = jnp.sum(d_n_one * x_normed, axis=0)
     grad_x = tensor_rows(d_x.astype(BF))
 
-    def spread(parts, axis):
-        mine = jnp.concatenate([m for m, _ in parts], axis=axis) if len(parts) > 1 else parts[0][0]
-        got = jnp.concatenate([g for _, g in parts], axis=axis) if len(parts) > 1 else parts[0][1]
-        return x_join(mine, got, axis)
-
-    sums = [mlp_sums(g) for g in chunk_grads]
-    grad_gate = spread([(m[:, :fc], g[:, :fc]) for m, g in sums], 1)
-    grad_up = spread([(m[:, fc : 2 * fc], g[:, fc : 2 * fc]) for m, g in sums], 1)
-    grad_down = spread([(m[:, 2 * fc :], g[:, 2 * fc :]) for m, g in sums], 1).T
+    chunks = ff_mine.shape[0]
+    fc = ff // chunks
+    mine = ff_mine.reshape(chunks, 3, fc, d_own)
+    got = ff_got.reshape(chunks, 3, fc, d_own).astype(F32)
+
+    def spread(i):
+        return x_join(mine[:, i].reshape(ff, d_own), got[:, i].reshape(ff, d_own), 0)
+
+    grad_down = spread(0)
+    grad_gate = spread(1).T
+    grad_up = spread(2).T
 
     def attn_sums(array):
         total = chain_sum(array.reshape(shards, ctx * d_own, array.shape[1]), shards)

time: 1370 us -> 1280 us (0.934)
  Pallas kernels: 102 us -> 513 us
  matrix products: 157 us -> 33.2 us
  waiting for transfers between devices: 352 us -> 246 us
  other arithmetic: 242 us -> 143 us
  local copies, waits for them, and re-layouts: 268 us -> 171 us
  starting transfers between devices: 198 us -> 118 us
    pallas_call x0 -> x1, Pallas kernels: none -> 411 us  [mlp_call(): pl.pallas_call(functools.partial(mlp_kernel, dims), in_specs=[any_spec] *...]
    dot_general x10 -> x4, matrix products: 97.9 us -> 27.1 us  [mm(): return lax.dot_general(left, right, dims, preferred_element_type=F32)]
    ppermute x15 -> x9, waiting for transfers between devices: 86.3 us -> 30.1 us  [chain_gather(): lax.ppermute(down, 'shard', [(i, i - 1) for i in range(1, shards - k + 1)])]
    dot_general x5 -> x1, matrix products: 59.2 us -> 6.08 us  [mm(): return jnp.dot(left, right, preferred_element_type=F32)]
    ppermute x12 -> x6, waiting for transfers between devices: 49.7 us -> 4 us  [chain_sum(): up = lax.ppermute(send, 'shard', [(i, i + 1) for i in range(0, k)])]
    unnamed x289 -> x170, local copies, waits for them, and re-layouts: 100 us -> 57 us
    ppermute x12 -> x6, starting transfers between devices: 60.9 us -> 22.7 us  [chain_sum(): up = lax.ppermute(send, 'shard', [(i, i + 1) for i in range(0, k)])]
    ppermute x66 -> x57, waiting for transfers between devices: 169 us -> 202 us  [swap(): return lax.ppermute(value, LEVEL, [(i, i ^ bit) for i in range(group)])]
  transfers between devices with their start and end apart: 128 -> 91, of which waited for: 47 -> 36; matrix products, arithmetic and copies ran while one was open for 41% -> 24% of each run, Pallas kernels for 7% -> 8%
where the time goes in v2:
time: 1280 us; the launch traced here: 1270 us
  Pallas kernels  513 us (40%)
  waiting for transfers between devices  246 us (19%)
  local copies, waits for them, and re-layouts  171 us (13%)
  other arithmetic  143 us (11%)
  starting transfers between devices  118 us (9%)
  blocking collectives  38.1 us (3%)
  matrix products  33.2 us (3%)
    pallas_call x1, Pallas kernels, mlp_call(): pl.pallas_call(functools.partial(mlp_kernel, dims), in_specs=[any_spec] *...  411 us
    ppermute x57, waiting for transfers between devices, swap(): return lax.ppermute(value, LEVEL, [(i, i ^ bit) for i in range(group)])  202 us
    unnamed x170, local copies, waits for them, and re-layouts  57 us
    pallas_call x1, Pallas kernels, attend_back_call(): pl.pallas_call(attend_back_kernel, grid_spec=pltpu.PrefetchScalarGridSpec...  48.6 us
    ppermute x57, starting transfers between devices, swap(): return lax.ppermute(value, LEVEL, [(i, i ^ bit) for i in range(group)])  47.5 us
    pallas_call x1, Pallas kernels, attend_call(): pl.pallas_call(attend_kernel, grid_spec=pltpu.PrefetchScalarGridSpec(num_...  40.5 us
    psum x1, blocking collectives, gain_sum(): total = lax.psum(part, ('shard', 'ctx', 'tensor'))  38.1 us
    ppermute x9, waiting for transfers between devices, chain_gather(): lax.ppermute(down, 'shard', [(i, i - 1) for i in range(1, shards - k + 1)])  30.1 us
  transfers between devices with their start and end apart: 91, of which 36 were waited for; matrix products, arithmetic and copies ran while one was open for 24% of the time, Pallas kernels for 8%

profile of v2, /device:TPU:0, one launch (start us, length us, event | category | flops | bytes accessed | tf_op | source)
XLA Modules:
  0.0 1266.3 jit_solution(8015458052277756462)
XLA Ops:
  1.9 6.3 collective-permute-start.24
  71.0 6.9 collective-permute-start.11
  82.3 10.4 collective-permute-done.27
  94.0 12.2 collective-permute-done.39
  133.1 10.5 collective-permute-done.1
  145.2 20.8 %collective-permute-done.40 = bf16[256,2048]{1,0:T(8,128)(2,1)S(1)} collective-permute-done((bf16[256,2048]{1,0:T(8,128)(2,1)S(1)}, bf16[256,2048]{1,0:T(8,128)(2,1)S(1)}, u32[]{:S(2)}, u32[]{:S(2)}) %collective-permute-start.40) | collective-permute-done | bytes 1048608 | tf_op jit(solution)/shard_map/ppermute | solution.py:31
  168.3 11.9 collective-permute-done.32
  188.5 6.8 collective-permute-done.14
  213.5 8.4 gather_fusion.2
  221.9 7.8 broadcast_select_fusion.1
  229.6 6.0 fusion.54
  245.9 7.7 pad_maximum_fusion
  253.5 17.7 %fusion = bf16[4,512,4,2,256]{4,3,2,1,0:T(2,128)(2,1)} fusion(bf16[2,4,4,512,256]{4,3,1,0,2:T(8,128)(2,1)} %bitcast.231, pred[4]{0:T(512)(128)(4,1)S(1)} %copy-done.40), kind=kLoop, calls=%fused_computation.13 | loop fusion | flops 4194304 | bytes 16777220 | tf_op jit(solution)/shard_map/transpose | solution.py:950
  271.2 14.4 %reshape.338 = bf16[2048,2048]{1,0:T(8,128)(2,1)} reshape(bf16[4,512,4,2,256]{4,3,2,1,0:T(2,128)(2,1)} %fusion) | data formatting | bytes 16777216 | tf_op jit(solution)/shard_map/reshape | solution.py:950
  292.6 13.2 %norm_qkv.1 = (bf16[2048,2048]{1,0:T(8,128)(2,1)}, f32[2048,768]{1,0:T(8,128)}) custom-call(bf16[2048,2048]{1,0:T(8,128)(2,1)} %slice_dynamic-update-slice_fusion.2.tok_ref, f32[1,2048]{1,0:T(1,128)S(1)} %bitcast.225, bf16[2048,768]{1,0:T(8,128)(2,1)S(1)} %bitcast_select_fusion.w_ref), custom_call_target="tpu_custom_call" | custom-call | flops 6442450944 | bytes 26214400 | tf_op jit(solution)/shard_map/norm_qkv/pallas_call | solution.py:158
  305.8 40.5 %attend.1 = (bf16[2048,256]{1,0:T(8,128)(2,1)}, bf16[2048,256]{1,0:T(8,128)(2,1)}, bf16[2048,256]{1,0:T(8,128)(2,1)}, bf16[2048,256]{1,0:T(8,128)(2,1)}, bf16[2048,256]{1,0:T(8,128)(2,1)}, /*index=5*/f32[8,2048]{1,0:T(8,128)}) custom-call(s32[17]{0:T(128)} %pad_add_fusion.slots, f32[2048,768]{1,0:T(8,128)} %get-tuple-element.25.lin_ref, ...), custom_call_target="tpu_custom_call" | custom-call | flops 8589934592 | bytes 11534336 | tf_op jit(solution)/shard_map/attend/pallas_call | solution.py:251
  369.3 6.1 multiply_reduce_fusion.2
  377.9 411.1 %feed_forward.1 = (bf16[2048,2048]{1,0:T(8,128)(2,1)}, bf16[2048,2048]{1,0:T(8,128)(2,1)}, f32[4,768,256]{2,1,0:T(8,128)}, bf16[4,768,256]{2,1,0:T(8,128)(2,1)},...) custom-call(bf16[256,2048]{1,0:T(8,128)(2,1)} %multiply_convert_fusion.n_own, ...), custom_call_target="tpu_custom_call" | custom-call | flops 77309411328 | bytes 104857600 | tf_op jit(solution)/shard_map/feed_forward/pallas_call | solution.py:816
  827.6 18.4 %collective-permute-done.45 = bf16[256,2048]{1,0:T(8,128)(2,1)S(1)} collective-permute-done((bf16[256,2048]{1,0:T(8,128)(2,1)S(1)}, bf16[256,2048]{1,0:T(8,128)(2,1)S(1)}, u32[]{:S(2)}, u32[]{:S(2)}) %collective-permute-start.45) | collective-permute-done | bytes 1048608 | tf_op jit(solution)/shard_map/ppermute | solution.py:31
  849.9 18.6 %collective-permute-done.52 = bf16[256,2048]{1,0:T(8,128)(2,1)S(1)} collective-permute-done((bf16[256,2048]{1,0:T(8,128)(2,1)S(1)}, bf16[256,2048]{1,0:T(8,128)(2,1)S(1)}, u32[]{:S(2)}, u32[]{:S(2)}) %collective-permute-start.52) | collective-permute-done | bytes 1048608 | tf_op jit(solution)/shard_map/ppermute | solution.py:31
  872.4 9.6 collective-permute-done.46
  882.5 10.0 collective-permute-done.53
  914.7 10.8 collective-permute-done.56
  937.5 48.6 %attend_back.1 = bf16[2048,768]{1,0:T(8,128)(2,1)} custom-call(s32[17]{0:T(128)} %pad_add_fusion.slots, bf16[2048,256]{1,0:T(8,128)(2,1)} %get-tuple-element.29.qs, bf16[2048,256]{1,0:T(8,128)(2,1)} %get-tuple-element.30.ks, bf16[2048,256]{1,0:T(8,128)(2,1)} %get-tuple-element.31.vs, bf16[2048,256]{1,0:T(8,128)(2,1)} %get-tuple-element.32.os, ...), custom_call_target="tpu_custom_call" | custom-call | flops 21474836480 | bytes 9437184 | tf_op jit(solution)/shard_map/attend_back/pallas_call | solution.py:336
  986.2 11.5 convolution_convert_fusion
  997.7 9.4 convolution_convert_fusion.1
  1045.9 15.8 %collective-permute-done.47 = bf16[256,2048]{1,0:T(8,128)(2,1)S(1)} collective-permute-done((bf16[256,2048]{1,0:T(8,128)(2,1)S(1)}, bf16[256,2048]{1,0:T(8,128)(2,1)S(1)}, u32[]{:S(2)}, u32[]{:S(2)}) %collective-permute-start.47) | collective-permute-done | bytes 1048608 | tf_op jit(solution)/shard_map/ppermute | solution.py:31
  1065.5 8.3 collective-permute-start.70
  1076.8 9.8 collective-permute-done.77
  1105.3 23.1 %collective-permute-done.64 = bf16[256,2048]{1,0:T(8,128)(2,1)S(1)} collective-permute-done((bf16[256,2048]{1,0:T(8,128)(2,1)S(1)}, bf16[256,2048]{1,0:T(8,128)(2,1)S(1)}, u32[]{:S(2)}, u32[]{:S(2)}) %collective-permute-start.64) | collective-permute-done | bytes 1048608 | tf_op jit(solution)/shard_map/ppermute | solution.py:31
  1208.9 38.1 %all-reduce = (f32[2048]{0:T(1024)S(1)}, f32[2048]{0:T(1024)S(1)}) all-reduce(f32[2048]{0:T(1024)S(1)} %get-tuple-element.59, f32[2048]{0:T(1024)S(1)} %copy-done.35), channel_id=1, replica_groups=mesh['shard'=4,'ctx'=2,'tensor'=4] {'shard','ctx','tensor'}, use_global_device_ids=true, to_apply=%region_5.8 | all-reduce | flops 4096 | bytes 32768 | tf_op jit(solution)/shard_map/psum | solution.py:1032
  1258.4 7.7 broadcast_select_fusion.2
  (510 shorter events, 404.7 us)
Async XLA Ops:
  0.6 67.3 %collective-permute-start.25 = (bf16[512,256]{1,0:T(8,128)(2,1)}, bf16[512,256]{1,0:T(8,128)(2,1)}, u32[]{:S(2)}, u32[]{:S(2)}) collective-permute-start(bf16[512,256]{1,0:T(8,128)(2,1)} %param.25), channel_id=1, source_target_pairs={{8,0},{16,8},{24,16},{9,1},{17,9},{25,17},{10,2},{18,10},{26,18},{... | collective-permute-start | bytes 786440 | tf_op jit(solution)/shard_map/ppermute | solution.py:114
  1.9 63.8 %collective-permute-start.24 = (bf16[512,256]{1,0:T(8,128)(2,1)}, bf16[512,256]{1,0:T(8,128)(2,1)}, u32[]{:S(2)}, u32[]{:S(2)}) collective-permute-start(bf16[512,256]{1,0:T(8,128)(2,1)} %param.25), channel_id=1, source_target_pairs={{0,8},{8,16},{16,24},{1,9},{9,17},{17,25},{2,10},{10,18},{18,26},{... | collective-permute-start | bytes 786440 | tf_op jit(solution)/shard_map/ppermute | solution.py:113
  11.1 59.5 %collective-permute-start.10 = (bf16[256,768]{1,0:T(8,128)(2,1)}, bf16[256,768]{1,0:T(8,128)(2,1)S(1)}, u32[]{:S(2)}, u32[]{:S(2)}) collective-permute-start(bf16[256,768]{1,0:T(8,128)(2,1)} %pad_maximum_fusion.25), channel_id=1, source_target_pairs={{0,4},{4,0},{1,5},{5,1},{2,6},{6,2},{3,7},{7,3},{8,12},{12,8},{9,1... | collective-permute-start | bytes 1179656 | tf_op jit(solution)/shard_map/ppermute | solution.py:925
  14.4 30.6 %collective-permute-start.3 = (bf16[2,256]{1,0:T(2,128)(2,1)S(1)}, bf16[2,256]{1,0:T(2,128)(2,1)S(1)}, u32[]{:S(2)}, u32[]{:S(2)}) collective-permute-start(bf16[2,256]{1,0:T(2,128)(2,1)S(1)} %pad_maximum_fusion.27), channel_id=1, source_target_pairs={{0,4},{4,0},{1,5},{5,1},{2,6},{6,2},{3,7},{7,3},{8,12},{12,8},{9,1... | collective-permute-start | bytes 3080 | tf_op jit(solution)/shard_map/ppermute | solution.py:918
  57.5 36.2 %collective-permute-start = (bf16[256,2048]{1,0:T(8,128)(2,1)}, bf16[256,2048]{1,0:T(8,128)(2,1)S(1)}, u32[]{:S(2)}, u32[]{:S(2)}) collective-permute-start(bf16[256,2048]{1,0:T(8,128)(2,1)} %slice_bitcast_fusion.5), channel_id=1, source_target_pairs={{0,4},{1,5},{2,6},{3,7},{4,0},{5,1},{6,2},{7,3},{8,12},{9,13},{10,... | collective-permute-start | bytes 3145736 | tf_op jit(solution)/shard_map/ppermute | solution.py:31
  65.5 40.7 %collective-permute-start.39 = (bf16[256,2048]{1,0:T(8,128)(2,1)}, bf16[256,2048]{1,0:T(8,128)(2,1)S(1)}, u32[]{:S(2)}, u32[]{:S(2)}) collective-permute-start(bf16[256,2048]{1,0:T(8,128)(2,1)} %slice_bitcast_fusion.4), channel_id=1, source_target_pairs={{0,4},{1,5},{2,6},{3,7},{4,0},{5,1},{6,2},{7,3},{8,12},{9,13},{10,... | collective-permute-start | bytes 3145736 | tf_op jit(solution)/shard_map/ppermute | solution.py:31
  71.0 39.3 %collective-permute-start.11 = (bf16[512,768]{1,0:T(8,128)(2,1)S(1)}, bf16[512,768]{1,0:T(8,128)(2,1)S(1)}, u32[]{:S(2)}, u32[]{:S(2)}) collective-permute-start(bf16[512,768]{1,0:T(8,128)(2,1)S(1)} %maximum_select_fusion.4), channel_id=1, source_target_pairs={{0,8},{8,16},{16,24},{1,9},{9,17},{17,25},{2,10},{10,18},{18,26},{... | collective-permute-start | bytes 2359304 | tf_op jit(solution)/shard_map/ppermute | solution.py:113
  80.0 30.4 %collective-permute-start.12 = (bf16[512,768]{1,0:T(8,128)(2,1)S(1)}, bf16[512,768]{1,0:T(8,128)(2,1)S(1)}, u32[]{:S(2)}, u32[]{:S(2)}) collective-permute-start(bf16[512,768]{1,0:T(8,128)(2,1)S(1)} %maximum_select_fusion.4), channel_id=1, source_target_pairs={{8,0},{16,8},{24,16},{9,1},{17,9},{25,17},{10,2},{18,10},{26,18},{... | collective-permute-start | bytes 2359304 | tf_op jit(solution)/shard_map/ppermute | solution.py:114
  93.6 31.8 %collective-permute-start.30 = (bf16[4,512,256]{2,1,0:T(8,128)(2,1)S(1)}, bf16[4,512,256]{2,1,0:T(8,128)(2,1)S(1)}, u32[]{:S(2)}, u32[]{:S(2)}) collective-permute-start(bf16[4,512,256]{2,1,0:T(8,128)(2,1)S(1)} %pad_maximum_fusion.15), channel_id=1, source_target_pairs={{0,1},{1,0},{2,3},{3,2},{4,5},{5,4},{6,7},{7,6},{8,9},{9,8},{10,11... | collective-permute-start | bytes 3145736 | tf_op jit(solution)/shard_map/ppermute | solution.py:31
  110.3 33.3 %collective-permute-start.1 = (bf16[256,2048]{1,0:T(8,128)(2,1)S(1)}, bf16[256,2048]{1,0:T(8,128)(2,1)S(1)}, u32[]{:S(2)}, u32[]{:S(2)}) collective-permute-start(bf16[256,2048]{1,0:T(8,128)(2,1)S(1)} %collective-permute-done), channel_id=1, source_target_pairs={{0,2},{1,3},{2,0},{3,1},{4,6},{5,7},{6,4},{7,5},{8,10},{9,11},{10,... | collective-permute-start | bytes 3145736 | tf_op jit(solution)/shard_map/ppermute | solution.py:31
  121.2 44.8 %collective-permute-start.40 = (bf16[256,2048]{1,0:T(8,128)(2,1)S(1)}, bf16[256,2048]{1,0:T(8,128)(2,1)S(1)}, u32[]{:S(2)}, u32[]{:S(2)}) collective-permute-start(bf16[256,2048]{1,0:T(8,128)(2,1)S(1)} %collective-permute-done.39), channel_id=1, source_target_pairs={{0,2},{1,3},{2,0},{3,1},{4,6},{5,7},{6,4},{7,5},{8,10},{9,11},{10,... | collective-permute-start | bytes 3145736 | tf_op jit(solution)/shard_map/ppermute | solution.py:31
  125.4 54.8 %collective-permute-start.32 = (bf16[4,512,256]{2,1,0:T(8,128)(2,1)S(1)}, bf16[4,512,256]{2,1,0:T(8,128)(2,1)}, u32[]{:S(2)}, u32[]{:S(2)}) collective-permute-start(bf16[4,512,256]{2,1,0:T(8,128)(2,1)S(1)} %pad_maximum_fusion.16), channel_id=1, source_target_pairs={{0,2},{1,3},{2,0},{3,1},{4,6},{5,7},{6,4},{7,5},{8,10},{9,11},{10,... | collective-permute-start | bytes 3145736 | tf_op jit(solution)/shard_map/ppermute | solution.py:31
  126.6 59.0 %collective-permute-start.36 = (bf16[4,512,256]{2,1,0:T(8,128)(2,1)S(1)}, bf16[4,512,256]{2,1,0:T(8,128)(2,1)}, u32[]{:S(2)}, u32[]{:S(2)}) collective-permute-start(bf16[4,512,256]{2,1,0:T(8,128)(2,1)S(1)} %pad_maximum_fusion.13), channel_id=1, source_target_pairs={{0,4},{1,5},{2,6},{3,7},{4,0},{5,1},{6,2},{7,3},{8,12},{9,13},{10,... | collective-permute-start | bytes 3145736 | tf_op jit(solution)/shard_map/ppermute | solution.py:31
  133.0 70.6 %collective-permute-start.35 = (bf16[4,256,256]{2,1,0:T(8,128)(2,1)}, bf16[4,256,256]{2,1,0:T(8,128)(2,1)}, u32[]{:S(2)}, u32[]{:S(2)}) collective-permute-start(bf16[4,256,256]{2,1,0:T(8,128)(2,1)} %collective-permute-done.33), channel_id=1, source_target_pairs={{0,1},{1,0},{2,3},{3,2},{4,5},{5,4},{6,7},{7,6},{8,9},{9,8},{10,11... | collective-permute-start | bytes 1572872 | tf_op jit(solution)/shard_map/ppermute | solution.py:31
  143.6 65.7 %collective-permute-start.37 = (bf16[4,256,256]{2,1,0:T(8,128)(2,1)}, bf16[4,256,256]{2,1,0:T(8,128)(2,1)}, u32[]{:S(2)}, u32[]{:S(2)}) collective-permute-start(bf16[4,256,256]{2,1,0:T(8,128)(2,1)} %collective-permute-done.31), channel_id=1, source_target_pairs={{0,1},{1,0},{2,3},{3,2},{4,5},{5,4},{6,7},{7,6},{8,9},{9,8},{10,11... | collective-permute-start | bytes 1572872 | tf_op jit(solution)/shard_map/ppermute | solution.py:31
  185.6 100.0 %collective-permute-start.2 = (bf16[512,2048]{1,0:T(8,128)(2,1)}, bf16[512,2048]{1,0:T(8,128)(2,1)}, u32[]{:S(2)}, u32[]{:S(2)}) collective-permute-start(bf16[512,2048]{1,0:T(8,128)(2,1)} %pad_maximum_fusion.7), channel_id=1, source_target_pairs={{0,1},{1,0},{2,3},{3,2},{4,5},{5,4},{6,7},{7,6},{8,9},{9,8},{10,11... | collective-permute-start | bytes 6291464 | tf_op jit(solution)/shard_map/ppermute | solution.py:31
  201.1 150.2 %collective-permute-start.41 = (bf16[512,2048]{1,0:T(8,128)(2,1)}, bf16[512,2048]{1,0:T(8,128)(2,1)}, u32[]{:S(2)}, u32[]{:S(2)}) collective-permute-start(bf16[512,2048]{1,0:T(8,128)(2,1)} %pad_maximum_fusion.8), channel_id=1, source_target_pairs={{0,1},{1,0},{2,3},{3,2},{4,5},{5,4},{6,7},{7,6},{8,9},{9,8},{10,11... | collective-permute-start | bytes 6291464 | tf_op jit(solution)/shard_map/ppermute | solution.py:31
  819.3 26.8 %collective-permute-start.45 = (bf16[256,2048]{1,0:T(8,128)(2,1)S(1)}, bf16[256,2048]{1,0:T(8,128)(2,1)S(1)}, u32[]{:S(2)}, u32[]{:S(2)}) collective-permute-start(bf16[256,2048]{1,0:T(8,128)(2,1)S(1)} %pad_maximum_fusion.18), channel_id=1, source_target_pairs={{0,2},{1,3},{2,0},{3,1},{4,6},{5,7},{6,4},{7,5},{8,10},{9,11},{10,... | collective-permute-start | bytes 3145736 | tf_op jit(solution)/shard_map/ppermute | solution.py:31
  826.8 41.7 %collective-permute-start.52 = (bf16[256,2048]{1,0:T(8,128)(2,1)S(1)}, bf16[256,2048]{1,0:T(8,128)(2,1)S(1)}, u32[]{:S(2)}, u32[]{:S(2)}) collective-permute-start(bf16[256,2048]{1,0:T(8,128)(2,1)S(1)} %pad_maximum_fusion.20), channel_id=1, source_target_pairs={{0,2},{1,3},{2,0},{3,1},{4,6},{5,7},{6,4},{7,5},{8,10},{9,11},{10,... | collective-permute-start | bytes 3145736 | tf_op jit(solution)/shard_map/ppermute | solution.py:31
  827.4 43.3 %collective-permute-start.50 = (bf16[256,2048]{1,0:T(8,128)(2,1)S(1)}, bf16[256,2048]{1,0:T(8,128)(2,1)S(1)}, u32[]{:S(2)}, u32[]{:S(2)}) collective-permute-start(bf16[256,2048]{1,0:T(8,128)(2,1)S(1)} %pad_maximum_fusion.19), channel_id=1, source_target_pairs={{0,4},{1,5},{2,6},{3,7},{4,0},{5,1},{6,2},{7,3},{8,12},{9,13},{10,... | collective-permute-start | bytes 3145736 | tf_op jit(solution)/shard_map/ppermute | solution.py:31
  846.2 35.8 %collective-permute-start.46 = (bf16[128,2048]{1,0:T(8,128)(2,1)S(1)}, bf16[128,2048]{1,0:T(8,128)(2,1)S(1)}, u32[]{:S(2)}, u32[]{:S(2)}) collective-permute-start(bf16[128,2048]{1,0:T(8,128)(2,1)S(1)} %add_convert_fusion.20), channel_id=1, source_target_pairs={{0,4},{1,5},{2,6},{3,7},{4,0},{5,1},{6,2},{7,3},{8,12},{9,13},{10,... | collective-permute-start | bytes 1572872 | tf_op jit(solution)/shard_map/ppermute | solution.py:31
  848.4 33.6 %collective-permute-start.44 = (bf16[128,2048]{1,0:T(8,128)(2,1)S(1)}, bf16[128,2048]{1,0:T(8,128)(2,1)S(1)}, u32[]{:S(2)}, u32[]{:S(2)}) collective-permute-start(bf16[128,2048]{1,0:T(8,128)(2,1)S(1)} %add_convert_fusion.22), channel_id=1, source_target_pairs={{0,2},{1,3},{2,0},{3,1},{4,6},{5,7},{6,4},{7,5},{8,10},{9,11},{10,... | collective-permute-start | bytes 1572872 | tf_op jit(solution)/shard_map/ppermute | solution.py:31
  901.7 172.3 %collective-permute-start.75 = (bf16[256,2048]{1,0:T(8,128)(2,1)}, bf16[256,2048]{1,0:T(8,128)(2,1)}, u32[]{:S(2)}, u32[]{:S(2)}) collective-permute-start(bf16[256,2048]{1,0:T(8,128)(2,1)} %get-tuple-element.66), channel_id=1, source_target_pairs={{0,1},{1,0},{2,3},{3,2},{4,5},{5,4},{6,7},{7,6},{8,9},{9,8},{10,11... | collective-permute-start | bytes 3145736 | tf_op jit(solution)/shard_map/ppermute | solution.py:31
  907.2 128.5 %collective-permute-start.78 = (bf16[128,2048]{1,0:T(8,128)(2,1)}, bf16[128,2048]{1,0:T(8,128)(2,1)}, u32[]{:S(2)}, u32[]{:S(2)}) collective-permute-start(bf16[128,2048]{1,0:T(8,128)(2,1)} %get-tuple-element.122), channel_id=1, source_target_pairs={{0,2},{1,3},{2,0},{3,1},{4,6},{5,7},{6,4},{7,5},{8,10},{9,11},{10,... | collective-permute-start | bytes 1572872 | tf_op jit(solution)/shard_map/ppermute | solution.py:31
  909.0 134.8 %collective-permute-start.76 = (bf16[128,2048]{1,0:T(8,128)(2,1)}, bf16[128,2048]{1,0:T(8,128)(2,1)}, u32[]{:S(2)}, u32[]{:S(2)}) collective-permute-start(bf16[128,2048]{1,0:T(8,128)(2,1)} %get-tuple-element.123), channel_id=1, source_target_pairs={{0,4},{1,5},{2,6},{3,7},{4,0},{5,1},{6,2},{7,3},{8,12},{9,13},{10,... | collective-permute-start | bytes 1572872 | tf_op jit(solution)/shard_map/ppermute | solution.py:31
  1010.2 29.3 %collective-permute-start.68 = (bf16[512,768]{0,1:T(8,128)(2,1)}, bf16[512,768]{0,1:T(8,128)(2,1)}, u32[]{:S(2)}, u32[]{:S(2)}) collective-permute-start(bf16[512,768]{0,1:T(8,128)(2,1)} %bitcast.73), channel_id=1, source_target_pairs={{0,8},{1,9},{2,10},{3,11},{4,12},{5,13},{6,14},{7,15}} | collective-permute-start | bytes 2359304 | tf_op jit(solution)/shard_map/ppermute | solution.py:139
  1039.5 61.6 %collective-permute-start.61 = (bf16[1024,2048]{1,0:T(8,128)(2,1)S(1)}, bf16[1024,2048]{1,0:T(8,128)(2,1)S(1)}, u32[]{:S(2)}, u32[]{:S(2)}) collective-permute-start(bf16[1024,2048]{1,0:T(8,128)(2,1)S(1)} %pad_maximum_fusion.4), channel_id=1, source_target_pairs={{0,1},{1,0},{2,3},{3,2},{4,5},{5,4},{6,7},{7,6},{8,9},{9,8},{10,11... | collective-permute-start | bytes 12582920 | tf_op jit(solution)/shard_map/ppermute | solution.py:31
  1064.4 30.9 %collective-permute-start.81 = (bf16[256,2048]{1,0:T(8,128)(2,1)S(1)}, bf16[256,2048]{1,0:T(8,128)(2,1)S(1)}, u32[]{:S(2)}, u32[]{:S(2)}) collective-permute-start(bf16[256,2048]{1,0:T(8,128)(2,1)S(1)} %pad_maximum_fusion.24), channel_id=1, source_target_pairs={{0,4},{1,5},{2,6},{3,7},{4,0},{5,1},{6,2},{7,3},{8,12},{9,13},{10,... | collective-permute-start | bytes 3145736 | tf_op jit(solution)/shard_map/ppermute | solution.py:31
  1095.3 93.1 %collective-permute-start.48 = (bf16[512,2048]{1,0:T(8,128)(2,1)}, bf16[512,2048]{1,0:T(8,128)(2,1)}, u32[]{:S(2)}, u32[]{:S(2)}) collective-permute-start(bf16[512,2048]{1,0:T(8,128)(2,1)} %pad_maximum_fusion.9), channel_id=1, source_target_pairs={{0,1},{1,0},{2,3},{3,2},{4,5},{5,4},{6,7},{7,6},{8,9},{9,8},{10,11... | collective-permute-start | bytes 6291464 | tf_op jit(solution)/shard_map/ppermute | solution.py:31
  1096.0 72.1 %collective-permute-start.74 = (bf16[256,768]{0,1:T(8,128)(2,1)}, bf16[256,768]{0,1:T(8,128)(2,1)S(1)}, u32[]{:S(2)}, u32[]{:S(2)}) collective-permute-start(bf16[256,768]{0,1:T(8,128)(2,1)} %dynamic-slice_convert_fusion), channel_id=1, source_target_pairs={{0,4},{4,0},{1,5},{5,1},{2,6},{6,2},{3,7},{7,3},{8,12},{12,8},{9,1... | collective-permute-start | bytes 1179656 | tf_op jit(solution)/shard_map/ppermute | solution.py:1021
  1103.4 27.6 %collective-permute-start.62 = (bf16[256,2048]{1,0:T(8,128)(2,1)S(1)}, bf16[256,2048]{1,0:T(8,128)(2,1)S(1)}, u32[]{:S(2)}, u32[]{:S(2)}) collective-permute-start(bf16[256,2048]{1,0:T(8,128)(2,1)S(1)} %pad_maximum_fusion.21), channel_id=1, source_target_pairs={{0,4},{1,5},{2,6},{3,7},{4,0},{5,1},{6,2},{7,3},{8,12},{9,13},{10,... | collective-permute-start | bytes 3145736 | tf_op jit(solution)/shard_map/ppermute | solution.py:31
  1175.8 72.4 %collective-permute-start.67 = (bf16[512,2048]{1,0:T(8,128)(2,1)}, bf16[512,2048]{1,0:T(8,128)(2,1)}, u32[]{:S(2)}, u32[]{:S(2)}) collective-permute-start(bf16[512,2048]{1,0:T(8,128)(2,1)} %pad_maximum_fusion.12), channel_id=1, source_target_pairs={{0,1},{1,0},{2,3},{3,2},{4,5},{5,4},{6,7},{7,6},{8,9},{9,8},{10,11... | collective-permute-start | bytes 6291464 | tf_op jit(solution)/shard_map/ppermute | solution.py:31
  (118 other events, 1516.3 us)

commit v3 on v2

--- a/solution.py
+++ b/solution.py
@@ -143,42 +143,6 @@
     return term(here).astype(F32) + up.astype(F32) + down.astype(F32)
 
 
-def qkv_kernel(tok_ref, gain_ref, w_ref, n_ref, out_ref):
-    x = tok_ref[...].astype(F32)
-    scale = lax.rsqrt(jnp.mean(x * x, axis=-1, keepdims=True) + EPS)
-    n = (x * scale * gain_ref[...]).astype(BF)
-    n_ref[...] = n
-    out_ref[...] = mm(n, w_ref[...])
-
-
-def qkv_call(tok, gain, weights):
-    rows, width = tok.shape
-    cols = weights.shape[1]
-    tile = 256
-    return pl.pallas_call(
-        qkv_kernel,
-        grid=(rows // tile,),
-        in_specs=[
-            pl.BlockSpec((tile, width), lambda i: (i, 0)),
-            pl.BlockSpec((1, width), lambda i: (0, 0)),
-            pl.BlockSpec((width, cols), lambda i: (0, 0)),
-        ],
-        out_specs=[
-            pl.BlockSpec((tile, width), lambda i: (i, 0)),
-            pl.BlockSpec((tile, cols), lambda i: (i, 0)),
-        ],
-        out_shape=[
-            jax.ShapeDtypeStruct((rows, width), BF),
-            jax.ShapeDtypeStruct((rows, cols), F32),
-        ],
-        compiler_params=pltpu.CompilerParams(vmem_limit_bytes=48 * 1024 * 1024),
-        cost_estimate=pl.CostEstimate(
-            flops=2 * rows * width * cols, bytes_accessed=rows * width * 4 + rows * cols * 4 + width * cols * 2, transcendentals=0
-        ),
-        name="norm_qkv",
-    )(tok, gain, weights)
-
-
 def turn(u, cos, sin):
     lane = lax.broadcasted_iota(jnp.int32, u.shape, 1)
     width = u.shape[1]
@@ -193,76 +157,8 @@
     return jnp.concatenate([table] * reps, axis=1) if reps > 1 else table
 
 
-def attend_kernel(slots, lin_ref, cos_ref, sin_ref, o_slot, qs, ks, vs, os, stats):
-    rows, cols = qs.shape
-    heads = cols // HDIM
-
-    def fill(b, carry):
-        src = pl.ds(pl.multiple_of(slots[b] * BLK, BLK), BLK)
-        dst = pl.ds(pl.multiple_of(b * BLK, BLK), BLK)
-        cos = wide(cos_ref[dst, :], cols)
-        sin = wide(sin_ref[dst, :], cols)
-        qs[dst, :] = turn(lin_ref[src, 0:cols], cos, sin).astype(BF)
-        ks[dst, :] = turn(lin_ref[src, cols : 2 * cols], cos, sin).astype(BF)
-        vs[dst, :] = lin_ref[src, 2 * cols : 3 * cols].astype(BF)
-        return carry
-
-    lax.fori_loop(0, rows // BLK, fill, 0)
-    live = slots[rows // BLK]
-    tiles = rows // QT
-    for t in range(tiles):
-        ext = (t + 1) * QT
-        lane = lax.broadcasted_iota(jnp.int32, (QT, cols), 1) // HDIM
-        qpos = lax.broadcasted_iota(jnp.int32, (QT, QT), 0)
-        kpos = lax.broadcasted_iota(jnp.int32, (QT, QT), 1)
-        diag = jnp.where(kpos <= qpos, 0.0, NEG)
-        dead = jnp.where(lax.broadcasted_iota(jnp.int32, (1, ext), 1) < live, 0.0, NEG)
-
-        def head(h, acc):
-            q = jnp.where(lane == h, qs[t * QT : ext, :] * BF(0.125), BF(0))
-            s = mm(q, ks[0:ext, :], NT) + dead
-            last = s[:, t * QT :] + diag
-            s = jnp.concatenate([s[:, : t * QT], last], axis=1) if t else last
-            top = jnp.max(s, axis=1, keepdims=True)
-            p = jnp.exp(s - top)
-            total = jnp.sum(p, axis=1, keepdims=True)
-            mixed = mm(p.astype(BF), vs[0:ext, :]) / total
-            note = jnp.broadcast_to(top + jnp.log(total), (QT, 128))
-            stats[pl.ds(h, 1), t * QT : ext] = jnp.transpose(note)[0:1, :]
-            return jnp.where(lane == h, mixed, acc)
-
-        acc = lax.fori_loop(0, heads, head, jnp.zeros((QT, cols), F32))
-        out = acc.astype(BF)
-        os[t * QT : ext, :] = out
-        for i in range(QT // BLK):
-            dst = pl.ds(pl.multiple_of(slots[t * (QT // BLK) + i] * BLK, BLK), BLK)
-            o_slot[dst, :] = out[i * BLK : (i + 1) * BLK, :]
-
-
 def full_spec(shape):
     return pl.BlockSpec(shape, lambda *_: (0,) * len(shape))
-
-
-def attend_call(slots, lin, cos, sin):
-    rows = lin.shape[0]
-    cols = lin.shape[1] // 3
-    heads = cols // HDIM
-    piece = jax.ShapeDtypeStruct((rows, cols), BF)
-    return pl.pallas_call(
-        attend_kernel,
-        grid_spec=pltpu.PrefetchScalarGridSpec(
-            num_scalar_prefetch=1,
-            grid=(1,),
-            in_specs=[full_spec(lin.shape), full_spec(cos.shape), full_spec(sin.shape)],
-            out_specs=[full_spec((rows, cols))] * 5 + [full_spec((8, rows))],
-        ),
-        out_shape=[piece] * 5 + [jax.ShapeDtypeStruct((8, rows), F32)],
-        compiler_params=pltpu.CompilerParams(vmem_limit_bytes=56 * 1024 * 1024),
-        cost_estimate=pl.CostEstimate(
-            flops=heads * rows * rows * HDIM * 8, bytes_accessed=rows * cols * 22, transcendentals=heads * rows * rows // 2
-        ),
-        name="attend",
-    )(slots, lin, cos, sin)
 
 
 def attend_back_kernel(slots, qs, ks, vs, os, stats, go_ref, cos_ref, sin_ref, out_ref, go, delta, dq):
@@ -360,8 +256,500 @@
     return index + bit - 2 * bit * ((index // bit) % 2)
 
 
+class Place:
+    def __init__(self, shards, ctx, tensor):
+        self.shards, self.ctx, self.tensor = shards, ctx, tensor
+        self.group = ctx * tensor
+        self.z = lax.axis_index("shard")
+        self.x = lax.axis_index("ctx")
+        self.t = lax.axis_index("tensor")
+        self.bits_y, self.bits_x = level_bits(ctx, tensor)
+
+    def peer(self, offset):
+        t, x = self.t, self.x
+        bit = 1
+        while bit < self.group:
+            if offset & bit:
+                if bit < self.tensor:
+                    t = flip(t, bit)
+                else:
+                    x = 1 - x
+            bit *= 2
+        return x, t
+
+    def peer_id(self, offset):
+        x, t = self.peer(offset)
+        return (self.z, x, t)
+
+    def above(self):
+        return (self.z + 1, self.x, self.t)
+
+    def below(self):
+        return (self.z - 1, self.x, self.t)
+
+    def meet(self, offsets, chain=True):
+        barrier = pltpu.get_barrier_semaphore()
+        z, shards = self.z, self.shards
+        for k in offsets:
+            pl.semaphore_signal(barrier, inc=1, device_id=self.peer_id(k), device_id_type=pl.DeviceIdType.MESH)
+        peers = len(offsets)
+        if chain:
+
+            @pl.when(z < shards - 1)
+            def _():
+                pl.semaphore_signal(barrier, inc=1, device_id=self.above(), device_id_type=pl.DeviceIdType.MESH)
+
+            @pl.when(z > 0)
+            def _():
+                pl.semaphore_signal(barrier, inc=1, device_id=self.below(), device_id_type=pl.DeviceIdType.MESH)
+
+            peers = peers + (z + shards - 1) // shards + (2 * shards - 2 - z) // shards
+        pl.semaphore_wait(barrier, peers)
+
+
+class Move:
+    def __init__(self, out, due, goes, comes):
+        self.out, self.due, self.goes, self.comes = out, due, goes, comes
+
+    def _run(self, cond, fn):
+        if cond is None:
+            fn()
+        else:
+            pl.when(cond)(fn)
+
+    def start(self):
+        self._run(self.goes, self.out.start)
+
+    def come(self):
+        self._run(self.comes, self.due.wait_recv)
+
+    def sent(self):
+        self._run(self.goes, self.out.wait_send)
+
+
+class Links:
+    def __init__(self, place, send_sems, recv_sems):
+        self.place, self.send_sems, self.recv_sems = place, send_sems, recv_sems
+        self.moves = []
+
+    def send(self, src, dst, where, land=None, goes=None, comes=None, start=True):
+        i = len(self.moves)
+        land = dst if land is None else land
+        safe = self.place.peer_id(1)
+
+        def copy(a, b, w):
+            return pltpu.make_async_remote_copy(
+                src_ref=a,
+                dst_ref=b,
+                send_sem=self.send_sems.at[i],
+                recv_sem=self.recv_sems.at[i],
+                device_id=w,
+                device_id_type=pl.DeviceIdType.MESH,
+            )
+
+        move = Move(copy(src, dst, where), copy(land, land, safe), goes, comes)
+        self.moves.append(move)
+        if start:
+            move.start()
+        return move
+
+    def all_sent(self):
+        for m in self.moves:
+            m.sent()
+
+
+    def chain(self, parts):
+        p = self.place
+        z, shards = p.z, p.shards
+        due = []
+        for k in range(1, shards):
+            for m in due:
+                m.come()
+            due = []
+            up = zip(parts(z - (k - 1)), parts(z - k))
+            for src, land in up:
+                due.append(self.send(src, src, p.above(), land, (z >= k - 1) & (z < shards - 1), z >= k))
+            down = zip(parts(z + (k - 1)), parts(z + k))
+            for src, land in down:
+                due.append(
+                    self.send(src, src, p.below(), land, (z + k - 1 <= shards - 1) & (z > 0), z + k <= shards - 1)
+                )
+            yield
+        for m in due:
+            m.come()
+
+    def spread(self, part, absolute=False):
+        p = self.place
+
+        def put(k, bit, h):
+            return self.send(part(k, h), part(k if absolute else k | bit, h), p.peer_id(bit), part(k | bit, h))
+
+        cores = [put(0, 1, None)]
+        have = [[0], [0]]
+        found = {}
+        orders = [p.bits_x + p.bits_y, p.bits_y + p.bits_x]
+        for stage in range(len(orders[0])):
+            step = []
+            for h in (0, 1):
+                bit = orders[h][stage]
+                step += [(k | bit, put(k, bit, h)) for k in have[h]]
+                have[h] = have[h] + [k | bit for k in have[h]]
+            yield
+            for k, m in step:
+                m.come()
+                found[k] = found.get(k, 0) + 1
+                if found[k] == 2:
+                    cores.append(put(k, 1, None))
+        yield
+        for m in cores:
+            m.come()
+
+    def rows(self, source, keep, own_rows, log):
+        p = self.place
+
+        def slot(k):
+            return keep.at[pl.ds(k * own_rows, own_rows), :]
+
+        mine = source.at[pl.ds(pl.multiple_of(p.t * own_rows, own_rows), own_rows), :]
+        first = self.send(mine, slot(p.tensor), p.peer_id(p.tensor))
+        log.append(first)
+        yield
+        first.come()
+        far = [p.tensor]
+        for bit in p.bits_y:
+            step = [self.send(slot(k), slot(k | bit), p.peer_id(bit)) for k in far]
+            log += step
+            yield
+            for m in step:
+                m.come()
+            far = far + [k | bit for k in far]
+        last = [self.send(slot(k), slot(k | 1), p.peer_id(1)) for k in far]
+        log += last
+        yield
+        for m in last:
+            m.come()
+
+
+def drain(*gens):
+    for g in gens:
+        for _ in g:
+            pass
+
+
+def first_kernel(
+    dims, place_s, at_s, live_s, tokens, cotangent, gains_in, wq, wk, wv, w_out, wg, wu, wd, cos_ref, sin_ref,
+    n_one_out, w_qkv_out, w_o_out, cot_out, gu_out, d_out, n_own_out, h_out, gains, qs, ks, vs, os, stats, o_rel,
+    n_one, w_qkv, w_o, qkv_rel, attn_rows, h_own, n_own, x_keep,
+    send_sems, recv_sems, own_sems,
+):
+    shards, ctx, tensor, fc, own_rows, d_own = dims
+    p = Place(shards, ctx, tensor)
+    z, x, t = p.z, p.x, p.t
+    group = p.group
+    rows, width = n_one.shape
+    cols = qs.shape[1]
+    heads = cols // HDIM
+    ff = wg.shape[1] // ctx
+    dz = ctx * d_own
+    links = Links(p, send_sems, recv_sems)
+    own_count = [0]
+
+    def own(src, dst):
+        i = own_count[0]
+        own_count[0] += 1
+        c = pltpu.make_async_copy(src, dst, own_sems.at[i])
+        c.start()
+        return c
+
+    p.meet(list(range(1, group)))
+
+    def d_at(xx):
+        return pl.ds(pl.multiple_of((z * ctx + xx) * d_own, d_own), d_own)
+
+    def z_at(b):
+        return pl.ds(pl.multiple_of(b * dz, dz), dz)
+
+    def part_cols(xx, size):
+        return pl.ds(pl.multiple_of(xx * size, size), size)
+
+    across = p.peer_id(tensor)
+
+    wo_rows = w_out.shape[0]
+
+    def o_at(tt, xx, zz):
+        return w_o.at[xx, pl.ds(pl.multiple_of(tt * wo_rows, wo_rows), wo_rows), pl.ds(pl.multiple_of(zz * d_own, d_own), d_own)]
+
+    own_o = own(w_out, o_at(t, x, z))
+    own_gain = own(gains_in, gains.at[:, d_at(x)])
+    own_w = [own(w.at[:, part_cols(x, cols)], w_qkv.at[d_at(x), i * cols : (i + 1) * cols]) for i, w in enumerate((wq, wk, wv))]
+    own_gain.wait()
+    gain_x = links.send(gains.at[:, d_at(x)], gains.at[:, d_at(x)], across, gains.at[:, d_at(1 - x)])
+    qkv_x = [
+        links.send(
+            w.at[:, part_cols(1 - x, cols)],
+            w_qkv.at[d_at(x), i * cols : (i + 1) * cols],
+            across,
+            w_qkv.at[d_at(1 - x), i * cols : (i + 1) * cols],
+        )
+        for i, w in enumerate((wq, wk, wv))
+    ]
+    tok_log = []
+    tok_rows = links.rows(tokens, n_one, own_rows, tok_log)
+    next(tok_rows)
+    own_tok = []
+    for k in range(tensor):
+        _, tt = p.peer(k)
+        src = tokens.at[pl.ds(pl.multiple_of(tt * own_rows, own_rows), own_rows), :]
+        own_tok.append(own(src, n_one.at[pl.ds(k * own_rows, own_rows), :]))
+    own_o.wait()
+    o_chain = links.chain(lambda b: [o_at(t, x, b)])
+    next(o_chain)
+    gain_x.come()
+    gain_chain = links.chain(lambda b: [gains.at[:, z_at(b)]])
+    next(gain_chain)
+    next(o_chain, None)
+    for c in own_w:
+        c.wait()
+    for m in qkv_x:
+        m.come()
+    next(gain_chain, None)
+    qkv_chain = links.chain(lambda b: [w_qkv.at[z_at(b), :]])
+    next(qkv_chain)
+
+    gu_pairs = [(wg, 0), (wu, 1)]
+
+    def gu_place(xx, i):
+        return gu_out.at[d_at(xx), i * fc : (i + 1) * fc]
+
+    ff_own = [own(w.at[:, pl.ds(pl.multiple_of(x * ff, fc), fc)], gu_place(x, i)) for w, i in gu_pairs]
+    ff_own.append(own(wd.at[pl.ds(pl.multiple_of(x * ff, fc), fc), :], d_out.at[:, d_at(x)]))
+    ff_x = [
+        links.send(w.at[:, pl.ds(pl.multiple_of((1 - x) * ff, fc), fc)], gu_place(x, i), across, gu_place(1 - x, i))
+        for w, i in gu_pairs
+    ]
+    ff_x.append(
+        links.send(wd.at[pl.ds(pl.multiple_of((1 - x) * ff, fc), fc), :], d_out.at[:, d_at(x)], across, d_out.at[:, d_at(1 - x)])
+    )
+    drain(gain_chain)
+    drain(o_chain)
+    for c in own_tok:
+        c.wait()
+    x_keep[...] = n_one[0:own_rows, :]
+    next(tok_rows, None)
+
+    def o_part(k, h):
+        xx, tt = p.peer(k)
+        size = wo_rows if h is None else wo_rows // 2
+        start = tt * wo_rows + (0 if h is None else h * size)
+        return w_o.at[xx, pl.ds(pl.multiple_of(start, size), size), :]
+
+    o_spread = links.spread(o_part, absolute=True)
+    next(o_spread)
+
+    def norm(r, carry):
+        at = pl.ds(pl.multiple_of(r * own_rows, own_rows), own_rows)
+        v = n_one[at, :].astype(F32)
+        scale = lax.rsqrt(jnp.mean(v * v, axis=-1, keepdims=True) + EPS)
+        n_one[at, :] = (v * scale * gains[0:1, :]).astype(BF)
+        return carry
+
+    next(qkv_chain, None)
+    lax.fori_loop(0, tensor, norm, 0)
+    for c in ff_own:
+        c.wait()
+    for m in ff_x:
+        m.come()
+    next(tok_rows, None)
+    next(qkv_chain, None)
+    ff_chain = links.chain(lambda b: [gu_out.at[z_at(b), :], d_out.at[:, z_at(b)]])
+    next(ff_chain)
+    drain(tok_rows)
+    for m in tok_log:
+        m.sent()
+    lax.fori_loop(tensor, group, norm, 0)
+    out_n = own(n_one, n_one_out)
+    next(o_spread, None)
+    drain(qkv_chain)
+    next(ff_chain, None)
+    out_w = own(w_qkv, w_qkv_out)
+
+    def project(r, carry):
+        at = pl.ds(pl.multiple_of(r * own_rows, own_rows), own_rows)
+        lin = mm(n_one[at, :], w_qkv[...])
+        per = own_rows // BLK
+        for i in range(per):
+            where = pl.ds(pl.multiple_of(r * own_rows + i * BLK, BLK), BLK)
+            cos, sin = wide(cos_ref[where, :], cols), wide(sin_ref[where, :], cols)
+            part = lin[i * BLK : (i + 1) * BLK, :]
+            dst = pl.ds(pl.multiple_of(r * own_rows + i * BLK, BLK), BLK)
+            qkv_rel[dst, 0:cols] = turn(part[:, 0:cols], cos, sin).astype(BF)
+            qkv_rel[dst, cols : 2 * cols] = turn(part[:, cols : 2 * cols], cos, sin).astype(BF)
+            qkv_rel[dst, 2 * cols : 3 * cols] = part[:, 2 * cols : 3 * cols].astype(BF)
+        return carry
+
+    lax.fori_loop(0, group, project, 0)
+    next(o_spread, None)
+
+    def fill(b, carry):
+        dst = pl.ds(pl.multiple_of(b * BLK, BLK), BLK)
+        found = picked(qkv_rel, place_s[b])
+        qs[dst, :] = found[:, 0:cols]
+        ks[dst, :] = found[:, cols : 2 * cols]
+        vs[dst, :] = found[:, 2 * cols : 3 * cols]
+        return carry
+
+    lax.fori_loop(0, rows // BLK, fill, 0)
+    cot_rows = links.rows(cotangent, cot_out, own_rows, [])
+    next(cot_rows)
+    own_cot = []
+    for k in range(tensor):
+        _, tt = p.peer(k)
+        src = cotangent.at[pl.ds(pl.multiple_of(tt * own_rows, own_rows), own_rows), :]
+        own_cot.append(own(src, cot_out.at[pl.ds(k * own_rows, own_rows), :]))
+    live = live_s[0]
+    for tile in range(rows // QT):
+        attend_tile(tile, live, qs, ks, vs, os, stats)
+        next(ff_chain, None)
+        next(o_spread, None)
+        next(cot_rows, None)
+
+    def back_to_rows(j, carry):
+        dst = pl.ds(pl.multiple_of(j * BLK, BLK), BLK)
+        o_rel[dst, :] = picked(os, at_s[j])
+        return carry
+
+    lax.fori_loop(0, rows // BLK, back_to_rows, 0)
+
+    def head_at(k):
+        xx, tt = p.peer(k)
+        return attn_rows.at[:, pl.ds(pl.multiple_of((tt * ctx + xx) * cols, cols), cols)]
+
+    swaps = [
+        links.send(o_rel.at[pl.ds(k * own_rows, own_rows), :], head_at(0), p.peer_id(k), head_at(k)) for k in range(1, group)
+    ]
+    own_heads = own(o_rel.at[pl.ds(0, own_rows), :], head_at(0))
+    drain(o_spread)
+    out_o = own(w_o, w_o_out)
+    own_heads.wait()
+    for m in swaps:
+        m.come()
+    for xx in range(ctx):
+        span = shards * d_own
+        mixed = mm(attn_rows[...], w_o[xx])
+        for zz in range(shards):
+            at = slice((zz * ctx + xx) * d_own, (zz * ctx + xx + 1) * d_own)
+            h_own[:, at] = x_keep[:, at].astype(F32) + mixed[:, zz * d_own : (zz + 1) * d_own]
+    h = h_own[...]
+    scale = lax.rsqrt(jnp.mean(h * h, axis=-1, keepdims=True) + EPS)
+    n_own[...] = (h * scale * gains[1:2, :]).astype(BF)
+    out_h = own(h_own, h_out)
+    out_own = own(n_own, n_own_out)
+    drain(ff_chain)
+    drain(cot_rows)
+    for c in own_cot:
+        c.wait()
+    for m in links.moves:
+        if m not in tok_log:
+            m.sent()
+    for c in (out_n, out_w, out_o, out_h, out_own):
+        c.wait()
+
+
+def picked(ref, block):
+    found = ref[0:BLK, :]
+    for j in range(1, ref.shape[0] // BLK):
+        found = jnp.where(block == j, ref[j * BLK : (j + 1) * BLK, :], found)
+    return found
+
+
+def attend_tile(t, live, qs, ks, vs, os, stats):
+    rows, cols = qs.shape
+    heads = cols // HDIM
+    ext = (t + 1) * QT
+    lane = lax.broadcasted_iota(jnp.int32, (QT, cols), 1) // HDIM
+    qpos = lax.broadcasted_iota(jnp.int32, (QT, QT), 0)
+    kpos = lax.broadcasted_iota(jnp.int32, (QT, QT), 1)
+    diag = jnp.where(kpos <= qpos, 0.0, NEG)
+    dead = jnp.where(lax.broadcasted_iota(jnp.int32, (1, ext), 1) < live, 0.0, NEG)
+
+    def head(h, acc):
+        q = jnp.where(lane == h, qs[t * QT : ext, :] * BF(0.125), BF(0))
+        s = mm(q, ks[0:ext, :], NT) + dead
+        last = s[:, t * QT :] + diag
+        s = jnp.concatenate([s[:, : t * QT], last], axis=1) if t else last
+        top = jnp.max(s, axis=1, keepdims=True)
+        e = jnp.exp(s - top)
+        total = jnp.sum(e, axis=1, keepdims=True)
+        mixed = mm(e.astype(BF), vs[0:ext, :]) / total
+        note = jnp.broadcast_to(top + jnp.log(total), (QT, 128))
+        stats[pl.ds(h, 1), t * QT : ext] = jnp.transpose(note)[0:1, :]
+        return jnp.where(lane == h, mixed, acc)
+
+    acc = lax.fori_loop(0, heads, head, jnp.zeros((QT, cols), F32))
+    os[t * QT : ext, :] = acc.astype(BF)
+
+
+def first_call(shards, ctx, tensor, place, at, live, tokens, cotangent, gains, wq, wk, wv, w_out, wg, wu, wd, cos, sin):
+    width = tokens.shape[1]
+    own_rows = tokens.shape[0] // tensor
+    group = ctx * tensor
+    rows = own_rows * group
+    d_own = wq.shape[0]
+    cols = wq.shape[1] // ctx
+    fc = 256
+    dims = (shards, ctx, tensor, fc, own_rows, d_own)
+    any_spec = pl.BlockSpec(memory_space=pl.ANY)
+    smem = pl.BlockSpec(memory_space=pltpu.SMEM)
+    vmem = pl.BlockSpec(memory_space=pltpu.VMEM)
+    piece = jax.ShapeDtypeStruct((rows, cols), BF)
+    moves = 400
+    dma = pltpu.SemaphoreType.DMA
+    return pl.pallas_call(
+        functools.partial(first_kernel, dims),
+        in_specs=[smem] * 3 + [any_spec] * 10 + [vmem] * 2,
+        out_specs=[any_spec] * 8 + [vmem] * 7,
+        out_shape=[
+            jax.ShapeDtypeStruct((rows, width), BF),
+            jax.ShapeDtypeStruct((width, 3 * cols), BF),
+            jax.ShapeDtypeStruct((ctx, width, shards * d_own), BF),
+            jax.ShapeDtypeStruct((rows, width), BF),
+            jax.ShapeDtypeStruct((width, 2 * fc), BF),
+            jax.ShapeDtypeStruct((fc, width), BF),
+            jax.ShapeDtypeStruct((own_rows, width), BF),
+            jax.ShapeDtypeStruct((own_rows, width), F32),
+            jax.ShapeDtypeStruct((8, width), F32),
+            piece,
+            piece,
+            piece,
+            piece,
+            jax.ShapeDtypeStruct((8, rows), F32),
+            piece,
+        ],
+        scratch_shapes=[
+            pltpu.VMEM((rows, width), BF),
+            pltpu.VMEM((width, 3 * cols), BF),
+            pltpu.VMEM((ctx, width, shards * d_own), BF),
+            pltpu.VMEM((rows, 3 * cols), BF),
+            pltpu.VMEM((own_rows, width), BF),
+            pltpu.VMEM((own_rows, width), F32),
+            pltpu.VMEM((own_rows, width), BF),
+            pltpu.VMEM((own_rows, width), BF),
+            dma((moves,)),
+            dma((moves,)),
+            dma((40,)),
+        ],
+        compiler_params=pltpu.CompilerParams(
+            collective_id=0, has_side_effects=True, vmem_limit_bytes=62 * 1024 * 1024
+        ),
+        cost_estimate=pl.CostEstimate(
+            flops=2 * rows * width * cols * 4, bytes_accessed=64 * 1024 * 1024, transcendentals=rows * rows * cols // HDIM
+        ),
+        name="first",
+    )(place, at, live, tokens, cotangent, gains, wq, wk, wv, w_out, wg, wu, wd, cos, sin)
+
+
 def mlp_kernel(
-    dims, n_own, cot_in, wg, wu, wd,
+    dims, n_own, cot_in, wg, wu, wd, gu_pre, d_pre,
     dn_out, out_out, mine_out, got_out, g_hbm, r_hbm,
     n2, cot, wgu_v, wd_v, hid, dgu, left_t, gt, st, ost, fin, away,
     lev_send, lev_recv, x_own, x_send, x_recv, a_send, a_recv, g_sem, s_sem, rs_send, rs_recv, fx_send, fx_recv, o_sem, c_sem,
@@ -376,30 +764,9 @@
     t = lax.axis_index("tensor")
     bits_y, bits_x = level_bits(ctx, tensor)
 
-    def mesh_id(bit):
-        return (z, x, flip(t, bit)) if bit < tensor else (z, 1 - x, t)
-
-    def above():
-        return (z + 1, x, t)
-
-    def below():
-        return (z - 1, x, t)
-
-    barrier = pltpu.get_barrier_semaphore()
-    partners = [1] + bits_y + bits_x
-    for bit in partners:
-        pl.semaphore_signal(barrier, inc=1, device_id=mesh_id(bit), device_id_type=pl.DeviceIdType.MESH)
-
-    @pl.when(z < shards - 1)
-    def _():
-        pl.semaphore_signal(barrier, inc=1, device_id=above(), device_id_type=pl.DeviceIdType.MESH)
-
-    @pl.when(z > 0)
-    def _():
-        pl.semaphore_signal(barrier, inc=1, device_id=below(), device_id_type=pl.DeviceIdType.MESH)
-
-    peers = len(partners) + (z + shards - 1) // shards + (2 * shards - 2 - z) // shards
-    pl.semaphore_wait(barrier, peers)
+    p = Place(shards, ctx, tensor)
+    above, below = p.above, p.below
+    p.meet([1] + bits_y + bits_x)
 
     here_too = (z, x, flip(t, 1))
 
@@ -475,65 +842,37 @@
         for d in x_copies(c, True):
             d.start()
 
-    x_start(0)
+    x_start(1)
+    pre_copies = [
+        pltpu.make_async_copy(gu_pre, wgu_v.at[0], x_own.at[0, 0]),
+        pltpu.make_async_copy(d_pre, wd_v.at[pl.ds(0, fc), :], x_own.at[0, 1]),
+    ]
+    for d in pre_copies:
+        d.start()
 
     half = rows_own // 2
-
-    def lev(src_k, dst_k, part, sem, bit):
-        if part is None:
-            s = pl.ds(src_k * rows_own, rows_own)
-            e = pl.ds(dst_k * rows_own, rows_own)
-        else:
-            s = pl.ds(src_k * rows_own + part * half, half)
-            e = pl.ds(dst_k * rows_own + part * half, half)
-        return remote(n2.at[s, :], n2.at[e, :], lev_send.at[sem], lev_recv.at[sem], mesh_id(bit))
-
+    links = Links(p, lev_send, lev_recv)
     cot_copy = pltpu.make_async_copy(cot_in, cot, c_sem.at[0])
     own_copy = pltpu.make_async_copy(n_own, n2.at[pl.ds(0, rows_own), :], c_sem.at[1])
     own_copy.start()
+    own_copy.wait()
+
+    def n_part(k, h):
+        if h is None:
+            return n2.at[pl.ds(k * rows_own, rows_own), :]
+        return n2.at[pl.ds(k * rows_own + h * half, half), :]
+
+    n_rows = links.spread(n_part)
+    next(n_rows)
     cot_copy.start()
-    own_copy.wait()
-    sem = 0
-    started = []
-
-    def go(src_k, dst_k, part, bit):
-        nonlocal sem
-        d = lev(src_k, dst_k, part, sem, bit)
-        d.start()
-        sem += 1
-        started.append(d)
-        return d
-
-    first = go(0, 1, None, 1)
-    have = [[0], [0]]
-    orders = [bits_x + bits_y, bits_y + bits_x]
-    core_moves = [first]
-    arrived = {}
-    stages = len(orders[0])
-    pending = []
-    for stage in range(stages):
-        now = []
-        for part in (0, 1):
-            bit = orders[part][stage]
-            for k in have[part]:
-                now.append((part, k | bit, go(k, k | bit, part, bit)))
-        for part in (0, 1):
-            bit = orders[part][stage]
-            have[part] = have[part] + [k | bit for k in have[part]]
-        pending.append(now)
-        if stage == 0:
-            for c in range(1, chunks):
-                x_start(c)
-            for d in x_copies(0, True):
-                d.wait()
-            for d in x_landed(0):
-                d.wait_recv()
-            hop_start(0, 1)
-        for part, k, d in now:
-            d.wait_recv()
-            arrived[k] = arrived.get(k, 0) + 1
-            if arrived[k] == 2:
-                core_moves.append(go(k, k | 1, None, 1))
+    for c in range(2, chunks):
+        x_start(c)
+    for d in x_copies(1, True):
+        d.wait()
+    for d in x_landed(1):
+        d.wait_recv()
+    hop_start(1, 1)
+    next(n_rows)
 
     def ag_round(r, top):
         for k in range(shards - 1, 0, -1):
@@ -541,7 +880,7 @@
                 continue
             c = r - k + 1
 
-            @pl.when((c >= 0) & (c < chunks))
+            @pl.when((c >= 1) & (c < chunks))
             def _(c=c, k=k):
                 if k == 1:
                     for d in x_copies(c, True):
@@ -552,11 +891,12 @@
                     hop_wait(c, k - 1)
                 hop_start(c, k)
 
-    for r in range(1, shards - 1):
+    for r in range(2, shards - 1):
         ag_round(jnp.int32(r), shards - 1)
-    for d in core_moves:
-        d.wait_recv()
+    drain(n_rows)
     cot_copy.wait()
+    for d in pre_copies:
+        d.wait()
 
     def block_of(i):
         down = shards - 1 - i
@@ -745,7 +1085,10 @@
     def slot_body(s, carry):
         @pl.when(s < chunks)
         def _():
-            hop_wait(s, shards - 1)
+            @pl.when(s >= 1)
+            def _():
+                hop_wait(s, shards - 1)
+
             phase_one(s)
             ag_round(s + shards - 1, shards - 1)
             phase_two(s)
@@ -769,9 +1112,8 @@
     for u in (2 * units - 2, 2 * units - 1):
         at = pl.ds((u % units) * ot, ot)
         pltpu.make_async_copy(ost.at[u % 2], out_out.at[at, :], o_sem.at[u % 2]).wait()
-    for d in started:
-        d.wait_send()
-    for c in range(chunks):
+    links.all_sent()
+    for c in range(1, chunks):
         for d in x_copies(c, False):
             d.wait_send()
         for k in range(1, shards):
@@ -797,7 +1139,7 @@
         fin_copy(c).wait_recv()
 
 
-def mlp_call(shards, ctx, tensor, n_own, cot, wg, wu, wd):
+def mlp_call(shards, ctx, tensor, n_own, cot, wg, wu, wd, gu_pre, d_pre):
     rows_own, width = n_own.shape
     group = ctx * tensor
     rows = rows_own * group
@@ -815,7 +1157,7 @@
     dma = pltpu.SemaphoreType.DMA
     return pl.pallas_call(
         functools.partial(mlp_kernel, dims),
-        in_specs=[any_spec] * 5,
+        in_specs=[any_spec] * 7,
         out_specs=[any_spec] * 6,
         out_shape=[
             jax.ShapeDtypeStruct((rows, width), BF),
@@ -861,7 +1203,7 @@
             flops=18 * rows * width * ff, bytes_accessed=100 * 1024 * 1024, transcendentals=rows * ff
         ),
         name="feed_forward",
-    )(n_own, cot, wg, wu, wd)
+    )(n_own, cot, wg, wu, wd, gu_pre, d_pre)
 
 
 def per_device(
@@ -884,24 +1226,9 @@
 
     slot = block_slot[0]
     place = ((slot // slots_each) ^ me) * slots_each + slot % slots_each
+    order = jnp.arange(slot.shape[0], dtype=jnp.int32)
+    at = jnp.sum(jnp.where(place[:, None] == order[None, :], order[:, None], 0), axis=0).astype(jnp.int32)
     slots = jnp.concatenate([place, seq_len]).astype(jnp.int32)
-
-    def level_rows_of(array):
-        local = jnp.take(array.reshape(tensor, own_rows, width), my_t ^ jnp.arange(tensor), axis=0)
-        blocks = [local[k] for k in range(tensor)]
-        half = own_rows // 2
-        have = [(0, blocks[0])]
-        got = swap(blocks[0], group, tensor)
-        far = {tensor: got}
-        bit = tensor // 2
-        while bit >= 1:
-            keys = sorted(far)
-            sent = jnp.concatenate([far[k] for k in keys], axis=0) if len(keys) > 1 else far[keys[0]]
-            got = swap(sent, group, bit)
-            for i, k in enumerate(keys):
-                far[k | bit] = got[i * own_rows : (i + 1) * own_rows]
-            bit //= 2
-        return jnp.concatenate([local.reshape(tensor * own_rows, width)] + [far[tensor + k] for k in range(tensor)], axis=0), blocks[0]
 
     def x_halves(array, axis):
         size = array.shape[axis] // ctx
@@ -913,19 +1240,6 @@
         return jnp.where(
             my_x == 0, jnp.concatenate([mine, got], axis=axis), jnp.concatenate([got, mine], axis=axis)
         )
-
-    gains = jnp.stack([attn_gain, mlp_gain], axis=0)
-    gains = x_join(gains, lax.ppermute(gains, "ctx", swap_x), 1)
-    gains = in_order(chain_gather(gains, shards), shards)
-    gains = jnp.transpose(gains, (1, 0, 2)).reshape(2, width).astype(F32)
-    gain_one, gain_two = gains[0:1], gains[1:2]
-
-    halves = [x_halves(w, 1) for w in (w_query, w_key, w_value)]
-    mine = jnp.concatenate([a for a, _ in halves], axis=1)
-    got = lax.ppermute(jnp.concatenate([b for _, b in halves], axis=1), "ctx", swap_x)
-    w_qkv = in_order(chain_gather(x_join(mine, got, 0), shards), shards).reshape(width, 3 * cols)
-
-    tok, tok_own = level_rows_of(tokens)
 
     angle_at = jnp.arange(level_rows, dtype=F32)
     lane = jnp.arange(128)
@@ -933,29 +1247,27 @@
     angles = angle_at[:, None] * freqs[None, :]
     cos = jnp.cos(angles)
     sin = jnp.sin(angles) * jnp.where(lane % HDIM < HDIM // 2, -1.0, 1.0)
-    n_one, lin = qkv_call(tok, gain_one, w_qkv)
-    o_slot, qs, ks, vs, os, stats = attend_call(slots, lin, cos, sin)
-
-    head_order = jnp.arange(group)
-    head_owner = (head_order % ctx) * tensor + head_order // ctx
-    got = level_exchange([o_slot[k * own_rows : (k + 1) * own_rows] for k in range(group)], group)
-    attn_rows = jnp.take(jnp.stack(got, axis=0), head_owner ^ me, axis=0)
-    attn_rows = jnp.transpose(attn_rows, (1, 0, 2)).reshape(own_rows, width)
-
-    pieces = jnp.stack(chain_gather(w_out, shards), axis=0)
-    every = jnp.stack(level_gather(pieces, ctx, tensor, axis=1), axis=0)
-    every = jnp.take(every, rel ^ me, axis=0)
-    every = jnp.take(every, (my_z - jnp.arange(shards)) % shards, axis=1)
-    every = every.reshape(ctx, tensor, shards, w_out.shape[0], d_own)
-    w_out_all = jnp.transpose(every, (1, 3, 2, 0, 4)).reshape(width, width)
-
-    x_own = tok_own.astype(F32)
-    hidden_res = x_own + mm(attn_rows, w_out_all)
+    at_pos = (at[:, None] * BLK + jnp.arange(BLK)[None, :]).reshape(-1).astype(F32)
+    angles = at_pos[:, None] * freqs[None, :]
+    cos_rel = jnp.cos(angles)
+    sin_rel = jnp.sin(angles) * jnp.where(lane % HDIM < HDIM // 2, -1.0, 1.0)
+    gains = jnp.concatenate([jnp.stack([attn_gain, mlp_gain], axis=0).astype(F32), jnp.zeros((6, d_own), F32)], axis=0)
+    n_one, w_qkv, w_o, cot, gu_pre, d_pre, n_two_own, hidden_res, gains, qs, ks, vs, os, stats, o_slot = first_call(
+        shards, ctx, tensor, place.astype(jnp.int32), at, seq_len, tokens, cotangent, gains,
+        w_query, w_key, w_value, w_out, w_gate, w_up, w_down, cos_rel, sin_rel,
+    )
+    gain_one, gain_two = gains[0:1], gains[1:2]
+
+    def own_block(array):
+        return lax.dynamic_slice_in_dim(array, my_t * own_rows, own_rows)
+
+    x_own = own_block(tokens).astype(F32)
+    cot_own = own_block(cotangent)
     scale_two = lax.rsqrt(jnp.mean(hidden_res * hidden_res, axis=-1, keepdims=True) + EPS)
     normed_two = hidden_res * scale_two
-    n_two_own = (normed_two * gain_two).astype(BF)
-    cot, cot_own = level_rows_of(cotangent)
-    dn_part, out_part, ff_mine, ff_got, _, _ = mlp_call(shards, ctx, tensor, n_two_own, cot, w_gate, w_up, w_down)
+    dn_part, out_part, ff_mine, ff_got, _, _ = mlp_call(
+        shards, ctx, tensor, n_two_own, cot, w_gate, w_up, w_down, gu_pre, d_pre
+    )
 
     def row_blocks(array):
         return [array[k * own_rows : (k + 1) * own_rows] for k in range(group)]
@@ -983,7 +1295,8 @@
     d_h = cot_f + scale_two * (scaled - normed_two * inner)
     gain_two_part = jnp.sum(d_n_two * normed_two, axis=0)
     d_h_low = d_h.astype(BF)
-    d_attn = mm(d_h_low, w_out_all, NT).astype(BF)
+    d_h_parts = jnp.transpose(d_h_low.reshape(own_rows, shards, ctx, d_own), (2, 0, 1, 3)).reshape(ctx, own_rows, shards * d_own)
+    d_attn = sum(mm(d_h_parts[i], w_o[i], NT) for i in range(ctx)).astype(BF)
     blocks = jnp.transpose(d_attn.reshape(own_rows, group, cols), (1, 0, 2))
     owner_rel = rel ^ me
     col_of = (owner_rel % tensor) * ctx + owner_rel // tensor

time: 1280 us -> 1110 us (0.87)
  Pallas kernels: 513 us -> 628 us
  local copies, waits for them, and re-layouts: 171 us -> 86.4 us
  waiting for transfers between devices: 246 us -> 174 us
  other arithmetic: 143 us -> 76.9 us
  starting transfers between devices: 118 us -> 60.4 us
    pallas_call x2 -> x1, Pallas kernels: 53.7 us -> 252 us  [first_call(): pl.pallas_call(functools.partial(first_kernel, dims), in_specs=[smem] * 3...]
    pallas_call x1, Pallas kernels: 411 us -> 328 us  [mlp_call(): pl.pallas_call(functools.partial(mlp_kernel, dims), in_specs=[any_spec] *...]
    ppermute x57 -> x35, waiting for transfers between devices: 202 us -> 134 us  [swap(): return lax.ppermute(value, LEVEL, [(i, i ^ bit) for i in range(group)])]
    gather x9 -> x0, local copies, waits for them, and re-layouts: 38.7 us -> none  [the longest x3 16.2 us: per_device(): every = jnp.take(every, (my_z - jnp.arange(shards)) % shards, axis=1)]
    ppermute x20 -> x0, starting transfers between devices: 36.2 us -> none  [the longest x9 22.5 us: chain_gather(): lax.ppermute(up, 'shard', [(i, i + 1) for i in range(k - 1, shards - 1)])]
    ppermute x20 -> x0, waiting for transfers between devices: 30.1 us -> none  [the longest x9 30.1 us: chain_gather(): lax.ppermute(down, 'shard', [(i, i - 1) for i in range(1, shards - k + 1)])]
    ppermute x6, waiting for transfers between devices: 4 us -> 27.5 us  [chain_sum(): up = lax.ppermute(send, 'shard', [(i, i + 1) for i in range(0, k)])]
    ppermute x57 -> x35, starting transfers between devices: 47.5 us -> 27.7 us  [swap(): return lax.ppermute(value, LEVEL, [(i, i ^ bit) for i in range(group)])]
  transfers between devices with their start and end apart: 91 -> 49, of which waited for: 36 -> 20; matrix products, arithmetic and copies ran while one was open for 24% -> 13% of each run, Pallas kernels for 8% -> 4%
where the time goes in v3:
time: 1110 us; the launch traced here: 1100 us
  Pallas kernels  628 us (57%)
  waiting for transfers between devices  174 us (16%)
  local copies, waits for them, and re-layouts  86.4 us (8%)
  other arithmetic  76.9 us (7%)
  starting transfers between devices  60.4 us (5%)
  blocking collectives  41.3 us (4%)
  matrix products  29.5 us (3%)
    pallas_call x1, Pallas kernels, mlp_call(): pl.pallas_call(functools.partial(mlp_kernel, dims), in_specs=[any_spec] *...  328 us
    pallas_call x1, Pallas kernels, first_call(): pl.pallas_call(functools.partial(first_kernel, dims), in_specs=[smem] * 3...  252 us
    ppermute x35, waiting for transfers between devices, swap(): return lax.ppermute(value, LEVEL, [(i, i ^ bit) for i in range(group)])  134 us
    pallas_call x1, Pallas kernels, attend_back_call(): pl.pallas_call(attend_back_kernel, grid_spec=pltpu.PrefetchScalarGridSpec...  48.3 us
    psum x1, blocking collectives, gain_sum(): total = lax.psum(part, ('shard', 'ctx', 'tensor'))  41.3 us
    unnamed x120, local copies, waits for them, and re-layouts  40.6 us
    dot_general x5, matrix products, mm(): return lax.dot_general(left, right, dims, preferred_element_type=F32)  29.5 us
    ppermute x35, starting transfers between devices, swap(): return lax.ppermute(value, LEVEL, [(i, i ^ bit) for i in range(group)])  27.7 us
  transfers between devices with their start and end apart: 49, of which 20 were waited for; matrix products, arithmetic and copies ran while one was open for 13% of the time, Pallas kernels for 4%

profile of v3, /device:TPU:0, one launch (start us, length us, event | category | flops | bytes accessed | tf_op | source)
XLA Modules:
  0.0 1099.8 jit_solution(15654398326130642096)
XLA Ops:
  4.1 9.2 fusion.30
  13.3 251.7 %first.1 = (bf16[2048,2048]{1,0:T(8,128)(2,1)}, bf16[2048,768]{1,0:T(8,128)(2,1)}, bf16[2,2048,1024]{2,1,0:T(8,128)(2,1)}, bf16[2048,2048]{1,0:T(8,128)(2,1)}, b...) custom-call(s32[16]{0:T(128)} %copy-done.29, ...), custom_call_target="tpu_custom_call" | custom-call | flops 8589934592 | bytes 67108864 | tf_op jit(solution)/shard_map/first/pallas_call | solution.py:707
  265.0 328.3 %feed_forward.1 = (bf16[2048,2048]{1,0:T(8,128)(2,1)}, bf16[2048,2048]{1,0:T(8,128)(2,1)}, f32[4,768,256]{2,1,0:T(8,128)}, bf16[4,768,256]{2,1,0:T(8,128)(2,1)},...) custom-call(bf16[256,2048]{1,0:T(8,128)(2,1)} %get-tuple-element.32.n_own, ...), custom_call_target="tpu_custom_call" | custom-call | flops 77309411328 | bytes 104857600 | tf_op jit(solution)/shard_map/feed_forward/pallas_call | solution.py:1158
  609.0 3.8 fusion.23
  622.9 4.7 add_convert_fusion.7
  628.3 3.1 add_convert_fusion.11
  636.0 18.0 %collective-permute-done.10 = bf16[256,2048]{1,0:T(8,128)(2,1)S(1)} collective-permute-done((bf16[256,2048]{1,0:T(8,128)(2,1)S(1)}, bf16[256,2048]{1,0:T(8,128)(2,1)S(1)}, u32[]{:S(2)}, u32[]{:S(2)}) %collective-permute-start.10) | collective-permute-done | bytes 1048608 | tf_op jit(solution)/shard_map/ppermute | solution.py:31
  656.4 20.0 %collective-permute-done.3 = bf16[256,2048]{1,0:T(8,128)(2,1)S(1)} collective-permute-done((bf16[256,2048]{1,0:T(8,128)(2,1)S(1)}, bf16[256,2048]{1,0:T(8,128)(2,1)S(1)}, u32[]{:S(2)}, u32[]{:S(2)}) %collective-permute-start.3) | collective-permute-done | bytes 1048608 | tf_op jit(solution)/shard_map/ppermute | solution.py:31
  678.9 9.0 collective-permute-done.11
  688.4 10.3 collective-permute-done.4
  701.6 3.6 constant_dynamic-update-slice_fusion.12
  708.1 3.5 fusion
  711.6 3.5 fusion.12
  725.0 35.4 %collective-permute-done.14 = bf16[256,256]{1,0:T(8,128)(2,1)S(1)} collective-permute-done((bf16[256,256]{1,0:T(8,128)(2,1)S(1)}, bf16[256,256]{1,0:T(8,128)(2,1)S(1)}, u32[]{:S(2)}, u32[]{:S(2)}) %collective-permute-start.14) | collective-permute-done | bytes 131104 | tf_op jit(solution)/shard_map/ppermute | solution.py:31
  767.4 3.1 collective-permute-done.17
  773.7 48.3 %attend_back.1 = bf16[2048,768]{1,0:T(8,128)(2,1)} custom-call(s32[17]{0:T(128)} %pad_add_fusion.slots, bf16[2048,256]{1,0:T(8,128)(2,1)} %get-tuple-element.39.qs, bf16[2048,256]{1,0:T(8,128)(2,1)} %get-tuple-element.40.ks, bf16[2048,256]{1,0:T(8,128)(2,1)} %get-tuple-element.41.vs, bf16[2048,256]{1,0:T(8,128)(2,1)} %get-tuple-element.42.os, ...), custom_call_target="tpu_custom_call" | custom-call | flops 21474836480 | bytes 9437184 | tf_op jit(solution)/shard_map/attend_back/pallas_call | solution.py:232
  822.0 10.8 convolution_convert_fusion.1
  832.9 9.0 convolution_convert_fusion
  870.4 11.1 %collective-permute-done.26 = bf16[512,768]{0,1:T(8,128)(2,1)S(1)} collective-permute-done((bf16[512,768]{0,1:T(8,128)(2,1)}, bf16[512,768]{0,1:T(8,128)(2,1)S(1)}, u32[]{:S(2)}, u32[]{:S(2)}) %collective-permute-start.26) | collective-permute-done | bytes 786464 | tf_op jit(solution)/shard_map/ppermute | solution.py:139
  882.4 4.9 collective-permute-start.27
  890.9 12.6 %collective-permute-done.27 = bf16[512,768]{0,1:T(8,128)(2,1)S(1)} collective-permute-done((bf16[512,768]{0,1:T(8,128)(2,1)S(1)}, bf16[512,768]{0,1:T(8,128)(2,1)S(1)}, u32[]{:S(2)}, u32[]{:S(2)}) %collective-permute-start.27) | collective-permute-done | bytes 786464 | tf_op jit(solution)/shard_map/ppermute | solution.py:139
  905.0 5.3 collective-permute-start.28
  913.1 10.9 collective-permute-done.31
  928.3 4.0 collective-permute-done.41
  937.7 22.8 %collective-permute-done.22 = bf16[256,2048]{1,0:T(8,128)(2,1)S(1)} collective-permute-done((bf16[256,2048]{1,0:T(8,128)(2,1)S(1)}, bf16[256,2048]{1,0:T(8,128)(2,1)S(1)}, u32[]{:S(2)}, u32[]{:S(2)}) %collective-permute-start.22) | collective-permute-done | bytes 1048608 | tf_op jit(solution)/shard_map/ppermute | solution.py:31
  975.2 5.1 collective-permute-start.42
  1005.1 3.2 collective-permute-done.24
  1020.2 4.7 collective-permute-start.44
  1034.1 5.2 gather_fusion.1
  1040.2 41.3 %all-reduce.1 = (f32[2048]{0:T(1024)S(1)}, f32[2048]{0:T(1024)S(1)}) all-reduce(f32[2048]{0:T(1024)S(1)} %get-tuple-element.83, f32[2048]{0:T(1024)S(1)} %copy-done.25), channel_id=1, replica_groups=mesh['shard'=4,'ctx'=2,'tensor'=4] {'shard','ctx','tensor'}, use_global_device_ids=true, to_apply=%region_6.8 | all-reduce | flops 4096 | bytes 32768 | tf_op jit(solution)/shard_map/psum | solution.py:1345
  1086.8 5.1 gather_fusion.2
  1091.9 7.7 broadcast_select_fusion
  (313 shorter events, 177.9 us)
Async XLA Ops:
  598.6 24.3 %collective-permute-start.7 = (bf16[1024,2048]{1,0:T(8,128)(2,1)}, bf16[1024,2048]{1,0:T(8,128)(2,1)}, u32[]{:S(2)}, u32[]{:S(2)}) collective-permute-start(bf16[1024,2048]{1,0:T(8,128)(2,1)} %pad_maximum_fusion.2), channel_id=1, source_target_pairs={{0,1},{1,0},{2,3},{3,2},{4,5},{5,4},{6,7},{7,6},{8,9},{9,8},{10,11... | collective-permute-start | bytes 12582920 | tf_op jit(solution)/shard_map/ppermute | solution.py:31
  602.9 25.3 %collective-permute-start = (bf16[1024,2048]{1,0:T(8,128)(2,1)}, bf16[1024,2048]{1,0:T(8,128)(2,1)}, u32[]{:S(2)}, u32[]{:S(2)}) collective-permute-start(bf16[1024,2048]{1,0:T(8,128)(2,1)} %pad_maximum_fusion), channel_id=1, source_target_pairs={{0,1},{1,0},{2,3},{3,2},{4,5},{5,4},{6,7},{7,6},{8,9},{9,8},{10,11... | collective-permute-start | bytes 12582920 | tf_op jit(solution)/shard_map/ppermute | solution.py:31
  628.0 26.0 %collective-permute-start.10 = (bf16[256,2048]{1,0:T(8,128)(2,1)S(1)}, bf16[256,2048]{1,0:T(8,128)(2,1)S(1)}, u32[]{:S(2)}, u32[]{:S(2)}) collective-permute-start(bf16[256,2048]{1,0:T(8,128)(2,1)S(1)} %pad_maximum_fusion.12), channel_id=1, source_target_pairs={{0,2},{1,3},{2,0},{3,1},{4,6},{5,7},{6,4},{7,5},{8,10},{9,11},{10,... | collective-permute-start | bytes 3145736 | tf_op jit(solution)/shard_map/ppermute | solution.py:31
  628.1 26.1 %collective-permute-start.8 = (bf16[256,2048]{1,0:T(8,128)(2,1)S(1)}, bf16[256,2048]{1,0:T(8,128)(2,1)S(1)}, u32[]{:S(2)}, u32[]{:S(2)}) collective-permute-start(bf16[256,2048]{1,0:T(8,128)(2,1)S(1)} %pad_maximum_fusion.11), channel_id=1, source_target_pairs={{0,4},{1,5},{2,6},{3,7},{4,0},{5,1},{6,2},{7,3},{8,12},{9,13},{10,... | collective-permute-start | bytes 3145736 | tf_op jit(solution)/shard_map/ppermute | solution.py:31
  631.7 44.7 %collective-permute-start.3 = (bf16[256,2048]{1,0:T(8,128)(2,1)S(1)}, bf16[256,2048]{1,0:T(8,128)(2,1)S(1)}, u32[]{:S(2)}, u32[]{:S(2)}) collective-permute-start(bf16[256,2048]{1,0:T(8,128)(2,1)S(1)} %pad_maximum_fusion.10), channel_id=1, source_target_pairs={{0,2},{1,3},{2,0},{3,1},{4,6},{5,7},{6,4},{7,5},{8,10},{9,11},{10,... | collective-permute-start | bytes 3145736 | tf_op jit(solution)/shard_map/ppermute | solution.py:31
  633.9 42.8 %collective-permute-start.1 = (bf16[256,2048]{1,0:T(8,128)(2,1)S(1)}, bf16[256,2048]{1,0:T(8,128)(2,1)S(1)}, u32[]{:S(2)}, u32[]{:S(2)}) collective-permute-start(bf16[256,2048]{1,0:T(8,128)(2,1)S(1)} %pad_maximum_fusion.9), channel_id=1, source_target_pairs={{0,4},{1,5},{2,6},{3,7},{4,0},{5,1},{6,2},{7,3},{8,12},{9,13},{10,... | collective-permute-start | bytes 3145736 | tf_op jit(solution)/shard_map/ppermute | solution.py:31
  654.1 33.8 %collective-permute-start.11 = (bf16[128,2048]{1,0:T(8,128)(2,1)S(1)}, bf16[128,2048]{1,0:T(8,128)(2,1)S(1)}, u32[]{:S(2)}, u32[]{:S(2)}) collective-permute-start(bf16[128,2048]{1,0:T(8,128)(2,1)S(1)} %add_convert_fusion.16), channel_id=1, source_target_pairs={{0,4},{1,5},{2,6},{3,7},{4,0},{5,1},{6,2},{7,3},{8,12},{9,13},{10,... | collective-permute-start | bytes 1572872 | tf_op jit(solution)/shard_map/ppermute | solution.py:31
  654.3 33.5 %collective-permute-start.9 = (bf16[128,2048]{1,0:T(8,128)(2,1)S(1)}, bf16[128,2048]{1,0:T(8,128)(2,1)S(1)}, u32[]{:S(2)}, u32[]{:S(2)}) collective-permute-start(bf16[128,2048]{1,0:T(8,128)(2,1)S(1)} %add_convert_fusion.18), channel_id=1, source_target_pairs={{0,2},{1,3},{2,0},{3,1},{4,6},{5,7},{6,4},{7,5},{8,10},{9,11},{10,... | collective-permute-start | bytes 1572872 | tf_op jit(solution)/shard_map/ppermute | solution.py:31
  676.6 22.1 %collective-permute-start.4 = (bf16[128,2048]{1,0:T(8,128)(2,1)S(1)}, bf16[128,2048]{1,0:T(8,128)(2,1)S(1)}, u32[]{:S(2)}, u32[]{:S(2)}) collective-permute-start(bf16[128,2048]{1,0:T(8,128)(2,1)S(1)} %add_convert_fusion.20), channel_id=1, source_target_pairs={{0,4},{1,5},{2,6},{3,7},{4,0},{5,1},{6,2},{7,3},{8,12},{9,13},{10,... | collective-permute-start | bytes 1572872 | tf_op jit(solution)/shard_map/ppermute | solution.py:31
  676.8 21.9 %collective-permute-start.2 = (bf16[128,2048]{1,0:T(8,128)(2,1)S(1)}, bf16[128,2048]{1,0:T(8,128)(2,1)S(1)}, u32[]{:S(2)}, u32[]{:S(2)}) collective-permute-start(bf16[128,2048]{1,0:T(8,128)(2,1)S(1)} %add_convert_fusion.22), channel_id=1, source_target_pairs={{0,2},{1,3},{2,0},{3,1},{4,6},{5,7},{6,4},{7,5},{8,10},{9,11},{10,... | collective-permute-start | bytes 1572872 | tf_op jit(solution)/shard_map/ppermute | solution.py:31
  707.0 198.1 %collective-permute-start.33 = (bf16[256,2048]{1,0:T(8,128)(2,1)S(1)}, bf16[256,2048]{1,0:T(8,128)(2,1)}, u32[]{:S(2)}, u32[]{:S(2)}) collective-permute-start(bf16[256,2048]{1,0:T(8,128)(2,1)S(1)} %get-tuple-element.90), channel_id=1, source_target_pairs={{0,1},{1,0},{2,3},{3,2},{4,5},{5,4},{6,7},{7,6},{8,9},{9,8},{10,11... | collective-permute-start | bytes 3145736 | tf_op jit(solution)/shard_map/ppermute | solution.py:31
  720.4 167.0 %collective-permute-start.5 = (bf16[256,2048]{1,0:T(8,128)(2,1)S(1)}, bf16[256,2048]{1,0:T(8,128)(2,1)S(1)}, u32[]{:S(2)}, u32[]{:S(2)}) collective-permute-start(bf16[256,2048]{1,0:T(8,128)(2,1)S(1)} %copy-done.1), channel_id=1, source_target_pairs={{0,2},{1,3},{2,0},{3,1},{4,6},{5,7},{6,4},{7,5},{8,10},{9,11},{10,... | collective-permute-start | bytes 3145736 | tf_op jit(solution)/shard_map/ppermute | solution.py:31
  720.8 146.5 %collective-permute-start.36 = (bf16[128,2048]{1,0:T(8,128)(2,1)}, bf16[128,2048]{1,0:T(8,128)(2,1)}, u32[]{:S(2)}, u32[]{:S(2)}) collective-permute-start(bf16[128,2048]{1,0:T(8,128)(2,1)} %get-tuple-element.144), channel_id=1, source_target_pairs={{0,2},{1,3},{2,0},{3,1},{4,6},{5,7},{6,4},{7,5},{8,10},{9,11},{10,... | collective-permute-start | bytes 1572872 | tf_op jit(solution)/shard_map/ppermute | solution.py:31
  722.5 37.9 %collective-permute-start.14 = (bf16[256,256]{1,0:T(8,128)(2,1)S(1)}, bf16[256,256]{1,0:T(8,128)(2,1)S(1)}, u32[]{:S(2)}, u32[]{:S(2)}) collective-permute-start(bf16[256,256]{1,0:T(8,128)(2,1)S(1)} %get-tuple-element.154), channel_id=1, source_target_pairs={{0,3},{1,2},{2,1},{3,0},{4,7},{5,6},{6,5},{7,4},{8,11},{9,10},{10,... | collective-permute-start | bytes 393224 | tf_op jit(solution)/shard_map/ppermute | solution.py:31
  724.7 35.9 %collective-permute-start.15 = (bf16[256,256]{1,0:T(8,128)(2,1)S(1)}, bf16[256,256]{1,0:T(8,128)(2,1)S(1)}, u32[]{:S(2)}, u32[]{:S(2)}) collective-permute-start(bf16[256,256]{1,0:T(8,128)(2,1)S(1)} %get-tuple-element.153), channel_id=1, source_target_pairs={{0,4},{1,5},{2,6},{3,7},{4,0},{5,1},{6,2},{7,3},{8,12},{9,13},{10,... | collective-permute-start | bytes 393224 | tf_op jit(solution)/shard_map/ppermute | solution.py:31
  861.2 20.2 %collective-permute-start.26 = (bf16[512,768]{0,1:T(8,128)(2,1)}, bf16[512,768]{0,1:T(8,128)(2,1)S(1)}, u32[]{:S(2)}, u32[]{:S(2)}) collective-permute-start(bf16[512,768]{0,1:T(8,128)(2,1)} %bitcast.155), channel_id=1, source_target_pairs={{0,8},{1,9},{2,10},{3,11},{4,12},{5,13},{6,14},{7,15}} | collective-permute-start | bytes 2359304 | tf_op jit(solution)/shard_map/ppermute | solution.py:139
  870.0 62.4 %collective-permute-start.19 = (bf16[1024,2048]{1,0:T(8,128)(2,1)S(1)}, bf16[1024,2048]{1,0:T(8,128)(2,1)S(1)}, u32[]{:S(2)}, u32[]{:S(2)}) collective-permute-start(bf16[1024,2048]{1,0:T(8,128)(2,1)S(1)} %pad_maximum_fusion.3), channel_id=1, source_target_pairs={{0,1},{1,0},{2,3},{3,2},{4,5},{5,4},{6,7},{7,6},{8,9},{9,8},{10,11... | collective-permute-start | bytes 12582920 | tf_op jit(solution)/shard_map/ppermute | solution.py:31
  882.4 21.1 %collective-permute-start.27 = (bf16[512,768]{0,1:T(8,128)(2,1)S(1)}, bf16[512,768]{0,1:T(8,128)(2,1)S(1)}, u32[]{:S(2)}, u32[]{:S(2)}) collective-permute-start(bf16[512,768]{0,1:T(8,128)(2,1)S(1)} %fusion.27), channel_id=1, source_target_pairs={{0,8},{8,16},{1,9},{9,17},{2,10},{10,18},{3,11},{11,19},{4,12},{12... | collective-permute-start | bytes 2359304 | tf_op jit(solution)/shard_map/ppermute | solution.py:139
  887.5 24.3 %collective-permute-start.35 = (bf16[256,2048]{1,0:T(8,128)(2,1)S(1)}, bf16[256,2048]{1,0:T(8,128)(2,1)S(1)}, u32[]{:S(2)}, u32[]{:S(2)}) collective-permute-start(bf16[256,2048]{1,0:T(8,128)(2,1)S(1)} %pad_maximum_fusion.15), channel_id=1, source_target_pairs={{0,2},{1,3},{2,0},{3,1},{4,6},{5,7},{6,4},{7,5},{8,10},{9,11},{10,... | collective-permute-start | bytes 3145736 | tf_op jit(solution)/shard_map/ppermute | solution.py:31
  890.3 36.3 %collective-permute-start.39 = (bf16[256,2048]{1,0:T(8,128)(2,1)S(1)}, bf16[256,2048]{1,0:T(8,128)(2,1)S(1)}, u32[]{:S(2)}, u32[]{:S(2)}) collective-permute-start(bf16[256,2048]{1,0:T(8,128)(2,1)S(1)} %pad_maximum_fusion.16), channel_id=1, source_target_pairs={{0,4},{1,5},{2,6},{3,7},{4,0},{5,1},{6,2},{7,3},{8,12},{9,13},{10,... | collective-permute-start | bytes 3145736 | tf_op jit(solution)/shard_map/ppermute | solution.py:31
  903.5 20.5 %collective-permute-start.31 = (bf16[512,768]{0,1:T(8,128)(2,1)S(1)}, bf16[512,768]{0,1:T(8,128)(2,1)S(1)}, u32[]{:S(2)}, u32[]{:S(2)}) collective-permute-start(bf16[512,768]{0,1:T(8,128)(2,1)S(1)} %fusion.26), channel_id=1, source_target_pairs={{8,0},{16,8},{24,16},{9,1},{17,9},{25,17},{10,2},{18,10},{26,18},{... | collective-permute-start | bytes 2359304 | tf_op jit(solution)/shard_map/ppermute | solution.py:142
  905.0 20.4 %collective-permute-start.28 = (bf16[512,768]{0,1:T(8,128)(2,1)S(1)}, bf16[512,768]{0,1:T(8,128)(2,1)S(1)}, u32[]{:S(2)}, u32[]{:S(2)}) collective-permute-start(bf16[512,768]{0,1:T(8,128)(2,1)S(1)} %fusion.28), channel_id=1, source_target_pairs={{0,8},{8,16},{16,24},{1,9},{9,17},{17,25},{2,10},{10,18},{18,26},{... | collective-permute-start | bytes 2359304 | tf_op jit(solution)/shard_map/ppermute | solution.py:139
  926.6 98.3 %collective-permute-start.6 = (bf16[512,2048]{1,0:T(8,128)(2,1)}, bf16[512,2048]{1,0:T(8,128)(2,1)}, u32[]{:S(2)}, u32[]{:S(2)}) collective-permute-start(bf16[512,2048]{1,0:T(8,128)(2,1)} %pad_maximum_fusion.5), channel_id=1, source_target_pairs={{0,1},{1,0},{2,3},{3,2},{4,5},{5,4},{6,7},{7,6},{8,9},{9,8},{10,11... | collective-permute-start | bytes 6291464 | tf_op jit(solution)/shard_map/ppermute | solution.py:31
  927.2 76.1 %collective-permute-start.32 = (bf16[256,768]{0,1:T(8,128)(2,1)}, bf16[256,768]{0,1:T(8,128)(2,1)S(1)}, u32[]{:S(2)}, u32[]{:S(2)}) collective-permute-start(bf16[256,768]{0,1:T(8,128)(2,1)} %dynamic-slice_convert_fusion), channel_id=1, source_target_pairs={{0,4},{4,0},{1,5},{5,1},{2,6},{6,2},{3,7},{7,3},{8,12},{12,8},{9,1... | collective-permute-start | bytes 1179656 | tf_op jit(solution)/shard_map/ppermute | solution.py:1334
  934.4 26.1 %collective-permute-start.22 = (bf16[256,2048]{1,0:T(8,128)(2,1)S(1)}, bf16[256,2048]{1,0:T(8,128)(2,1)S(1)}, u32[]{:S(2)}, u32[]{:S(2)}) collective-permute-start(bf16[256,2048]{1,0:T(8,128)(2,1)S(1)} %pad_maximum_fusion.14), channel_id=1, source_target_pairs={{0,2},{1,3},{2,0},{3,1},{4,6},{5,7},{6,4},{7,5},{8,10},{9,11},{10,... | collective-permute-start | bytes 3145736 | tf_op jit(solution)/shard_map/ppermute | solution.py:31
  937.1 25.0 %collective-permute-start.20 = (bf16[256,2048]{1,0:T(8,128)(2,1)S(1)}, bf16[256,2048]{1,0:T(8,128)(2,1)S(1)}, u32[]{:S(2)}, u32[]{:S(2)}) collective-permute-start(bf16[256,2048]{1,0:T(8,128)(2,1)S(1)} %pad_maximum_fusion.13), channel_id=1, source_target_pairs={{0,4},{1,5},{2,6},{3,7},{4,0},{5,1},{6,2},{7,3},{8,12},{9,13},{10,... | collective-permute-start | bytes 3145736 | tf_op jit(solution)/shard_map/ppermute | solution.py:31
  972.6 23.4 %collective-permute-start.45 = (bf16[512,256]{0,1:T(8,128)(2,1)}, bf16[512,256]{0,1:T(8,128)(2,1)}, u32[]{:S(2)}, u32[]{:S(2)}) collective-permute-start(bf16[512,256]{0,1:T(8,128)(2,1)} %bitcast.160), channel_id=1, source_target_pairs={{24,16},{25,17},{26,18},{27,19},{28,20},{29,21},{30,22},{31,23}} | collective-permute-start | bytes 786440 | tf_op jit(solution)/shard_map/ppermute | solution.py:142
  975.2 24.1 %collective-permute-start.42 = (bf16[512,256]{0,1:T(8,128)(2,1)}, bf16[512,256]{0,1:T(8,128)(2,1)}, u32[]{:S(2)}, u32[]{:S(2)}) collective-permute-start(bf16[512,256]{0,1:T(8,128)(2,1)} %bitcast.159), channel_id=1, source_target_pairs={{0,8},{1,9},{2,10},{3,11},{4,12},{5,13},{6,14},{7,15}} | collective-permute-start | bytes 786440 | tf_op jit(solution)/shard_map/ppermute | solution.py:139
  984.7 23.6 %collective-permute-start.24 = (bf16[256,2048]{1,0:T(8,128)(2,1)S(1)}, bf16[256,2048]{1,0:T(8,128)(2,1)S(1)}, u32[]{:S(2)}, u32[]{:S(2)}) collective-permute-start(bf16[256,2048]{1,0:T(8,128)(2,1)S(1)} %fusion.19), channel_id=1, source_target_pairs={{0,2},{1,3},{2,0},{3,1},{4,6},{5,7},{6,4},{7,5},{8,10},{9,11},{10,... | collective-permute-start | bytes 3145736 | tf_op jit(solution)/shard_map/ppermute | solution.py:31
  997.9 18.8 %collective-permute-start.46 = (bf16[512,256]{0,1:T(8,128)(2,1)}, bf16[512,256]{0,1:T(8,128)(2,1)}, u32[]{:S(2)}, u32[]{:S(2)}) collective-permute-start(bf16[512,256]{0,1:T(8,128)(2,1)} %fusion.33), channel_id=1, source_target_pairs={{16,8},{24,16},{17,9},{25,17},{18,10},{26,18},{19,11},{27,19},{20,... | collective-permute-start | bytes 786440 | tf_op jit(solution)/shard_map/ppermute | solution.py:142
  1001.1 18.0 %collective-permute-start.43 = (bf16[512,256]{0,1:T(8,128)(2,1)}, bf16[512,256]{0,1:T(8,128)(2,1)}, u32[]{:S(2)}, u32[]{:S(2)}) collective-permute-start(bf16[512,256]{0,1:T(8,128)(2,1)} %fusion.35), channel_id=1, source_target_pairs={{0,8},{8,16},{1,9},{9,17},{2,10},{10,18},{3,11},{11,19},{4,12},{12... | collective-permute-start | bytes 786440 | tf_op jit(solution)/shard_map/ppermute | solution.py:139
  1009.7 73.1 %collective-permute-start.25 = (bf16[512,2048]{1,0:T(8,128)(2,1)}, bf16[512,2048]{1,0:T(8,128)(2,1)}, u32[]{:S(2)}, u32[]{:S(2)}) collective-permute-start(bf16[512,2048]{1,0:T(8,128)(2,1)} %pad_maximum_fusion.8), channel_id=1, source_target_pairs={{0,1},{1,0},{2,3},{3,2},{4,5},{5,4},{6,7},{7,6},{8,9},{9,8},{10,11... | collective-permute-start | bytes 6291464 | tf_op jit(solution)/shard_map/ppermute | solution.py:31
  (60 other events, 515.5 us)

commit v4 on v3

--- a/solution.py
+++ b/solution.py
@@ -25,10 +25,6 @@
     if dims is None:
         return jnp.dot(left, right, preferred_element_type=F32)
     return lax.dot_general(left, right, dims, preferred_element_type=F32)
-
-
-def swap(value, group, bit):
-    return lax.ppermute(value, LEVEL, [(i, i ^ bit) for i in range(group)])
 
 
 def level_bits(ctx, tensor):
@@ -45,102 +41,8 @@
     return bits_y, bits_x
 
 
-def level_gather(block, ctx, tensor, axis=0):
-    group = ctx * tensor
-    bits_y, bits_x = level_bits(ctx, tensor)
-    half = block.shape[axis] // 2
-    whole = {0: block, 1: swap(block, group, 1)}
-    parts = [lax.slice_in_dim(block, 0, half, axis=axis), lax.slice_in_dim(block, half, 2 * half, axis=axis)]
-    found = [{0: parts[0]}, {0: parts[1]}]
-    for which, order in enumerate((bits_x + bits_y, bits_y + bits_x)):
-        have = [(0, parts[which])]
-        for bit in order:
-            sent = jnp.concatenate([v for _, v in have], axis=axis) if len(have) > 1 else have[0][1]
-            got = swap(sent, group, bit)
-            core = swap(got, group, 1)
-            new = []
-            for i, (k, _) in enumerate(have):
-                piece = lax.slice_in_dim(got, i * half, (i + 1) * half, axis=axis)
-                new.append((k | bit, piece))
-                found[which][k | bit] = piece
-                found[which][k | bit | 1] = lax.slice_in_dim(core, i * half, (i + 1) * half, axis=axis)
-            have = have + new
-    out = []
-    for k in range(group):
-        if k in whole:
-            out.append(whole[k])
-        else:
-            out.append(jnp.concatenate([found[0][k], found[1][k]], axis=axis))
-    return out
-
-
 def plus(a, b):
     return (a.astype(F32) + b.astype(F32)).astype(BF)
-
-
-def level_sum(blocks, ctx, tensor):
-    group = ctx * tensor
-    bits_y, bits_x = level_bits(ctx, tensor)
-    rows = blocks[0].shape[0]
-    half = rows // 2
-    evens = list(range(0, group, 2))
-    got = swap(jnp.concatenate([blocks[k | 1] for k in evens], axis=0), group, 1)
-    chip = {k: plus(blocks[k], got[i * rows : (i + 1) * rows]) for i, k in enumerate(evens)}
-    done = []
-    for which, order in enumerate((bits_x + bits_y, bits_y + bits_x)):
-        have = {k: v[which * half : (which + 1) * half] for k, v in chip.items()}
-        for bit in order:
-            leave = sorted(k for k in have if k & bit)
-            got = swap(jnp.concatenate([have[k] for k in leave], axis=0), group, bit)
-            for i, k in enumerate(leave):
-                piece = got[i * half : (i + 1) * half]
-                own = have[k ^ bit]
-                have[k ^ bit] = plus(own, piece) if len(leave) > 1 else own.astype(F32) + piece.astype(F32)
-                del have[k]
-        done.append(have[0])
-    return jnp.concatenate(done, axis=0)
-
-
-def level_exchange(blocks, group):
-    return [blocks[0]] + [swap(blocks[k], group, k) for k in range(1, group)]
-
-
-def chain_gather(own, shards):
-    here = lax.axis_index("shard")
-    ups, downs = [], []
-    up = down = own
-    for k in range(1, shards):
-        up = lax.ppermute(up, "shard", [(i, i + 1) for i in range(k - 1, shards - 1)])
-        down = lax.ppermute(down, "shard", [(i, i - 1) for i in range(1, shards - k + 1)])
-        ups.append(up)
-        downs.append(down)
-    rel = [own]
-    for k in range(1, shards):
-        rel.append(jnp.where(here >= k, ups[k - 1], downs[shards - k - 1]))
-    return rel
-
-
-def in_order(rel, shards):
-    here = lax.axis_index("shard")
-    order = (here - jnp.arange(shards)) % shards
-    return jnp.take(jnp.stack(rel, axis=0), order, axis=0)
-
-
-def chain_sum(terms, shards):
-    here = lax.axis_index("shard")
-
-    def term(index):
-        return lax.dynamic_index_in_dim(terms, jnp.clip(index, 0, shards - 1), 0, keepdims=False)
-
-    up = down = None
-    for k in range(1, shards):
-        send = term(here + shards - k)
-        send = send if up is None else plus(send, up)
-        up = lax.ppermute(send, "shard", [(i, i + 1) for i in range(0, k)])
-        send = term(here - (shards - k))
-        send = send if down is None else plus(send, down)
-        down = lax.ppermute(send, "shard", [(i, i - 1) for i in range(shards - k, shards)])
-    return term(here).astype(F32) + up.astype(F32) + down.astype(F32)
 
 
 def turn(u, cos, sin):
@@ -155,101 +57,6 @@
 def wide(table, cols):
     reps = cols // table.shape[1]
     return jnp.concatenate([table] * reps, axis=1) if reps > 1 else table
-
-
-def full_spec(shape):
-    return pl.BlockSpec(shape, lambda *_: (0,) * len(shape))
-
-
-def attend_back_kernel(slots, qs, ks, vs, os, stats, go_ref, cos_ref, sin_ref, out_ref, go, delta, dq):
-    rows, cols = qs.shape
-    heads = cols // HDIM
-
-    def fill(b, carry):
-        src = pl.ds(pl.multiple_of(slots[b] * BLK, BLK), BLK)
-        dst = pl.ds(pl.multiple_of(b * BLK, BLK), BLK)
-        go[dst, :] = go_ref[src, :]
-        return carry
-
-    lax.fori_loop(0, rows // BLK, fill, 0)
-    pick = (
-        lax.broadcasted_iota(jnp.int32, (8, cols), 0) == lax.broadcasted_iota(jnp.int32, (8, cols), 1) // HDIM
-    ).astype(F32)
-    for t in range(rows // QT):
-        part = slice(t * QT, (t + 1) * QT)
-        both = go[part, :].astype(F32) * os[part, :].astype(F32)
-        delta[:, part] = lax.dot_general(
-            pick, both, NT, precision=lax.Precision.HIGHEST, preferred_element_type=F32
-        )
-    dq[...] = jnp.zeros_like(dq)
-    live = slots[rows // BLK]
-    tiles = rows // QT
-
-    def store(t, column, value, sign):
-        cos = wide(cos_ref[t * QT : (t + 1) * QT, :], cols)
-        sin = wide(sin_ref[t * QT : (t + 1) * QT, :], cols)
-        done = (turn(value, cos, -sin) if sign else value).astype(BF)
-        for i in range(QT // BLK):
-            dst = pl.ds(pl.multiple_of(slots[t * (QT // BLK) + i] * BLK, BLK), BLK)
-            out_ref[dst, column * cols : (column + 1) * cols] = done[i * BLK : (i + 1) * BLK, :]
-
-    for t in range(tiles):
-        begin = t * QT
-        count = rows - begin
-        lane_k = lax.broadcasted_iota(jnp.int32, (QT, cols), 1) // HDIM
-        lane_q = lax.broadcasted_iota(jnp.int32, (count, cols), 1) // HDIM
-        kpos = lax.broadcasted_iota(jnp.int32, (QT, QT), 0)
-        qpos = lax.broadcasted_iota(jnp.int32, (QT, QT), 1)
-        diag = jnp.where(kpos <= qpos, 0.0, NEG)
-        dead = jnp.where(lax.broadcasted_iota(jnp.int32, (QT, 1), 0) + begin < live, 0.0, NEG)
-
-        def head(h, carry):
-            dk, dv = carry
-            kt = ks[begin : begin + QT, :]
-            qm = jnp.where(lane_q == h, qs[begin:, :] * BF(0.125), BF(0))
-            gm = jnp.where(lane_q == h, go[begin:, :], BF(0))
-            s = mm(kt, qm, NT) + dead
-            first = s[:, :QT] + diag
-            s = jnp.concatenate([first, s[:, QT:]], axis=1) if count > QT else first
-            p = jnp.exp(s - stats[pl.ds(h, 1), begin:])
-            dp = mm(vs[begin : begin + QT, :], gm, NT)
-            ds = (p * (dp - delta[pl.ds(h, 1), begin:])).astype(BF)
-            km = jnp.where(lane_k == h, kt * BF(0.125), BF(0))
-            dq[begin:, :] += mm(ds, km, TN)
-            return dk + mm(ds, qm), dv + mm(p.astype(BF), gm)
-
-        zero = jnp.zeros((QT, cols), F32)
-        dk, dv = lax.fori_loop(0, heads, head, (zero, zero))
-        store(t, 1, dk, True)
-        store(t, 2, dv, False)
-    for t in range(tiles):
-        store(t, 0, dq[t * QT : (t + 1) * QT, :], True)
-
-
-def attend_back_call(slots, qs, ks, vs, os, stats, go, cos, sin):
-    rows, cols = qs.shape
-    heads = cols // HDIM
-    return pl.pallas_call(
-        attend_back_kernel,
-        grid_spec=pltpu.PrefetchScalarGridSpec(
-            num_scalar_prefetch=1,
-            grid=(1,),
-            in_specs=[full_spec(qs.shape)] * 4
-            + [full_spec(stats.shape), full_spec(go.shape), full_spec(cos.shape), full_spec(sin.shape)],
-            out_specs=full_spec((rows, 3 * cols)),
-            scratch_shapes=[
-                pltpu.VMEM((rows, cols), BF),
-                pltpu.VMEM((8, rows), F32),
-                pltpu.VMEM((rows, cols), F32),
-            ],
-        ),
-        out_shape=jax.ShapeDtypeStruct((rows, 3 * cols), BF),
-        compiler_params=pltpu.CompilerParams(vmem_limit_bytes=60 * 1024 * 1024),
-        cost_estimate=pl.CostEstimate(
-            flops=heads * rows * rows * HDIM * 20, bytes_accessed=rows * cols * 18, transcendentals=heads * rows * rows // 2
-        ),
-        name="attend_back",
-    )(slots, qs, ks, vs, os, stats, go, cos, sin)
 
 
 def flip(index, bit):
@@ -1206,13 +1013,511 @@
     )(n_own, cot, wg, wu, wd, gu_pre, d_pre)
 
 
+def last_kernel(
+    dims, place_s, at_s, live_s, dn_part, out_part, h_in, cot_in, tokens, gains_in, n_one, w_qkv_in, w_o_in, o_rel_in,
+    qs, ks, vs, os, stats, cos_ref, sin_ref,
+    result, grad_x, mine_o, got_o, mine_w, got_w, gain_out, dh_all, dh_keep, o_land, o_parts,
+    big, w_qkv, chip, c_land, parts_land, stage_own, tile_h, tile_c, gains, dh_low, d_attn, go_rel, go, delta, dq,
+    d_seq, d_rel, left_o, left_w, g_o, r_o, g_w, r_w, away_o, away_w, g_sum, g_land, g_chain, half_sum,
+    send_sems, recv_sems, own_sems,
+):
+    shards, ctx, tensor, own_rows, d_own = dims
+    p = Place(shards, ctx, tensor)
+    z, x, t = p.z, p.x, p.t
+    group = p.group
+    rows, cols = qs.shape
+    width = dh_low.shape[1]
+    heads = cols // HDIM
+    dz = ctx * d_own
+    half = own_rows // 2
+    links = Links(p, send_sems, recv_sems)
+    count = [0]
+
+    def own(src, dst):
+        i = count[0]
+        count[0] += 1
+        c = pltpu.make_async_copy(src, dst, own_sems.at[i])
+        c.start()
+        return c
+
+    p.meet(list(range(1, group)))
+
+    def block(k):
+        return pl.ds(k * own_rows, own_rows)
+
+    def mine(k=0):
+        _, tt = p.peer(k)
+        return pl.ds(pl.multiple_of(tt * own_rows, own_rows), own_rows)
+
+    orders = [p.bits_x + p.bits_y, p.bits_y + p.bits_x]
+
+    def halves(land, in_hbm=False):
+        have = [list(range(0, group, 2)), list(range(0, group, 2))]
+        spot = 0
+        for stage in range(len(orders[0])):
+            step = []
+            for h in (0, 1):
+                bit = orders[h][stage]
+                leave = [k for k in have[h] if k & bit]
+                for i, k in enumerate(leave):
+                    at = pl.ds(h * half, half)
+                    dst = land.at[h, spot + i]
+                    step.append((h, k, bit, spot + i, links.send(chip.at[k // 2, at, :], dst, p.peer_id(bit))))
+                have[h] = [k for k in have[h] if not k & bit]
+            spot += len(leave)
+            yield
+            for h, k, bit, i, m in step:
+                m.come()
+                at = pl.ds(h * half, half)
+                keep = (k ^ bit) // 2
+                if in_hbm:
+                    own(land.at[h, i], stage_own.at[pl.ds(0, half), :]).wait()
+                    came = stage_own[0:half, :].astype(F32)
+                else:
+                    came = land[h, i].astype(F32)
+                total = chip[keep, at, :].astype(F32) + came
+                if stage == len(orders[0]) - 1:
+                    half_sum[at, :] = total
+                else:
+                    chip[keep, at, :] = total.astype(BF)
+            for h, k, bit, i, m in step:
+                m.sent()
+                done_moves.append(m)
+
+    done_moves = []
+
+    odd = list(range(1, group, 2))
+    core = [links.send(dn_part.at[block(k), :], c_land.at[k // 2], p.peer_id(1)) for k in odd]
+    even = [own(dn_part.at[block(k - 1), :], chip.at[k // 2]) for k in odd]
+    load_gain = own(gains_in, gains)
+    load_o = own(w_o_in, big)
+    load_w = own(w_qkv_in, w_qkv)
+    core_out = [links.send(out_part.at[block(k), :], o_land.at[k // 2], p.peer_id(1), start=False) for k in odd]
+    for i in range(group // 2):
+        even[i].wait()
+        core[i].come()
+        chip[i] = plus(chip[i], c_land[i])
+    sums = halves(parts_land)
+    next(sums)
+    for m in core_out:
+        m.start()
+    load_gain.wait()
+    for _ in sums:
+        pass
+
+    per = tile_h.shape[0]
+    for r in range(own_rows // per):
+        at = pl.ds(r * per, per)
+        a, b = own(h_in.at[at, :], tile_h), own(cot_in.at[at, :], tile_c)
+        a.wait()
+        b.wait()
+        h = tile_h[...]
+        dn = half_sum[at, :]
+        scale = lax.rsqrt(jnp.mean(h * h, axis=-1, keepdims=True) + EPS)
+        normed = h * scale
+        scaled = dn * gains[1:2, :]
+        inner = jnp.mean(scaled * normed, axis=-1, keepdims=True)
+        d_h = tile_c[...].astype(F32) + scale * (scaled - normed * inner)
+        part = jnp.sum(dn * normed, axis=0, keepdims=True)
+        g_sum[0, 0:1, :] = part if r == 0 else g_sum[0, 0:1, :] + part
+        dh_low[at, :] = d_h.astype(BF)
+        tile_h[...] = d_h
+        own(tile_h, dh_keep.at[at, :]).wait()
+    own(dh_low, dh_all.at[block(0), :]).wait()
+
+    def dh_part(k, h):
+        if h is None:
+            return dh_all.at[block(k), :]
+        return dh_all.at[pl.ds(k * own_rows + h * half, half), :]
+
+    load_o.wait()
+    wo_rows = width // tensor
+    for tt in range(tensor):
+        acc = jnp.zeros((own_rows, wo_rows), F32)
+        for xx in range(ctx):
+            left = jnp.concatenate(
+                [dh_low[:, (zz * ctx + xx) * d_own : (zz * ctx + xx + 1) * d_own] for zz in range(shards)], axis=1
+            )
+            acc = acc + mm(left, big[xx * width + tt * wo_rows : xx * width + (tt + 1) * wo_rows, :], NT)
+        d_attn[:, tt * wo_rows : (tt + 1) * wo_rows] = acc.astype(BF)
+
+    def heads_of(k):
+        xx, tt = p.peer(k)
+        return d_attn.at[:, pl.ds(pl.multiple_of((tt * ctx + xx) * cols, cols), cols)]
+
+    swaps = [links.send(heads_of(k), go_rel.at[block(k), :], p.peer_id(k)) for k in range(1, group)]
+    own_heads = own(heads_of(0), go_rel.at[block(0), :])
+    dh_rows = links.spread(dh_part)
+    next(dh_rows)
+    load_n = []
+    per_n = shards // ctx
+    for d in range(shards):
+        load_n.append(
+            own(
+                n_one.at[:, d * dz : (d + 1) * dz],
+                big.at[(d // per_n) * rows : (d // per_n + 1) * rows, (d % per_n) * dz : (d % per_n + 1) * dz],
+            )
+        )
+    load_left = own(o_rel_in, d_rel.at[:, 0:cols])
+
+    def output():
+        for i in range(group // 2):
+            even_copy = own(out_part.at[block(2 * i), :], chip.at[i])
+            core_out[i].come()
+            land_copy = own(o_land.at[i], stage_own)
+            even_copy.wait()
+            land_copy.wait()
+            chip[i] = plus(chip[i], stage_own[...])
+        steps = halves(o_parts, True)
+        for _ in steps:
+            yield
+        for r in range(own_rows // per):
+            at = pl.ds(r * per, per)
+            own(h_in.at[at, :], tile_h).wait()
+            stage_own[at, :] = (tile_h[...] + half_sum[at, :]).astype(BF)
+        own(stage_own, result.at[mine(), :]).wait()
+        yield from everywhere(result)
+
+    def everywhere(ref):
+        def put(k, bit):
+            return links.send(ref.at[mine(k), :], ref.at[mine(k), :], p.peer_id(bit), ref.at[mine(k | bit), :])
+
+        cores = [put(0, 1)]
+        have = [0]
+        for bit in p.bits_y:
+            step = [put(k, bit) for k in have]
+            yield
+            for m in step:
+                m.come()
+            new = [k | bit for k in have]
+            cores += [put(k, 1) for k in new]
+            have = have + new
+        yield
+        for m in cores:
+            m.come()
+
+    own_heads.wait()
+    for m in swaps:
+        m.come()
+
+    def fill(b, carry):
+        go[pl.ds(pl.multiple_of(b * BLK, BLK), BLK), :] = picked(go_rel, place_s[b])
+        return carry
+
+    lax.fori_loop(0, rows // BLK, fill, 0)
+    load_left.wait()
+    for k in range(group):
+        left_o[:, k * own_rows : (k + 1) * own_rows] = d_rel[k * own_rows : (k + 1) * own_rows, 0:cols].T
+    head_row = lax.broadcasted_iota(jnp.int32, (8, cols), 0)
+    head_col = lax.broadcasted_iota(jnp.int32, (8, cols), 1) // HDIM
+    pick = jnp.where(head_row == head_col, 1.0, 0.0)
+    for i in range(rows // QT):
+        part = slice(i * QT, (i + 1) * QT)
+        both = go[part, :].astype(F32) * os[part, :].astype(F32)
+        delta[:, part] = lax.dot_general(pick, both, NT, precision=lax.Precision.HIGHEST, preferred_element_type=F32)
+    dq[...] = jnp.zeros_like(dq)
+    live = live_s[0]
+    tiles = rows // QT
+
+    def store(i, column, value, turned):
+        at = slice(i * QT, (i + 1) * QT)
+        if turned:
+            value = turn(value, wide(cos_ref[at, :], cols), -wide(sin_ref[at, :], cols))
+        d_seq[at, column * cols : (column + 1) * cols] = value.astype(BF)
+
+    out_steps = output()
+
+    def grads_o():
+        steps = sums_along(g_o, r_o, dq.at[pl.ds(0, cols), :], away_o, got_o, mine_o)
+        dh_block = d_rel.at[:, pl.ds(0, dz)]
+        for i in range(shards):
+            d = far_first(i)
+            own(dh_all.at[:, pl.ds(pl.multiple_of(d * dz, dz), dz)], dh_block).wait()
+            g_o[d] = mm(left_o[...], d_rel[:, 0:dz]).astype(BF)
+            if i < shards - 2:
+                next(steps)
+                yield
+        for _ in steps:
+            yield
+
+    def far_first(i):
+        down = shards - 1 - i
+        down = down - jnp.where(down <= z, 1, 0)
+        up = i + jnp.where(i >= z, 1, 0)
+        return z if i == shards - 1 else jnp.where(2 * z < shards, down, up)
+
+    def sums_along(g, r, fin, away, got_ref, mine_ref):
+        before = [None, None]
+        for k in range(1, shards):
+            now = []
+            for way in (0, 1):
+                d = z + shards - k if way == 0 else z - (shards - k)
+                came = z + shards - (k + 1) if way == 0 else z - (shards - (k + 1))
+                goes = z < k if way == 0 else z >= shards - k
+                comes = (z >= 1) & (z <= k) if way == 0 else (z <= shards - 2) & (z >= shards - 1 - k)
+                if k > 1:
+                    before[way].come()
+                    mid = (z >= 1) & (z < k) if way == 0 else (z <= shards - 2) & (z >= shards - k)
+
+                    @pl.when(mid)
+                    def _(d=d):
+                        g[d] = plus(g[d], r[d])
+
+                last = way == 1 and k == shards - 1
+                dst = r.at[shards] if last else r.at[d]
+                land = r.at[shards] if last else r.at[came]
+                now.append(links.send(g.at[d], dst, p.above() if way == 0 else p.below(), land, goes, comes))
+            before = now
+            yield
+        for m in before:
+            m.come()
+
+        def half_of(xx):
+            at = pl.ds(pl.multiple_of(xx * d_own, d_own), d_own)
+            fin[...] = g[z, :, at].astype(F32)
+
+            @pl.when(z > 0)
+            def _():
+                fin[...] += r[z, :, at].astype(F32)
+
+            @pl.when(z < shards - 1)
+            def _():
+                fin[...] += r[shards, :, at].astype(F32)
+
+        half_of(1 - x)
+        away[...] = fin[...].astype(BF)
+        across = links.send(away, got_ref, p.peer_id(tensor))
+        half_of(x)
+        keep = own(fin, mine_ref)
+        yield
+        across.come()
+        keep.wait()
+
+    o_steps = None
+    next(out_steps)
+    for i in range(tiles):
+        begin = i * QT
+
+        def head(h, carry):
+            dk, dv = carry
+            kt = ks[begin : begin + QT, :]
+            lane = lax.broadcasted_iota(jnp.int32, (QT, cols), 1) // HDIM
+            km = jnp.where(lane == h, kt * BF(0.125), BF(0))
+            dead = jnp.where(lax.broadcasted_iota(jnp.int32, (QT, 1), 0) + begin < live, 0.0, NEG)
+            for j in range(i, tiles):
+                at = slice(j * QT, (j + 1) * QT)
+                qm = jnp.where(lane == h, qs[at, :] * BF(0.125), BF(0))
+                gm = jnp.where(lane == h, go[at, :], BF(0))
+                s = mm(kt, qm, NT) + dead
+                if j == i:
+                    kpos = lax.broadcasted_iota(jnp.int32, (QT, QT), 0)
+                    qpos = lax.broadcasted_iota(jnp.int32, (QT, QT), 1)
+                    s = s + jnp.where(kpos <= qpos, 0.0, NEG)
+                e = jnp.exp(s - stats[pl.ds(h, 1), at])
+                dp = mm(vs[begin : begin + QT, :], gm, NT)
+                ds = (e * (dp - delta[pl.ds(h, 1), at])).astype(BF)
+                dq[at, :] += mm(ds, km, TN)
+                dk = dk + mm(ds, qm)
+                dv = dv + mm(e.astype(BF), gm)
+            return dk, dv
+
+        zero = jnp.zeros((QT, cols), F32)
+        dk, dv = lax.fori_loop(0, heads, head, (zero, zero))
+        store(i, 1, dk, True)
+        store(i, 2, dv, False)
+        store(i, 0, dq[begin : begin + QT, :], True)
+        next(out_steps, None)
+        if i == 0:
+            next(dh_rows, None)
+        elif i == 1:
+            drain(dh_rows)
+            o_steps = grads_o()
+            next(o_steps, None)
+        else:
+            next(o_steps, None)
+
+    def back_to_rows(j, carry):
+        dst = pl.ds(pl.multiple_of(j * BLK, BLK), BLK)
+        d_rel[dst, :] = picked(d_seq, at_s[j])
+        return carry
+
+    lax.fori_loop(0, rows // BLK, back_to_rows, 0)
+    drain(out_steps)
+    load_w.wait()
+
+    def d_n_one(k):
+        return mm(d_rel[k * own_rows : (k + 1) * own_rows, :], w_qkv[...], NT).astype(BF)
+
+    core = []
+    for i, k in enumerate(odd):
+        chip[i] = d_n_one(k)
+        core.append(links.send(chip.at[i], c_land.at[i], p.peer_id(1)))
+    next(o_steps, None)
+    for k in range(group):
+        left_w[:, k * own_rows : (k + 1) * own_rows] = d_rel[k * own_rows : (k + 1) * own_rows, :].T
+    for c in load_n:
+        c.wait()
+
+    def n_block(d):
+        row = pl.ds(pl.multiple_of((d // per_n) * rows, rows), rows)
+        return big[row, pl.ds(pl.multiple_of((d % per_n) * dz, dz), dz)]
+
+    w_steps = sums_along(g_w, r_w, dq.at[pl.ds(cols, 3 * cols), :], away_w, got_w, mine_w)
+
+    def grad_w(i):
+        d = far_first(i)
+        g_w[d] = mm(left_w[...], n_block(d)).astype(BF)
+
+    grad_w(0)
+    next(w_steps)
+    grad_w(1)
+    for i in range(group // 2):
+        core[i].sent()
+        done_moves.append(core[i])
+        core[i].come()
+        chip[i] = plus(d_n_one(2 * i), c_land[i])
+    sums = halves(parts_land)
+    next(sums)
+    next(w_steps, None)
+    for i in range(2, shards):
+        grad_w(i)
+        if i < shards - 1:
+            next(w_steps, None)
+    next(o_steps, None)
+    for _ in sums:
+        pass
+    for r in range(own_rows // per):
+        at = pl.ds(r * per, per)
+        src = pl.ds(pl.multiple_of(t * own_rows + r * per, per), per)
+        a, b = own(dh_keep.at[at, :], tile_h), own(tokens.at[src, :], tile_c)
+        a.wait()
+        b.wait()
+        v = tile_c[...].astype(F32)
+        dn = half_sum[at, :]
+        scale = lax.rsqrt(jnp.mean(v * v, axis=-1, keepdims=True) + EPS)
+        normed = v * scale
+        scaled = dn * gains[0:1, :]
+        inner = jnp.mean(scaled * normed, axis=-1, keepdims=True)
+        stage_own[at, :] = (tile_h[...] + scale * (scaled - normed * inner)).astype(BF)
+        part = jnp.sum(dn * normed, axis=0, keepdims=True)
+        g_sum[0, 1:2, :] = part if r == 0 else g_sum[0, 1:2, :] + part
+    g_sum[0, 2:8, :] = jnp.zeros((6, width), F32)
+    own(stage_own, grad_x.at[mine(), :]).wait()
+    x_steps = everywhere(grad_x)
+    next(x_steps)
+    bit, i = 1, 0
+    while bit < group:
+        m = links.send(g_sum.at[i], g_land.at[i], p.peer_id(bit))
+        m.come()
+        g_sum[i + 1] = g_sum[i] + g_land[i]
+        bit, i = bit * 2, i + 1
+    own(g_sum.at[i], g_chain.at[z]).wait()
+    g_steps = links.chain(lambda b: [g_chain.at[b]])
+    next(g_steps)
+    next(w_steps, None)
+    next(x_steps, None)
+    drain(g_steps)
+    total = g_chain[0]
+    for b in range(1, shards):
+        total = total + g_chain[b]
+    g_land[0] = total
+    own(g_land.at[0, :, pl.ds(pl.multiple_of((z * ctx + x) * d_own, d_own), d_own)], gain_out).wait()
+    drain(o_steps, x_steps, w_steps)
+    for m in links.moves:
+        if m not in done_moves:
+            m.sent()
+
+
+def last_call(
+    shards, ctx, tensor, place, at, live, dn_part, out_part, hidden, cot, tokens, gains, n_one, w_qkv, w_o, o_rel,
+    qs, ks, vs, os, stats, cos, sin,
+):
+    rows, cols = qs.shape
+    width = hidden.shape[1]
+    own_rows = hidden.shape[0]
+    group = ctx * tensor
+    d_own = width // (shards * ctx)
+    dz = ctx * d_own
+    dims = (shards, ctx, tensor, own_rows, d_own)
+    any_spec = pl.BlockSpec(memory_space=pl.ANY)
+    smem = pl.BlockSpec(memory_space=pltpu.SMEM)
+    vmem = pl.BlockSpec(memory_space=pltpu.VMEM)
+    dma = pltpu.SemaphoreType.DMA
+    half = own_rows // 2
+    per = min(64, own_rows)
+    bits = group.bit_length() - 1
+
+    def out(shape, kind=BF):
+        return jax.ShapeDtypeStruct(shape, kind)
+
+    parts = (2, group // 2 - 1, half, width)
+    return pl.pallas_call(
+        functools.partial(last_kernel, dims),
+        in_specs=[smem] * 3 + [any_spec] * 10 + [vmem] * 7,
+        out_specs=[any_spec] * 11,
+        out_shape=[
+            out((tensor * own_rows, width)),
+            out((tensor * own_rows, width)),
+            out((cols, d_own), F32),
+            out((cols, d_own)),
+            out((3 * cols, d_own), F32),
+            out((3 * cols, d_own)),
+            out((8, d_own), F32),
+            out((rows, width)),
+            out((own_rows, width), F32),
+            out((group // 2, own_rows, width)),
+            out(parts),
+        ],
+        scratch_shapes=[
+            pltpu.VMEM((ctx * width, shards * d_own), BF),
+            pltpu.VMEM((width, 3 * cols), BF),
+            pltpu.VMEM((group // 2, own_rows, width), BF),
+            pltpu.VMEM((group // 2, own_rows, width), BF),
+            pltpu.VMEM(parts, BF),
+            pltpu.VMEM((own_rows, width), BF),
+            pltpu.VMEM((per, width), F32),
+            pltpu.VMEM((per, width), BF),
+            pltpu.VMEM((8, width), F32),
+            pltpu.VMEM((own_rows, width), BF),
+            pltpu.VMEM((own_rows, width), BF),
+            pltpu.VMEM((rows, cols), BF),
+            pltpu.VMEM((rows, cols), BF),
+            pltpu.VMEM((8, rows), F32),
+            pltpu.VMEM((rows, cols), F32),
+            pltpu.VMEM((rows, 3 * cols), BF),
+            pltpu.VMEM((rows, 3 * cols), BF),
+            pltpu.VMEM((cols, rows), BF),
+            pltpu.VMEM((3 * cols, rows), BF),
+            pltpu.VMEM((shards, cols, dz), BF),
+            pltpu.VMEM((shards + 1, cols, dz), BF),
+            pltpu.VMEM((shards, 3 * cols, dz), BF),
+            pltpu.VMEM((shards + 1, 3 * cols, dz), BF),
+            pltpu.VMEM((cols, d_own), BF),
+            pltpu.VMEM((3 * cols, d_own), BF),
+            pltpu.VMEM((bits + 1, 8, width), F32),
+            pltpu.VMEM((bits, 8, width), F32),
+            pltpu.VMEM((shards, 8, width), F32),
+            pltpu.VMEM((own_rows, width), F32),
+            dma((300,)),
+            dma((300,)),
+            dma((100,)),
+        ],
+        compiler_params=pltpu.CompilerParams(
+            collective_id=2, has_side_effects=True, vmem_limit_bytes=63 * 1024 * 1024
+        ),
+        cost_estimate=pl.CostEstimate(
+            flops=2 * rows * width * cols * 8, bytes_accessed=64 * 1024 * 1024, transcendentals=rows * rows * cols // HDIM
+        ),
+        name="last",
+    )(place, at, live, dn_part, out_part, hidden, cot, tokens, gains, n_one, w_qkv, w_o, o_rel, qs, ks, vs, os, stats, cos, sin)
+
+
 def per_device(
     shards, ctx, tensor, tokens, cotangent, seq_len, block_slot, attn_gain, w_query, w_key, w_value, w_out, mlp_gain, w_gate, w_up, w_down
 ):
     group = ctx * tensor
     my_x = lax.axis_index("ctx")
     my_t = lax.axis_index("tensor")
-    my_z = lax.axis_index("shard")
     me = my_x * tensor + my_t
     width = tokens.shape[1]
     own_rows = tokens.shape[0] // tensor
@@ -1221,20 +1526,10 @@
     d_own = w_query.shape[0]
     cols = w_query.shape[1] // ctx
     ff = w_gate.shape[1] // ctx
-    rel = jnp.arange(group, dtype=jnp.int32)
-    swap_x = [(i, i ^ 1) for i in range(ctx)]
-
     slot = block_slot[0]
     place = ((slot // slots_each) ^ me) * slots_each + slot % slots_each
     order = jnp.arange(slot.shape[0], dtype=jnp.int32)
     at = jnp.sum(jnp.where(place[:, None] == order[None, :], order[:, None], 0), axis=0).astype(jnp.int32)
-    slots = jnp.concatenate([place, seq_len]).astype(jnp.int32)
-
-    def x_halves(array, axis):
-        size = array.shape[axis] // ctx
-        mine = lax.dynamic_slice_in_dim(array, my_x * size, size, axis=axis)
-        other = lax.dynamic_slice_in_dim(array, (1 - my_x) * size, size, axis=axis)
-        return mine, other
 
     def x_join(mine, got, axis):
         return jnp.where(
@@ -1256,66 +1551,14 @@
         shards, ctx, tensor, place.astype(jnp.int32), at, seq_len, tokens, cotangent, gains,
         w_query, w_key, w_value, w_out, w_gate, w_up, w_down, cos_rel, sin_rel,
     )
-    gain_one, gain_two = gains[0:1], gains[1:2]
-
-    def own_block(array):
-        return lax.dynamic_slice_in_dim(array, my_t * own_rows, own_rows)
-
-    x_own = own_block(tokens).astype(F32)
-    cot_own = own_block(cotangent)
-    scale_two = lax.rsqrt(jnp.mean(hidden_res * hidden_res, axis=-1, keepdims=True) + EPS)
-    normed_two = hidden_res * scale_two
     dn_part, out_part, ff_mine, ff_got, _, _ = mlp_call(
         shards, ctx, tensor, n_two_own, cot, w_gate, w_up, w_down, gu_pre, d_pre
     )
 
-    def row_blocks(array):
-        return [array[k * own_rows : (k + 1) * own_rows] for k in range(group)]
-
-    d_n_two = level_sum(row_blocks(dn_part), ctx, tensor)
-    out_own = hidden_res + level_sum(row_blocks(out_part), ctx, tensor)
-
-    def tensor_rows(own):
-        have = [(0, own)]
-        bit = tensor // 2
-        while bit >= 1:
-            sent = jnp.concatenate([v for _, v in have], axis=0) if len(have) > 1 else have[0][1]
-            got = swap(sent, group, bit)
-            have = have + [(k | bit, got[i * own_rows : (i + 1) * own_rows]) for i, (k, _) in enumerate(have)]
-            bit //= 2
-        have = [v for _, v in sorted(have, key=lambda e: e[0])]
-        ordered = jnp.take(jnp.stack(have, axis=0), my_t ^ jnp.arange(tensor), axis=0)
-        return ordered.reshape(tensor * own_rows, width)
-
-    result = tensor_rows(out_own.astype(BF))
-
-    cot_f = cot_own.astype(F32)
-    scaled = d_n_two * gain_two
-    inner = jnp.mean(scaled * normed_two, axis=-1, keepdims=True)
-    d_h = cot_f + scale_two * (scaled - normed_two * inner)
-    gain_two_part = jnp.sum(d_n_two * normed_two, axis=0)
-    d_h_low = d_h.astype(BF)
-    d_h_parts = jnp.transpose(d_h_low.reshape(own_rows, shards, ctx, d_own), (2, 0, 1, 3)).reshape(ctx, own_rows, shards * d_own)
-    d_attn = sum(mm(d_h_parts[i], w_o[i], NT) for i in range(ctx)).astype(BF)
-    blocks = jnp.transpose(d_attn.reshape(own_rows, group, cols), (1, 0, 2))
-    owner_rel = rel ^ me
-    col_of = (owner_rel % tensor) * ctx + owner_rel // tensor
-    blocks = jnp.take(blocks, col_of, axis=0)
-    go = jnp.concatenate(level_exchange([blocks[k] for k in range(group)], group), axis=0)
-    d_qkv = attend_back_call(slots, qs, ks, vs, os, stats, go, cos, sin)
-
-    d_h_all = jnp.concatenate(level_gather(d_h_low, ctx, tensor), axis=0)
-    grad_wo = mm(d_h_all, o_slot, TN).astype(BF)
-    grad_wqkv = mm(n_one, d_qkv, TN).astype(BF)
-    d_n_one = level_sum(row_blocks(mm(d_qkv, w_qkv, NT).astype(BF)), ctx, tensor)
-    x_scale = lax.rsqrt(jnp.mean(x_own * x_own, axis=-1, keepdims=True) + EPS)
-    x_normed = x_own * x_scale
-    scaled = d_n_one * gain_one
-    inner = jnp.mean(scaled * x_normed, axis=-1, keepdims=True)
-    d_x = d_h + x_scale * (scaled - x_normed * inner)
-    gain_one_part = jnp.sum(d_n_one * x_normed, axis=0)
-    grad_x = tensor_rows(d_x.astype(BF))
-
+    result, grad_x, mine_o, got_o, mine_w, got_w, gain_sums, _, _, _, _ = last_call(
+        shards, ctx, tensor, place.astype(jnp.int32), at, seq_len, dn_part, out_part, hidden_res, cot, tokens, gains,
+        n_one, w_qkv, w_o.reshape(ctx * width, shards * d_own), o_slot, qs, ks, vs, os, stats, cos, sin,
+    )
     chunks = ff_mine.shape[0]
     fc = ff // chunks
     mine = ff_mine.reshape(chunks, 3, fc, d_own)
@@ -1328,25 +1571,11 @@
     grad_gate = spread(1).T
     grad_up = spread(2).T
 
-    def attn_sums(array):
-        total = chain_sum(array.reshape(shards, ctx * d_own, array.shape[1]), shards)
-        mine, other = x_halves(total, 0)
-        got = lax.ppermute(other.astype(BF), "ctx", swap_x).astype(F32)
-        return mine, got
-
-    mine, got = attn_sums(grad_wo)
-    grad_out = x_join(mine, got, 1).T
-    mine, got = attn_sums(grad_wqkv)
-    grad_q = x_join(mine[:, :cols], got[:, :cols], 1)
-    grad_k = x_join(mine[:, cols : 2 * cols], got[:, cols : 2 * cols], 1)
-    grad_v = x_join(mine[:, 2 * cols :], got[:, 2 * cols :], 1)
-
-    def gain_sum(part):
-        total = lax.psum(part, ("shard", "ctx", "tensor"))
-        return lax.dynamic_slice_in_dim(total, (my_z * ctx + my_x) * d_own, d_own)
-
-    grad_gain_two = gain_sum(gain_two_part)
-    grad_gain_one = gain_sum(gain_one_part)
+    grad_out = x_join(mine_o, got_o.astype(F32), 0)
+    mine = mine_w.reshape(3, cols, d_own)
+    got = got_w.reshape(3, cols, d_own).astype(F32)
+    grad_q, grad_k, grad_v = (x_join(mine[i], got[i], 0).T for i in range(3))
+    grad_gain_two, grad_gain_one = gain_sums[0], gain_sums[1]
     return (
         result,
         grad_x,

time: 1110 us -> 935 us (0.84)
  Pallas kernels: 628 us -> 884 us
  waiting for transfers between devices: 174 us -> 0 us
  local copies, waits for them, and re-layouts: 86.4 us -> 23.8 us
  starting transfers between devices: 60.4 us -> 0 us
  other arithmetic: 76.9 us -> 20.9 us
  blocking collectives: 41.3 us -> 0 us
  matrix products: 29.5 us -> 0 us
    pallas_call x1, Pallas kernels: 48.3 us -> 304 us  [last_call(): pl.pallas_call(functools.partial(last_kernel, dims), in_specs=[smem] * 3...]
    ppermute x49 -> x0, waiting for transfers between devices: 174 us -> none  [the longest x35 134 us: swap(): return lax.ppermute(value, LEVEL, [(i, i ^ bit) for i in range(group)])]
    ppermute x49 -> x0, starting transfers between devices: 60.4 us -> none  [the longest x35 27.7 us: swap(): return lax.ppermute(value, LEVEL, [(i, i ^ bit) for i in range(group)])]
    psum x1 -> x0, blocking collectives: 41.3 us -> none  [gain_sum(): total = lax.psum(part, ('shard', 'ctx', 'tensor'))]
    dot_general x5 -> x0, matrix products: 29.5 us -> none  [mm(): return lax.dot_general(left, right, dims, preferred_element_type=F32)]
    unnamed x120 -> x19, local copies, waits for them, and re-layouts: 40.6 us -> 17.9 us
    convert_element_type x19 -> x1, other arithmetic: 19.5 us -> 0.92 us  [per_device(): grad_out = x_join(mine_o, got_o.astype(F32), 0)]
    dynamic_slice x9 -> x0, local copies, waits for them, and re-layouts: 13.2 us -> none  [the longest x6 11.9 us: term(): lax.dynamic_index_in_dim(terms, jnp.clip(index, 0, shards - 1), 0, keepdi...]
  transfers between devices with their start and end apart: 49 -> 0, of which waited for: 20 -> 0; matrix products, arithmetic and copies ran while one was open for 13% -> 0% of each run, Pallas kernels for 4% -> 0%
where the time goes in v4:
time: 935 us; the launch traced here: 931 us
  Pallas kernels  884 us (95%)
  local copies, waits for them, and re-layouts  23.8 us (3%)
  other arithmetic  20.9 us (2%)
    pallas_call x1, Pallas kernels, mlp_call(): pl.pallas_call(functools.partial(mlp_kernel, dims), in_specs=[any_spec] *...  328 us
    pallas_call x1, Pallas kernels, last_call(): pl.pallas_call(functools.partial(last_kernel, dims), in_specs=[smem] * 3...  304 us
    pallas_call x1, Pallas kernels, first_call(): pl.pallas_call(functools.partial(first_kernel, dims), in_specs=[smem] * 3...  252 us

profile of v4, /device:TPU:0, one launch (start us, length us, event | category | flops | bytes accessed | tf_op | source)
XLA Modules:
  0.0 930.6 jit_solution(4398775183917127670)
XLA Ops:
  1.3 0.7 fusion.11.place_s
  2.0 0.0 copy-start.4
  2.0 0.1 select_reduce_fusion.at_s
  2.1 0.7 stack.9
  2.7 0.7 stack.10
  3.4 0.6 fusion.10.gains_in
  4.0 0.1 convert_bitcast_fusion
  4.1 9.2 fusion.2
  13.3 251.8 %first.1 = (bf16[2048,2048]{1,0:T(8,128)(2,1)}, bf16[2048,768]{1,0:T(8,128)(2,1)}, bf16[2,2048,1024]{2,1,0:T(8,128)(2,1)}, bf16[2048,2048]{1,0:T(8,128)(2,1)}, b...) custom-call(s32[16]{0:T(128)} %copy-done.4, ...), custom_call_target="tpu_custom_call" | custom-call | flops 8589934592 | bytes 67108864 | tf_op jit(solution)/shard_map/first/pallas_call | solution.py:514
  265.1 328.4 %feed_forward.1 = (bf16[2048,2048]{1,0:T(8,128)(2,1)}, bf16[2048,2048]{1,0:T(8,128)(2,1)}, f32[4,768,256]{2,1,0:T(8,128)}, bf16[4,768,256]{2,1,0:T(8,128)(2,1)},...) custom-call(bf16[256,2048]{1,0:T(8,128)(2,1)} %get-tuple-element.37.n_own, ...), custom_call_target="tpu_custom_call" | custom-call | flops 77309411328 | bytes 104857600 | tf_op jit(solution)/shard_map/feed_forward/pallas_call | solution.py:965
  593.5 304.1 %last.1 = (bf16[1024,2048]{1,0:T(8,128)(2,1)}, bf16[1024,2048]{1,0:T(8,128)(2,1)}, f32[256,256]{1,0:T(8,128)}, bf16[256,256]{1,0:T(8,128)(2,1)}, f32[768,256]{1,...) custom-call(s32[16]{0:T(128)} %copy-done.4, ...), custom_call_target="tpu_custom_call" | custom-call | flops 17179869184 | bytes 67108864 | tf_op jit(solution)/shard_map/last/pallas_call | solution.py:1454
  897.6 1.3 fusion.20
  898.9 0.9 convert_element_type.39
  899.9 1.9 maximum_select_fusion.6
  901.7 1.9 fusion.18
  903.6 0.0 copy-done.3
  903.6 0.9 fusion.19
  904.5 1.0 copy.31
  905.5 2.2 fusion.5
  907.7 2.0 copy.30
  909.7 1.9 fusion.4
  911.6 2.0 copy.29
  913.7 0.2 fusion.16
  913.9 1.2 copy-done
  915.1 0.3 fusion.17
  915.4 1.6 maximum_select_fusion.2
  916.9 0.2 fusion.1
  917.2 1.6 fusion
  918.8 2.9 copy.32
  921.6 1.8 copy.33
  923.4 4.9 copy.37
  928.4 2.0 copy.38
  (12 shorter events, 0.1 us)
Async XLA Ops:
  2.0 11.3 %copy-start.4 = (s32[16]{0:T(128)}, s32[16]{0:T(128)S(1)}, u32[]{:S(2)}) copy-start(s32[16]{0:T(128)S(1)} %fusion.11.place_s) | copy-start | bytes 196
  2.1 11.2 %copy-start.5 = (s32[16]{0:T(128)}, s32[16]{0:T(128)S(1)}, u32[]{:S(2)}) copy-start(s32[16]{0:T(128)S(1)} %select_reduce_fusion.at_s) | copy-start | bytes 196
  897.6 6.0 copy-start.3
  905.5 8.1 copy-start.2
  913.7 1.4 copy-start
  923.4 4.9 copy-start.1

commit v5 on v4

--- a/solution.py
+++ b/solution.py
@@ -16,6 +16,7 @@
 BF = jnp.bfloat16
 F32 = jnp.float32
 QT = 512
+PRE = 2
 
 NT = (((1,), (1,)), ((), ()))
 TN = (((0,), (0,)), ((), ()))
@@ -115,8 +116,8 @@
 
 
 class Move:
-    def __init__(self, out, due, goes, comes):
-        self.out, self.due, self.goes, self.comes = out, due, goes, comes
+    def __init__(self, out, due, goes, comes, place=None):
+        self.out, self.due, self.goes, self.comes, self.place = out, due, goes, comes, place
 
     def _run(self, cond, fn):
         if cond is None:
@@ -154,7 +155,7 @@
                 device_id_type=pl.DeviceIdType.MESH,
             )
 
-        move = Move(copy(src, dst, where), copy(land, land, safe), goes, comes)
+        move = Move(copy(src, dst, where), copy(land, land, safe), goes, comes, i)
         self.moves.append(move)
         if start:
             move.start()
@@ -246,7 +247,7 @@
 def first_kernel(
     dims, place_s, at_s, live_s, tokens, cotangent, gains_in, wq, wk, wv, w_out, wg, wu, wd, cos_ref, sin_ref,
     n_one_out, w_qkv_out, w_o_out, cot_out, gu_out, d_out, n_own_out, h_out, gains, qs, ks, vs, os, stats, o_rel,
-    n_one, w_qkv, w_o, qkv_rel, attn_rows, h_own, n_own, x_keep,
+    n_one, w_qkv, w_o, qkv_rel, attn_rows, h_own, n_own, x_keep, gu_v, d_v,
     send_sems, recv_sems, own_sems,
 ):
     shards, ctx, tensor, fc, own_rows, d_own = dims
@@ -325,18 +326,33 @@
 
     gu_pairs = [(wg, 0), (wu, 1)]
 
-    def gu_place(xx, i):
-        return gu_out.at[d_at(xx), i * fc : (i + 1) * fc]
-
-    ff_own = [own(w.at[:, pl.ds(pl.multiple_of(x * ff, fc), fc)], gu_place(x, i)) for w, i in gu_pairs]
-    ff_own.append(own(wd.at[pl.ds(pl.multiple_of(x * ff, fc), fc), :], d_out.at[:, d_at(x)]))
-    ff_x = [
-        links.send(w.at[:, pl.ds(pl.multiple_of((1 - x) * ff, fc), fc)], gu_place(x, i), across, gu_place(1 - x, i))
-        for w, i in gu_pairs
-    ]
-    ff_x.append(
-        links.send(wd.at[pl.ds(pl.multiple_of((1 - x) * ff, fc), fc), :], d_out.at[:, d_at(x)], across, d_out.at[:, d_at(1 - x)])
-    )
+    def gu_place(c, xx, i):
+        return gu_v.at[c, d_at(xx), i * fc : (i + 1) * fc]
+
+    def ff_begin(c):
+        at = [pl.ds(pl.multiple_of(xx * ff + c * fc, fc), fc) for xx in (x, 1 - x)]
+        d_rows = slice(c * fc, (c + 1) * fc)
+        mine = [own(w.at[:, at[0]], gu_place(c, x, i)) for w, i in gu_pairs]
+        mine.append(own(wd.at[at[0], :], d_v.at[d_rows, d_at(x)]))
+        came = [links.send(w.at[:, at[1]], gu_place(c, x, i), across, gu_place(c, 1 - x, i)) for w, i in gu_pairs]
+        came.append(links.send(wd.at[at[1], :], d_v.at[d_rows, d_at(x)], across, d_v.at[d_rows, d_at(1 - x)]))
+        return mine, came
+
+    def ff_moves():
+        running = []
+        for c in range(PRE + shards):
+            if c < PRE:
+                mine, came = begun[c]
+                for m in mine:
+                    m.wait()
+                for m in came:
+                    m.come()
+                running.append(links.chain(lambda b, c=c: [gu_v.at[c, z_at(b), :], d_v.at[c * fc : (c + 1) * fc, z_at(b)]]))
+            for g in running:
+                next(g, None)
+            yield
+
+    begun = [ff_begin(0)]
     drain(gain_chain)
     drain(o_chain)
     for c in own_tok:
@@ -362,13 +378,11 @@
 
     next(qkv_chain, None)
     lax.fori_loop(0, tensor, norm, 0)
-    for c in ff_own:
-        c.wait()
-    for m in ff_x:
-        m.come()
     next(tok_rows, None)
     next(qkv_chain, None)
-    ff_chain = links.chain(lambda b: [gu_out.at[z_at(b), :], d_out.at[:, z_at(b)]])
+    for c in range(1, PRE):
+        begun.append(ff_begin(c))
+    ff_chain = ff_moves()
     next(ff_chain)
     drain(tok_rows)
     for m in tok_log:
@@ -408,11 +422,6 @@
     lax.fori_loop(0, rows // BLK, fill, 0)
     cot_rows = links.rows(cotangent, cot_out, own_rows, [])
     next(cot_rows)
-    own_cot = []
-    for k in range(tensor):
-        _, tt = p.peer(k)
-        src = cotangent.at[pl.ds(pl.multiple_of(tt * own_rows, own_rows), own_rows), :]
-        own_cot.append(own(src, cot_out.at[pl.ds(k * own_rows, own_rows), :]))
     live = live_s[0]
     for tile in range(rows // QT):
         attend_tile(tile, live, qs, ks, vs, os, stats)
@@ -452,13 +461,13 @@
     out_h = own(h_own, h_out)
     out_own = own(n_own, n_own_out)
     drain(ff_chain)
+    out_gu = own(gu_v, gu_out)
+    out_d = own(d_v, d_out)
     drain(cot_rows)
-    for c in own_cot:
-        c.wait()
     for m in links.moves:
         if m not in tok_log:
             m.sent()
-    for c in (out_n, out_w, out_o, out_h, out_own):
+    for c in (out_n, out_w, out_o, out_h, out_own, out_gu, out_d):
         c.wait()
 
 
@@ -503,7 +512,7 @@
     rows = own_rows * group
     d_own = wq.shape[0]
     cols = wq.shape[1] // ctx
-    fc = 256
+    fc = cols
     dims = (shards, ctx, tensor, fc, own_rows, d_own)
     any_spec = pl.BlockSpec(memory_space=pl.ANY)
     smem = pl.BlockSpec(memory_space=pltpu.SMEM)
@@ -520,8 +529,8 @@
             jax.ShapeDtypeStruct((width, 3 * cols), BF),
             jax.ShapeDtypeStruct((ctx, width, shards * d_own), BF),
             jax.ShapeDtypeStruct((rows, width), BF),
-            jax.ShapeDtypeStruct((width, 2 * fc), BF),
-            jax.ShapeDtypeStruct((fc, width), BF),
+            jax.ShapeDtypeStruct((PRE, width, 2 * fc), BF),
+            jax.ShapeDtypeStruct((PRE * fc, width), BF),
             jax.ShapeDtypeStruct((own_rows, width), BF),
             jax.ShapeDtypeStruct((own_rows, width), F32),
             jax.ShapeDtypeStruct((8, width), F32),
@@ -541,6 +550,8 @@
             pltpu.VMEM((own_rows, width), F32),
             pltpu.VMEM((own_rows, width), BF),
             pltpu.VMEM((own_rows, width), BF),
+            pltpu.VMEM((PRE, width, 2 * fc), BF),
+            pltpu.VMEM((PRE * fc, width), BF),
             dma((moves,)),
             dma((moves,)),
             dma((40,)),
@@ -556,13 +567,12 @@
 
 
 def mlp_kernel(
-    dims, n_own, cot_in, wg, wu, wd, gu_pre, d_pre,
+    dims, n_own, cot_far, cotangent, wg, wu, wd, gu_pre, d_pre,
     dn_out, out_out, mine_out, got_out, g_hbm, r_hbm,
     n2, cot, wgu_v, wd_v, hid, dgu, left_t, gt, st, ost, fin, away,
     lev_send, lev_recv, x_own, x_send, x_recv, a_send, a_recv, g_sem, s_sem, rs_send, rs_recv, fx_send, fx_recv, o_sem, c_sem,
 ):
-    shards, ctx, tensor, chunks, fc, rows_own, d_own = dims
-    group = ctx * tensor
+    shards, ctx, tensor, chunks, kept, fc, rows_own, d_own = dims
     rows, width = n2.shape
     dz = ctx * d_own
     ff = chunks * fc
@@ -649,17 +659,23 @@
         for d in x_copies(c, True):
             d.start()
 
-    x_start(1)
+    if chunks > PRE:
+        x_start(PRE)
     pre_copies = [
-        pltpu.make_async_copy(gu_pre, wgu_v.at[0], x_own.at[0, 0]),
-        pltpu.make_async_copy(d_pre, wd_v.at[pl.ds(0, fc), :], x_own.at[0, 1]),
+        pltpu.make_async_copy(gu_pre, wgu_v.at[pl.ds(0, PRE)], x_own.at[0, 0]),
+        pltpu.make_async_copy(d_pre, wd_v.at[pl.ds(0, PRE * fc), :], x_own.at[0, 1]),
     ]
     for d in pre_copies:
         d.start()
 
     half = rows_own // 2
     links = Links(p, lev_send, lev_recv)
-    cot_copy = pltpu.make_async_copy(cot_in, cot, c_sem.at[0])
+    near = tensor * rows_own
+    cot_copies = [pltpu.make_async_copy(cot_far.at[pl.ds(near, near), :], cot.at[pl.ds(near, near), :], c_sem.at[0])]
+    for k in range(tensor):
+        _, tt = p.peer(k)
+        src = cotangent.at[pl.ds(pl.multiple_of(tt * rows_own, rows_own), rows_own), :]
+        cot_copies.append(pltpu.make_async_copy(src, cot.at[pl.ds(k * rows_own, rows_own), :], c_sem.at[3 + k]))
     own_copy = pltpu.make_async_copy(n_own, n2.at[pl.ds(0, rows_own), :], c_sem.at[1])
     own_copy.start()
     own_copy.wait()
@@ -671,14 +687,16 @@
 
     n_rows = links.spread(n_part)
     next(n_rows)
-    cot_copy.start()
-    for c in range(2, chunks):
+    for d in cot_copies:
+        d.start()
+    for c in range(PRE + 1, chunks):
         x_start(c)
-    for d in x_copies(1, True):
-        d.wait()
-    for d in x_landed(1):
-        d.wait_recv()
-    hop_start(1, 1)
+    if chunks > PRE:
+        for d in x_copies(PRE, True):
+            d.wait()
+        for d in x_landed(PRE):
+            d.wait_recv()
+        hop_start(PRE, 1)
     next(n_rows)
 
     def ag_round(r, top):
@@ -687,7 +705,7 @@
                 continue
             c = r - k + 1
 
-            @pl.when((c >= 1) & (c < chunks))
+            @pl.when((c >= PRE) & (c < chunks))
             def _(c=c, k=k):
                 if k == 1:
                     for d in x_copies(c, True):
@@ -698,10 +716,11 @@
                     hop_wait(c, k - 1)
                 hop_start(c, k)
 
-    for r in range(2, shards - 1):
+    for r in range(PRE + 1, shards):
         ag_round(jnp.int32(r), shards - 1)
     drain(n_rows)
-    cot_copy.wait()
+    for d in cot_copies:
+        d.wait()
     for d in pre_copies:
         d.wait()
 
@@ -734,20 +753,23 @@
     def runs(way):
         return z != 0 if way == 0 else z != shards - 1
 
+    def at_slot(first):
+        return first // 2, (first >= 0) & (first % 2 == 0) & (first // 2 < kept)
+
     def rs_step(s):
         for way in (0, 1):
             for k in range(1, shards):
-                c = s - (k - 1)
-
-                @pl.when((c >= 0) & (c < chunks) & starts(way))
+                c, due = at_slot(s - (k - 1))
+
+                @pl.when(due & starts(way))
                 def _(c=c, way=way, k=k):
                     d = target(way, k)
                     rs_send_copy(g_hbm.at[c, d], c, way, d).start()
 
         for i, (way, k) in enumerate(combos):
-            c = s - (k - 1)
-
-            @pl.when((c >= 0) & (c < chunks) & sends(way, k) & runs(way))
+            c, due = at_slot(s - (k - 1))
+
+            @pl.when(due & sends(way, k) & runs(way))
             def _(c=c, way=way, k=k, i=i):
                 d = target(way, k)
 
@@ -760,9 +782,9 @@
                 pltpu.make_async_copy(r_hbm.at[c, way, d], st.at[2 * i + 1], s_sem.at[2 * i + 1]).start()
 
         last = 2 * len(combos)
-        c_fin = s - (shards - 1)
-
-        @pl.when((c_fin >= 0) & (c_fin < chunks))
+        c_fin, due_fin = at_slot(s - (shards - 1))
+
+        @pl.when(due_fin)
         def _():
             pltpu.make_async_copy(g_hbm.at[c_fin, z], st.at[last], s_sem.at[last]).start()
             for way in (0, 1):
@@ -778,9 +800,9 @@
                     st[slot] = jnp.zeros(st.shape[1:], BF)
 
         for i, (way, k) in enumerate(combos):
-            c = s - (k - 1)
-
-            @pl.when((c >= 0) & (c < chunks) & sends(way, k) & runs(way))
+            c, due = at_slot(s - (k - 1))
+
+            @pl.when(due & sends(way, k) & runs(way))
             def _(c=c, way=way, k=k, i=i):
                 d = target(way, k)
                 pltpu.make_async_copy(g_hbm.at[c, d], st.at[2 * i], s_sem.at[2 * i]).wait()
@@ -788,7 +810,7 @@
                 st[2 * i] = (st[2 * i].astype(F32) + st[2 * i + 1].astype(F32)).astype(BF)
                 rs_send_copy(st.at[2 * i], c, way, d).start()
 
-        @pl.when((c_fin >= 0) & (c_fin < chunks))
+        @pl.when(due_fin)
         def _():
             pltpu.make_async_copy(g_hbm.at[c_fin, z], st.at[last], s_sem.at[last]).wait()
             for way in (0, 1):
@@ -886,18 +908,18 @@
                 ost[slot, :, cols] = acc.astype(BF)
             pltpu.make_async_copy(ost.at[slot], out_out.at[at, :], o_sem.at[slot]).start()
 
-    tail_slots = shards - 1
+    tail_slots = 2 * (kept - 1) + shards - chunks if 2 * (kept - 1) + shards > chunks else 1
     per_slot = -(-2 * units // tail_slots)
 
     def slot_body(s, carry):
         @pl.when(s < chunks)
         def _():
-            @pl.when(s >= 1)
+            @pl.when(s >= PRE)
             def _():
                 hop_wait(s, shards - 1)
 
             phase_one(s)
-            ag_round(s + shards - 1, shards - 1)
+            ag_round(s + shards, shards - 1)
             phase_two(s)
 
         @pl.when(s >= chunks)
@@ -920,7 +942,7 @@
         at = pl.ds((u % units) * ot, ot)
         pltpu.make_async_copy(ost.at[u % 2], out_out.at[at, :], o_sem.at[u % 2]).wait()
     links.all_sent()
-    for c in range(1, chunks):
+    for c in range(PRE, chunks):
         for d in x_copies(c, False):
             d.wait_send()
         for k in range(1, shards):
@@ -931,28 +953,28 @@
             @pl.when(starts(way))
             def _(way=way, k=k):
                 d = target(way, k)
-                for c in range(chunks):
+                for c in range(kept):
                     rs_send_copy(g_hbm.at[c, d], c, way, d).wait_send()
 
     for i, (way, k) in enumerate(combos):
 
         @pl.when(sends(way, k) & runs(way))
         def _(way=way, k=k, i=i):
-            rs_send_copy(st.at[2 * i], chunks - 1, way, target(way, k)).wait_send()
-
-    pltpu.make_async_copy(fin, mine_out.at[chunks - 1], c_sem.at[2]).wait()
-    fin_copy(chunks - 1).wait_send()
-    for c in range(chunks):
+            rs_send_copy(st.at[2 * i], kept - 1, way, target(way, k)).wait_send()
+
+    pltpu.make_async_copy(fin, mine_out.at[kept - 1], c_sem.at[2]).wait()
+    fin_copy(kept - 1).wait_send()
+    for c in range(kept):
         fin_copy(c).wait_recv()
 
 
-def mlp_call(shards, ctx, tensor, n_own, cot, wg, wu, wd, gu_pre, d_pre):
+def mlp_call(shards, ctx, tensor, n_own, cot, cotangent, wg, wu, wd, gu_pre, d_pre):
     rows_own, width = n_own.shape
     group = ctx * tensor
     rows = rows_own * group
     d_own = wg.shape[0]
     ff = wg.shape[1] // ctx
-    fc = 256
+    fc = gu_pre.shape[2] // 2
     chunks = ff // fc
     dz = ctx * d_own
     any_spec = pl.BlockSpec(memory_space=pl.ANY)
@@ -960,19 +982,20 @@
     halves = 2 ** (len(bits_y) + len(bits_x)) - 1
     moves = 2 * halves + halves + 1
     stage = 4 * (shards - 2) + 3
-    dims = (shards, ctx, tensor, chunks, fc, rows_own, d_own)
+    kept = chunks - chunks // 2
+    dims = (shards, ctx, tensor, chunks, kept, fc, rows_own, d_own)
     dma = pltpu.SemaphoreType.DMA
     return pl.pallas_call(
         functools.partial(mlp_kernel, dims),
-        in_specs=[any_spec] * 7,
+        in_specs=[any_spec] * 8,
         out_specs=[any_spec] * 6,
         out_shape=[
             jax.ShapeDtypeStruct((rows, width), BF),
             jax.ShapeDtypeStruct((rows, width), BF),
-            jax.ShapeDtypeStruct((chunks, 3 * fc, d_own), F32),
-            jax.ShapeDtypeStruct((chunks, 3 * fc, d_own), BF),
+            jax.ShapeDtypeStruct((kept, 3 * fc, d_own), F32),
+            jax.ShapeDtypeStruct((kept, 3 * fc, d_own), BF),
             jax.ShapeDtypeStruct((chunks, shards, 3 * fc, dz), BF),
-            jax.ShapeDtypeStruct((chunks, 2, shards, 3 * fc, dz), BF),
+            jax.ShapeDtypeStruct((kept, 2, shards, 3 * fc, dz), BF),
         ],
         scratch_shapes=[
             pltpu.VMEM((rows, width), BF),
@@ -1001,7 +1024,7 @@
             dma((chunks,)),
             dma((chunks,)),
             dma((2,)),
-            dma((3,)),
+            dma((3 + tensor,)),
         ],
         compiler_params=pltpu.CompilerParams(
             collective_id=1, has_side_effects=True, vmem_limit_bytes=63 * 1024 * 1024
@@ -1010,18 +1033,18 @@
             flops=18 * rows * width * ff, bytes_accessed=100 * 1024 * 1024, transcendentals=rows * ff
         ),
         name="feed_forward",
-    )(n_own, cot, wg, wu, wd, gu_pre, d_pre)
+    )(n_own, cot, cotangent, wg, wu, wd, gu_pre, d_pre)
 
 
 def last_kernel(
-    dims, place_s, at_s, live_s, dn_part, out_part, h_in, cot_in, tokens, gains_in, n_one, w_qkv_in, w_o_in, o_rel_in,
-    qs, ks, vs, os, stats, cos_ref, sin_ref,
-    result, grad_x, mine_o, got_o, mine_w, got_w, gain_out, dh_all, dh_keep, o_land, o_parts,
-    big, w_qkv, chip, c_land, parts_land, stage_own, tile_h, tile_c, gains, dh_low, d_attn, go_rel, go, delta, dq,
-    d_seq, d_rel, left_o, left_w, g_o, r_o, g_w, r_w, away_o, away_w, g_sum, g_land, g_chain, half_sum,
+    dims, place_s, at_s, live_s, g_late, dn_part, out_part, h_in, cot_in, tokens, gains_in, n_one, w_qkv_in, w_o_in, o_rel_in,
+    os_in, qs, ks, vs, stats, cos_ref, sin_ref,
+    result, grad_x, mine_o, got_o, mine_w, got_w, gain_out, mine_late, got_late, dh_all, dh_keep, o_land, o_parts, r_late,
+    big, w_qkv, chip, c_land, parts_land, stage_own, tile_h, gains, dh_low, go_rel, go, delta, dq,
+    d_rel, left_o, left_w, g_o, r_o, g_w, r_w, away_o, g_sum, g_land, g_chain, half_sum, fin_late, away_late,
     send_sems, recv_sems, own_sems,
 ):
-    shards, ctx, tensor, own_rows, d_own = dims
+    shards, ctx, tensor, own_rows, d_own, kept = dims
     p = Place(shards, ctx, tensor)
     z, x, t = p.z, p.x, p.t
     group = p.group
@@ -1030,6 +1053,7 @@
     heads = cols // HDIM
     dz = ctx * d_own
     half = own_rows // 2
+    d_seq = big.at[pl.ds(0, rows), pl.ds(0, 3 * cols)]
     links = Links(p, send_sems, recv_sems)
     count = [0]
 
@@ -1086,10 +1110,136 @@
 
     done_moves = []
 
+    late = r_late.shape[0]
+    late_moves = {}
+
+    def late_wait(copies, conds):
+        for c, cond in zip(copies, conds):
+            pl.when(cond)(c.wait)
+
+    def tile_copy(src, slot, sem):
+        return pltpu.make_async_copy(src, g_w.at[slot], own_sems.at[sem])
+
+    for c in range(late):
+        for k in range(1, shards):
+            for way in (0, 1):
+                d = z + shards - k if way == 0 else z - (shards - k)
+                came = z + shards - (k + 1) if way == 0 else z - (shards - (k + 1))
+                last = way == 1 and k == shards - 1
+                dst = r_late.at[c, shards] if last else r_late.at[c, d]
+                land = r_late.at[c, shards] if last else r_late.at[c, came]
+                end = z == 0 if way == 0 else z == shards - 1
+                mid = (z >= 1) & (z < k) if way == 0 else (z <= shards - 2) & (z >= shards - k)
+                comes = (z >= 1) & (z <= k) if way == 0 else (z <= shards - 2) & (z >= shards - 1 - k)
+                where = p.above() if way == 0 else p.below()
+                src = g_late.at[kept + c, d]
+                move = links.send(src, dst, where, land, end, comes)
+                pair = g_w.at[2 * way]
+                add = Move(
+                    pltpu.make_async_remote_copy(
+                        src_ref=pair,
+                        dst_ref=dst,
+                        send_sem=links.send_sems.at[move.place],
+                        recv_sem=links.recv_sems.at[move.place],
+                        device_id=where,
+                        device_id_type=pl.DeviceIdType.MESH,
+                    ),
+                    move.due,
+                    mid,
+                    comes,
+                )
+                late_moves[c, k, way] = (move, add, d, mid)
+
+    def late_sums():
+        sent = []
+        sem = late_sem
+        for c in range(late):
+            for k in range(2, shards):
+                copies = []
+                for m in sent:
+                    m.sent()
+                sent = []
+                for way in (0, 1):
+                    late_moves[c, k - 1, way][0].come()
+                    _, add, d, mid = late_moves[c, k, way]
+                    pair = [
+                        tile_copy(g_late.at[kept + c, d], 2 * way, sem),
+                        tile_copy(r_late.at[c, d], 2 * way + 1, sem + 1),
+                    ]
+                    sem += 2
+                    for cp in pair:
+                        pl.when(mid)(cp.start)
+                    copies.append((way, add, mid, pair))
+                for way, add, mid, pair in copies:
+
+                    @pl.when(mid)
+                    def _(way=way, pair=pair):
+                        for cp in pair:
+                            cp.wait()
+                        g_w[2 * way] = plus(g_w[2 * way], g_w[2 * way + 1])
+
+                    add.start()
+                    sent.append(add)
+                yield
+            for m in sent:
+                m.sent()
+            sent = []
+            for way in (0, 1):
+                late_moves[c, shards - 1, way][0].come()
+            has_low, has_high = z > 0, z < shards - 1
+            loads = [
+                (tile_copy(g_late.at[kept + c, z], 0, sem), None),
+                (tile_copy(r_late.at[c, z], 1, sem + 1), has_low),
+                (tile_copy(r_late.at[c, shards], 2, sem + 2), has_high),
+            ]
+            sem += 3
+            for cp, cond in loads:
+                cp.start() if cond is None else pl.when(cond)(cp.start)
+            for cp, cond in loads:
+                cp.wait() if cond is None else pl.when(cond)(cp.wait)
+
+            fin = fin_late.at[pl.ds(0, 3 * cols), :]
+
+            def half_of(xx):
+                at = pl.ds(pl.multiple_of(xx * d_own, d_own), d_own)
+                fin[...] = g_w[0, :, at].astype(F32)
+
+                @pl.when(has_low)
+                def _():
+                    fin[...] += g_w[1, :, at].astype(F32)
+
+                @pl.when(has_high)
+                def _():
+                    fin[...] += g_w[2, :, at].astype(F32)
+
+            half_of(1 - x)
+            if c > 0:
+                across_late[-1].sent()
+                done_moves.append(across_late[-1])
+            away_late[...] = fin[...].astype(BF)
+            across_late.append(links.send(away_late, got_late.at[c], p.peer_id(tensor)))
+            half_of(x)
+            keep = tile_out(c, sem)
+            sem += 1
+            keep.start()
+            keep.wait()
+            yield
+
+    def tile_out(c, sem):
+        return pltpu.make_async_copy(fin_late.at[pl.ds(0, 3 * cols), :], mine_late.at[c], own_sems.at[sem])
+
+    across_late = []
+    late_sem = 120
+    late_steps = late_sums()
+
     odd = list(range(1, group, 2))
     core = [links.send(dn_part.at[block(k), :], c_land.at[k // 2], p.peer_id(1)) for k in odd]
     even = [own(dn_part.at[block(k - 1), :], chip.at[k // 2]) for k in odd]
     load_gain = own(gains_in, gains)
+    load_h = [
+        own(h_in.at[:, j * cols : (j + 1) * cols], dq.at[j * own_rows : (j + 1) * own_rows, :]) for j in range(width // cols)
+    ]
+    load_cot = own(cot_in.at[mine(), :], stage_own)
     load_o = own(w_o_in, big)
     load_w = own(w_qkv_in, w_qkv)
     core_out = [links.send(out_part.at[block(k), :], o_land.at[k // 2], p.peer_id(1), start=False) for k in odd]
@@ -1099,31 +1249,39 @@
         chip[i] = plus(chip[i], c_land[i])
     sums = halves(parts_land)
     next(sums)
+    next(late_steps, None)
     for m in core_out:
         m.start()
     load_gain.wait()
     for _ in sums:
         pass
 
-    per = tile_h.shape[0]
+    per = tile_h.shape[1]
+    spans = [(slice(j * own_rows, (j + 1) * own_rows), slice(j * cols, (j + 1) * cols)) for j in range(width // cols)]
+
+    def spread_out(r):
+        return jnp.concatenate([dq[j * own_rows + r * per : j * own_rows + (r + 1) * per, :] for j in range(len(spans))], axis=1)
+
+    for c in load_h:
+        c.wait()
+    load_cot.wait()
     for r in range(own_rows // per):
         at = pl.ds(r * per, per)
-        a, b = own(h_in.at[at, :], tile_h), own(cot_in.at[at, :], tile_c)
-        a.wait()
-        b.wait()
-        h = tile_h[...]
+        h = spread_out(r)
         dn = half_sum[at, :]
         scale = lax.rsqrt(jnp.mean(h * h, axis=-1, keepdims=True) + EPS)
         normed = h * scale
         scaled = dn * gains[1:2, :]
         inner = jnp.mean(scaled * normed, axis=-1, keepdims=True)
-        d_h = tile_c[...].astype(F32) + scale * (scaled - normed * inner)
+        d_h = stage_own[at, :].astype(F32) + scale * (scaled - normed * inner)
         part = jnp.sum(dn * normed, axis=0, keepdims=True)
         g_sum[0, 0:1, :] = part if r == 0 else g_sum[0, 0:1, :] + part
         dh_low[at, :] = d_h.astype(BF)
-        tile_h[...] = d_h
-        own(tile_h, dh_keep.at[at, :]).wait()
+        for j, (_, c) in enumerate(spans):
+            dq[j * own_rows + r * per : j * own_rows + (r + 1) * per, :] = d_h[:, c]
+    keep_dh = [own(dq.at[a, :], dh_keep.at[:, c]) for a, c in spans]
     own(dh_low, dh_all.at[block(0), :]).wait()
+    next(late_steps, None)
 
     def dh_part(k, h):
         if h is None:
@@ -1139,26 +1297,18 @@
                 [dh_low[:, (zz * ctx + xx) * d_own : (zz * ctx + xx + 1) * d_own] for zz in range(shards)], axis=1
             )
             acc = acc + mm(left, big[xx * width + tt * wo_rows : xx * width + (tt + 1) * wo_rows, :], NT)
-        d_attn[:, tt * wo_rows : (tt + 1) * wo_rows] = acc.astype(BF)
+        stage_own[:, tt * wo_rows : (tt + 1) * wo_rows] = acc.astype(BF)
 
     def heads_of(k):
         xx, tt = p.peer(k)
-        return d_attn.at[:, pl.ds(pl.multiple_of((tt * ctx + xx) * cols, cols), cols)]
+        return stage_own.at[:, pl.ds(pl.multiple_of((tt * ctx + xx) * cols, cols), cols)]
 
     swaps = [links.send(heads_of(k), go_rel.at[block(k), :], p.peer_id(k)) for k in range(1, group)]
     own_heads = own(heads_of(0), go_rel.at[block(0), :])
     dh_rows = links.spread(dh_part)
     next(dh_rows)
-    load_n = []
-    per_n = shards // ctx
-    for d in range(shards):
-        load_n.append(
-            own(
-                n_one.at[:, d * dz : (d + 1) * dz],
-                big.at[(d // per_n) * rows : (d // per_n + 1) * rows, (d % per_n) * dz : (d % per_n + 1) * dz],
-            )
-        )
     load_left = own(o_rel_in, d_rel.at[:, 0:cols])
+    load_tok = own(tokens.at[mine(), :], dh_low)
 
     def output():
         for i in range(group // 2):
@@ -1171,10 +1321,13 @@
         steps = halves(o_parts, True)
         for _ in steps:
             yield
+        loads = [own(h_in.at[pl.ds(r * per, per), :], tile_h.at[r]) for r in range(2)]
         for r in range(own_rows // per):
             at = pl.ds(r * per, per)
-            own(h_in.at[at, :], tile_h).wait()
-            stage_own[at, :] = (tile_h[...] + half_sum[at, :]).astype(BF)
+            loads[r].wait()
+            stage_own[at, :] = (tile_h[r % 2] + half_sum[at, :]).astype(BF)
+            if r + 2 < own_rows // per:
+                loads.append(own(h_in.at[pl.ds((r + 2) * per, per), :], tile_h.at[r % 2]))
         own(stage_own, result.at[mine(), :]).wait()
         yield from everywhere(result)
 
@@ -1196,25 +1349,33 @@
         for m in cores:
             m.come()
 
+    next(late_steps, None)
     own_heads.wait()
     for m in swaps:
         m.come()
+    for m in swaps:
+        m.sent()
+        done_moves.append(m)
 
     def fill(b, carry):
         go[pl.ds(pl.multiple_of(b * BLK, BLK), BLK), :] = picked(go_rel, place_s[b])
         return carry
 
     lax.fori_loop(0, rows // BLK, fill, 0)
+    load_os = own(os_in, go_rel)
     load_left.wait()
     for k in range(group):
         left_o[:, k * own_rows : (k + 1) * own_rows] = d_rel[k * own_rows : (k + 1) * own_rows, 0:cols].T
+    load_os.wait()
     head_row = lax.broadcasted_iota(jnp.int32, (8, cols), 0)
     head_col = lax.broadcasted_iota(jnp.int32, (8, cols), 1) // HDIM
     pick = jnp.where(head_row == head_col, 1.0, 0.0)
     for i in range(rows // QT):
         part = slice(i * QT, (i + 1) * QT)
-        both = go[part, :].astype(F32) * os[part, :].astype(F32)
+        both = go[part, :].astype(F32) * go_rel[part, :].astype(F32)
         delta[:, part] = lax.dot_general(pick, both, NT, precision=lax.Precision.HIGHEST, preferred_element_type=F32)
+    for c in keep_dh:
+        c.wait()
     dq[...] = jnp.zeros_like(dq)
     live = live_s[0]
     tiles = rows // QT
@@ -1228,7 +1389,7 @@
     out_steps = output()
 
     def grads_o():
-        steps = sums_along(g_o, r_o, dq.at[pl.ds(0, cols), :], away_o, got_o, mine_o)
+        steps = sums_along(g_o, r_o, fin_late.at[pl.ds(0, cols), :], away_o, got_o, mine_o)
         dh_block = d_rel.at[:, pl.ds(0, dz)]
         for i in range(shards):
             d = far_first(i)
@@ -1326,6 +1487,7 @@
         store(i, 1, dk, True)
         store(i, 2, dv, False)
         store(i, 0, dq[begin : begin + QT, :], True)
+        next(late_steps, None)
         next(out_steps, None)
         if i == 0:
             next(dh_rows, None)
@@ -1342,15 +1504,33 @@
         return carry
 
     lax.fori_loop(0, rows // BLK, back_to_rows, 0)
+    drain(late_steps)
+    for m in across_late:
+        m.come()
+    across_late[-1].sent()
+    done_moves.append(across_late[-1])
     drain(out_steps)
     load_w.wait()
 
-    def d_n_one(k):
-        return mm(d_rel[k * own_rows : (k + 1) * own_rows, :], w_qkv[...], NT).astype(BF)
-
+    def d_n_one(k, c):
+        return mm(d_rel[k * own_rows : (k + 1) * own_rows, :], w_qkv[c, :], NT)
+
+    quarters = [slice(c, c + width // 4) for c in range(0, width, width // 4)]
+
+    load_n = []
+    per_n = shards // ctx
+    for d in range(shards):
+        load_n.append(
+            own(
+                n_one.at[:, d * dz : (d + 1) * dz],
+                big.at[(d // per_n) * rows : (d // per_n + 1) * rows, (d % per_n) * dz : (d % per_n + 1) * dz],
+            )
+        )
+    load_dh = [own(dh_keep.at[:, c], dq.at[a, :]) for a, c in spans]
     core = []
     for i, k in enumerate(odd):
-        chip[i] = d_n_one(k)
+        for c in quarters:
+            chip[i, :, c] = d_n_one(k, c).astype(BF)
         core.append(links.send(chip.at[i], c_land.at[i], p.peer_id(1)))
     next(o_steps, None)
     for k in range(group):
@@ -1362,11 +1542,13 @@
         row = pl.ds(pl.multiple_of((d // per_n) * rows, rows), rows)
         return big[row, pl.ds(pl.multiple_of((d % per_n) * dz, dz), dz)]
 
-    w_steps = sums_along(g_w, r_w, dq.at[pl.ds(cols, 3 * cols), :], away_w, got_w, mine_w)
+    w_steps = sums_along(g_w, r_w, fin_late.at[pl.ds(0, 3 * cols), :], away_late, got_w, mine_w)
 
     def grad_w(i):
         d = far_first(i)
-        g_w[d] = mm(left_w[...], n_block(d)).astype(BF)
+        for i in range(3):
+            at = slice(i * cols, (i + 1) * cols)
+            g_w[d, at, :] = mm(left_w[at, :], n_block(d)).astype(BF)
 
     grad_w(0)
     next(w_steps)
@@ -1375,7 +1557,8 @@
         core[i].sent()
         done_moves.append(core[i])
         core[i].come()
-        chip[i] = plus(d_n_one(2 * i), c_land[i])
+        for c in quarters:
+            chip[i, :, c] = (d_n_one(2 * i, c) + c_land[i, :, c].astype(F32)).astype(BF)
     sums = halves(parts_land)
     next(sums)
     next(w_steps, None)
@@ -1386,19 +1569,18 @@
     next(o_steps, None)
     for _ in sums:
         pass
+    for c in load_dh:
+        c.wait()
+    load_tok.wait()
     for r in range(own_rows // per):
         at = pl.ds(r * per, per)
-        src = pl.ds(pl.multiple_of(t * own_rows + r * per, per), per)
-        a, b = own(dh_keep.at[at, :], tile_h), own(tokens.at[src, :], tile_c)
-        a.wait()
-        b.wait()
-        v = tile_c[...].astype(F32)
+        v = dh_low[at, :].astype(F32)
         dn = half_sum[at, :]
         scale = lax.rsqrt(jnp.mean(v * v, axis=-1, keepdims=True) + EPS)
         normed = v * scale
         scaled = dn * gains[0:1, :]
         inner = jnp.mean(scaled * normed, axis=-1, keepdims=True)
-        stage_own[at, :] = (tile_h[...] + scale * (scaled - normed * inner)).astype(BF)
+        stage_own[at, :] = (spread_out(r) + scale * (scaled - normed * inner)).astype(BF)
         part = jnp.sum(dn * normed, axis=0, keepdims=True)
         g_sum[0, 1:2, :] = part if r == 0 else g_sum[0, 1:2, :] + part
     g_sum[0, 2:8, :] = jnp.zeros((6, width), F32)
@@ -1429,8 +1611,8 @@
 
 
 def last_call(
-    shards, ctx, tensor, place, at, live, dn_part, out_part, hidden, cot, tokens, gains, n_one, w_qkv, w_o, o_rel,
-    qs, ks, vs, os, stats, cos, sin,
+    shards, ctx, tensor, place, at, live, g_late, dn_part, out_part, hidden, cot, tokens, gains, n_one, w_qkv, w_o, o_rel,
+    os, qs, ks, vs, stats, cos, sin,
 ):
     rows, cols = qs.shape
     width = hidden.shape[1]
@@ -1438,13 +1620,15 @@
     group = ctx * tensor
     d_own = width // (shards * ctx)
     dz = ctx * d_own
-    dims = (shards, ctx, tensor, own_rows, d_own)
+    chunks = g_late.shape[0]
+    late = chunks // 2
+    dims = (shards, ctx, tensor, own_rows, d_own, chunks - late)
     any_spec = pl.BlockSpec(memory_space=pl.ANY)
     smem = pl.BlockSpec(memory_space=pltpu.SMEM)
     vmem = pl.BlockSpec(memory_space=pltpu.VMEM)
     dma = pltpu.SemaphoreType.DMA
     half = own_rows // 2
-    per = min(64, own_rows)
+    per = min(32, own_rows)
     bits = group.bit_length() - 1
 
     def out(shape, kind=BF):
@@ -1453,8 +1637,8 @@
     parts = (2, group // 2 - 1, half, width)
     return pl.pallas_call(
         functools.partial(last_kernel, dims),
-        in_specs=[smem] * 3 + [any_spec] * 10 + [vmem] * 7,
-        out_specs=[any_spec] * 11,
+        in_specs=[smem] * 3 + [any_spec] * 12 + [vmem] * 6,
+        out_specs=[any_spec] * 14,
         out_shape=[
             out((tensor * own_rows, width)),
             out((tensor * own_rows, width)),
@@ -1463,10 +1647,13 @@
             out((3 * cols, d_own), F32),
             out((3 * cols, d_own)),
             out((8, d_own), F32),
+            out((late, 3 * cols, d_own), F32),
+            out((late, 3 * cols, d_own)),
             out((rows, width)),
             out((own_rows, width), F32),
             out((group // 2, own_rows, width)),
             out(parts),
+            out((late, shards + 1, 3 * cols, dz)),
         ],
         scratch_shapes=[
             pltpu.VMEM((ctx * width, shards * d_own), BF),
@@ -1475,16 +1662,13 @@
             pltpu.VMEM((group // 2, own_rows, width), BF),
             pltpu.VMEM(parts, BF),
             pltpu.VMEM((own_rows, width), BF),
-            pltpu.VMEM((per, width), F32),
-            pltpu.VMEM((per, width), BF),
+            pltpu.VMEM((2, per, width), F32),
             pltpu.VMEM((8, width), F32),
-            pltpu.VMEM((own_rows, width), BF),
             pltpu.VMEM((own_rows, width), BF),
             pltpu.VMEM((rows, cols), BF),
             pltpu.VMEM((rows, cols), BF),
             pltpu.VMEM((8, rows), F32),
             pltpu.VMEM((rows, cols), F32),
-            pltpu.VMEM((rows, 3 * cols), BF),
             pltpu.VMEM((rows, 3 * cols), BF),
             pltpu.VMEM((cols, rows), BF),
             pltpu.VMEM((3 * cols, rows), BF),
@@ -1493,14 +1677,15 @@
             pltpu.VMEM((shards, 3 * cols, dz), BF),
             pltpu.VMEM((shards + 1, 3 * cols, dz), BF),
             pltpu.VMEM((cols, d_own), BF),
-            pltpu.VMEM((3 * cols, d_own), BF),
             pltpu.VMEM((bits + 1, 8, width), F32),
             pltpu.VMEM((bits, 8, width), F32),
             pltpu.VMEM((shards, 8, width), F32),
             pltpu.VMEM((own_rows, width), F32),
+            pltpu.VMEM((3 * cols, d_own), F32),
+            pltpu.VMEM((3 * cols, d_own), BF),
             dma((300,)),
             dma((300,)),
-            dma((100,)),
+            dma((240,)),
         ],
         compiler_params=pltpu.CompilerParams(
             collective_id=2, has_side_effects=True, vmem_limit_bytes=63 * 1024 * 1024
@@ -1509,7 +1694,7 @@
             flops=2 * rows * width * cols * 8, bytes_accessed=64 * 1024 * 1024, transcendentals=rows * rows * cols // HDIM
         ),
         name="last",
-    )(place, at, live, dn_part, out_part, hidden, cot, tokens, gains, n_one, w_qkv, w_o, o_rel, qs, ks, vs, os, stats, cos, sin)
+    )(place, at, live, g_late, dn_part, out_part, hidden, cot, tokens, gains, n_one, w_qkv, w_o, o_rel, os, qs, ks, vs, stats, cos, sin)
 
 
 def per_device(
@@ -1551,14 +1736,16 @@
         shards, ctx, tensor, place.astype(jnp.int32), at, seq_len, tokens, cotangent, gains,
         w_query, w_key, w_value, w_out, w_gate, w_up, w_down, cos_rel, sin_rel,
     )
-    dn_part, out_part, ff_mine, ff_got, _, _ = mlp_call(
-        shards, ctx, tensor, n_two_own, cot, w_gate, w_up, w_down, gu_pre, d_pre
+    dn_part, out_part, ff_mine, ff_got, g_late, _ = mlp_call(
+        shards, ctx, tensor, n_two_own, cot, cotangent, w_gate, w_up, w_down, gu_pre, d_pre
     )
 
-    result, grad_x, mine_o, got_o, mine_w, got_w, gain_sums, _, _, _, _ = last_call(
-        shards, ctx, tensor, place.astype(jnp.int32), at, seq_len, dn_part, out_part, hidden_res, cot, tokens, gains,
-        n_one, w_qkv, w_o.reshape(ctx * width, shards * d_own), o_slot, qs, ks, vs, os, stats, cos, sin,
+    result, grad_x, mine_o, got_o, mine_w, got_w, gain_sums, late_mine, late_got, *_ = last_call(
+        shards, ctx, tensor, place.astype(jnp.int32), at, seq_len, g_late, dn_part, out_part, hidden_res, cotangent, tokens, gains,
+        n_one, w_qkv, w_o.reshape(ctx * width, shards * d_own), o_slot, os, qs, ks, vs, stats, cos, sin,
     )
+    ff_mine = jnp.concatenate([ff_mine, late_mine], axis=0)
+    ff_got = jnp.concatenate([ff_got, late_got], axis=0)
     chunks = ff_mine.shape[0]
     fc = ff // chunks
     mine = ff_mine.reshape(chunks, 3, fc, d_own)

time: 935 us -> 772 us (0.83)
  Pallas kernels: 884 us -> 721 us
    pallas_call x1, Pallas kernels: 328 us -> 214 us  [mlp_call(): pl.pallas_call(functools.partial(mlp_kernel, dims), in_specs=[any_spec] *...]
    pallas_call x1, Pallas kernels: 252 us -> 220 us  [first_call(): pl.pallas_call(functools.partial(first_kernel, dims), in_specs=[smem] * 3...]
    pallas_call x1, Pallas kernels: 304 us -> 288 us  [last_call(): pl.pallas_call(functools.partial(last_kernel, dims), in_specs=[smem] * 3...]
where the time goes in v5:
time: 772 us; the launch traced here: 761 us
  Pallas kernels  721 us (93%)
  other arithmetic  20.4 us (3%)
  local copies, waits for them, and re-layouts  17.9 us (2%)
    pallas_call x1, Pallas kernels, last_call(): pl.pallas_call(functools.partial(last_kernel, dims), in_specs=[smem] * 3...  288 us
    pallas_call x1, Pallas kernels, first_call(): pl.pallas_call(functools.partial(first_kernel, dims), in_specs=[smem] * 3...  220 us
    pallas_call x1, Pallas kernels, mlp_call(): pl.pallas_call(functools.partial(mlp_kernel, dims), in_specs=[any_spec] *...  214 us

profile of v5, /device:TPU:0, one launch (start us, length us, event | category | flops | bytes accessed | tf_op | source)
XLA Modules:
  0.0 761.4 jit_solution(13881029139433824458)
XLA Ops:
  1.3 0.7 fusion.11.place_s
  2.0 0.0 copy-start.4
  2.0 0.1 select_reduce_fusion.at_s
  2.1 0.7 stack.9
  2.7 0.7 stack.10
  3.4 0.6 fusion.10.gains_in
  4.0 0.1 convert_bitcast_fusion
  4.1 9.2 %fusion.2 = (f32[2048,128]{1,0:T(8,128)}, f32[2048,128]{1,0:T(8,128)}, f32[2048,128]{1,0:T(8,128)}, f32[2048,128]{1,0:T(8,128)}) fusion(f32[128]{0:T(128)S(1)} %get-tuple-element.109, f32[128]{0:T(128)S(1)} %get-tuple-element.110, f32[2048]{0:T(1024)S(1)} %convert_bitcast_fusion), kind=kLoop, calls=%fused_computation.9 | loop fusion | flops 1048576 | bytes 4203520 | tf_op jit(solution)/shard_map/mul | solution.py:1733
  13.3 220.4 %first.1 = (bf16[2048,2048]{1,0:T(8,128)(2,1)}, bf16[2048,768]{1,0:T(8,128)(2,1)}, bf16[2,2048,1024]{2,1,0:T(8,128)(2,1)}, bf16[2048,2048]{1,0:T(8,128)(2,1)}, b...) custom-call(s32[16]{0:T(128)} %copy-done.4, ...), custom_call_target="tpu_custom_call" | custom-call | flops 8589934592 | bytes 67108864 | tf_op jit(solution)/shard_map/first/pallas_call | solution.py:523
  233.7 213.5 %feed_forward.1 = (bf16[2048,2048]{1,0:T(8,128)(2,1)}, bf16[2048,2048]{1,0:T(8,128)(2,1)}, f32[2,768,256]{2,1,0:T(8,128)}, bf16[2,768,256]{2,1,0:T(8,128)(2,1)},...) custom-call(bf16[256,2048]{1,0:T(8,128)(2,1)} %get-tuple-element.40.n_own, ...), custom_call_target="tpu_custom_call" | custom-call | flops 77309411328 | bytes 104857600 | tf_op jit(solution)/shard_map/feed_forward/pallas_call | solution.py:988
  447.2 287.5 %last.1 = (bf16[1024,2048]{1,0:T(8,128)(2,1)}, bf16[1024,2048]{1,0:T(8,128)(2,1)}, f32[256,256]{1,0:T(8,128)}, bf16[256,256]{1,0:T(8,128)(2,1)}, f32[768,256]{1,...) custom-call(s32[16]{0:T(128)} %copy-done.4, ...), custom_call_target="tpu_custom_call" | custom-call | flops 17179869184 | bytes 67108864 | tf_op jit(solution)/shard_map/last/pallas_call | solution.py:1638
  734.8 1.3 fusion.20
  736.1 0.9 convert_element_type.39
  737.1 1.9 maximum_select_fusion.6
  739.0 1.3 pad_maximum_fusion.1
  740.3 0.0 copy-done.2
  740.3 0.1 fusion.18
  740.4 0.1 fusion.19
  740.5 1.0 copy.31
  741.6 1.0 copy.30
  742.6 1.0 copy.29
  743.6 2.1 pad_maximum_fusion
  745.7 0.2 fusion.16
  745.9 0.3 fusion.17
  746.2 1.6 maximum_select_fusion.2
  747.8 0.2 fusion.1
  748.1 1.6 fusion
  749.6 2.9 copy.32
  752.5 1.8 copy.33
  754.3 4.9 copy.37
  759.2 0.0 copy-done
  759.2 2.0 copy.38
  (14 shorter events, 0.1 us)
Async XLA Ops:
  2.0 11.3 %copy-start.4 = (s32[16]{0:T(128)}, s32[16]{0:T(128)S(1)}, u32[]{:S(2)}) copy-start(s32[16]{0:T(128)S(1)} %fusion.11.place_s) | copy-start | bytes 196
  2.1 11.2 %copy-start.5 = (s32[16]{0:T(128)}, s32[16]{0:T(128)S(1)}, u32[]{:S(2)}) copy-start(s32[16]{0:T(128)S(1)} %select_reduce_fusion.at_s) | copy-start | bytes 196
  447.2 291.8 %copy-start.3 = (bf16[2,768,256]{2,1,0:T(8,128)(2,1)S(1)}, bf16[2,768,256]{2,1,0:T(8,128)(2,1)}, u32[]{:S(2)}) copy-start(bf16[2,768,256]{2,1,0:T(8,128)(2,1)} %get-tuple-element.67) | copy-start | bytes 2359300
  737.1 3.3 copy-start.2
  739.0 1.4 copy-start.1
  754.3 4.9 copy-start

commit v6 on v5

--- a/solution.py
+++ b/solution.py
@@ -246,7 +246,7 @@
 
 def first_kernel(
     dims, place_s, at_s, live_s, tokens, cotangent, gains_in, wq, wk, wv, w_out, wg, wu, wd, cos_ref, sin_ref,
-    n_one_out, w_qkv_out, w_o_out, cot_out, gu_out, d_out, n_own_out, h_out, gains, qs, ks, vs, os, stats, o_rel,
+    n_one_out, w_qkv_out, w_o_out, cot_out, gu_out, d_out, n_all, h_out, gains, qs, ks, vs, os, stats, o_rel,
     n_one, w_qkv, w_o, qkv_rel, attn_rows, h_own, n_own, x_keep, gu_v, d_v,
     send_sems, recv_sems, own_sems,
 ):
@@ -384,6 +384,8 @@
         begun.append(ff_begin(c))
     ff_chain = ff_moves()
     next(ff_chain)
+    cot_rows = links.rows(cotangent, cot_out, own_rows, [])
+    next(cot_rows)
     drain(tok_rows)
     for m in tok_log:
         m.sent()
@@ -391,7 +393,6 @@
     out_n = own(n_one, n_one_out)
     next(o_spread, None)
     drain(qkv_chain)
-    next(ff_chain, None)
     out_w = own(w_qkv, w_qkv_out)
 
     def project(r, carry):
@@ -409,7 +410,6 @@
         return carry
 
     lax.fori_loop(0, group, project, 0)
-    next(o_spread, None)
 
     def fill(b, carry):
         dst = pl.ds(pl.multiple_of(b * BLK, BLK), BLK)
@@ -420,14 +420,16 @@
         return carry
 
     lax.fori_loop(0, rows // BLK, fill, 0)
-    cot_rows = links.rows(cotangent, cot_out, own_rows, [])
-    next(cot_rows)
+    next(ff_chain, None)
     live = live_s[0]
-    for tile in range(rows // QT):
+    tiles = rows // QT
+    for tile in range(tiles):
         attend_tile(tile, live, qs, ks, vs, os, stats)
-        next(ff_chain, None)
-        next(o_spread, None)
-        next(cot_rows, None)
+        if tile == 1:
+            next(cot_rows, None)
+        if tile == 2:
+            next(o_spread, None)
+    next(ff_chain, None)
 
     def back_to_rows(j, carry):
         dst = pl.ds(pl.multiple_of(j * BLK, BLK), BLK)
@@ -446,6 +448,7 @@
     own_heads = own(o_rel.at[pl.ds(0, own_rows), :], head_at(0))
     drain(o_spread)
     out_o = own(w_o, w_o_out)
+    next(cot_rows, None)
     own_heads.wait()
     for m in swaps:
         m.come()
@@ -459,15 +462,28 @@
     scale = lax.rsqrt(jnp.mean(h * h, axis=-1, keepdims=True) + EPS)
     n_own[...] = (h * scale * gains[1:2, :]).astype(BF)
     out_h = own(h_own, h_out)
-    out_own = own(n_own, n_own_out)
+    own(n_own, n_all.at[pl.ds(0, own_rows), :]).wait()
+
+    def n_part(k, h):
+        if h is None:
+            return n_all.at[pl.ds(k * own_rows, own_rows), :]
+        return n_all.at[pl.ds(k * own_rows + h * (own_rows // 2), own_rows // 2), :]
+
+    n_spread = links.spread(n_part)
+    next(n_spread)
+    next(ff_chain, None)
+    next(n_spread, None)
+    next(cot_rows, None)
+    next(n_spread, None)
     drain(ff_chain)
     out_gu = own(gu_v, gu_out)
     out_d = own(d_v, d_out)
     drain(cot_rows)
+    drain(n_spread)
     for m in links.moves:
         if m not in tok_log:
             m.sent()
-    for c in (out_n, out_w, out_o, out_h, out_own, out_gu, out_d):
+    for c in (out_n, out_w, out_o, out_h, out_gu, out_d):
         c.wait()
 
 
@@ -531,7 +547,7 @@
             jax.ShapeDtypeStruct((rows, width), BF),
             jax.ShapeDtypeStruct((PRE, width, 2 * fc), BF),
             jax.ShapeDtypeStruct((PRE * fc, width), BF),
-            jax.ShapeDtypeStruct((own_rows, width), BF),
+            jax.ShapeDtypeStruct((rows, width), BF),
             jax.ShapeDtypeStruct((own_rows, width), F32),
             jax.ShapeDtypeStruct((8, width), F32),
             piece,
@@ -567,10 +583,10 @@
 
 
 def mlp_kernel(
-    dims, n_own, cot_far, cotangent, wg, wu, wd, gu_pre, d_pre,
+    dims, n_in, cot_far, cotangent, wg, wu, wd, gu_pre, d_pre,
     dn_out, out_out, mine_out, got_out, g_hbm, r_hbm,
     n2, cot, wgu_v, wd_v, hid, dgu, left_t, gt, st, ost, fin, away,
-    lev_send, lev_recv, x_own, x_send, x_recv, a_send, a_recv, g_sem, s_sem, rs_send, rs_recv, fx_send, fx_recv, o_sem, c_sem,
+    x_own, x_send, x_recv, a_send, a_recv, g_sem, s_sem, rs_send, rs_recv, fx_send, fx_recv, o_sem, c_sem,
 ):
     shards, ctx, tensor, chunks, kept, fc, rows_own, d_own = dims
     rows, width = n2.shape
@@ -579,11 +595,9 @@
     z = lax.axis_index("shard")
     x = lax.axis_index("ctx")
     t = lax.axis_index("tensor")
-    bits_y, bits_x = level_bits(ctx, tensor)
-
     p = Place(shards, ctx, tensor)
     above, below = p.above, p.below
-    p.meet([1] + bits_y + bits_x)
+    p.meet([1, tensor])
 
     here_too = (z, x, flip(t, 1))
 
@@ -668,25 +682,13 @@
     for d in pre_copies:
         d.start()
 
-    half = rows_own // 2
-    links = Links(p, lev_send, lev_recv)
     near = tensor * rows_own
     cot_copies = [pltpu.make_async_copy(cot_far.at[pl.ds(near, near), :], cot.at[pl.ds(near, near), :], c_sem.at[0])]
     for k in range(tensor):
         _, tt = p.peer(k)
         src = cotangent.at[pl.ds(pl.multiple_of(tt * rows_own, rows_own), rows_own), :]
         cot_copies.append(pltpu.make_async_copy(src, cot.at[pl.ds(k * rows_own, rows_own), :], c_sem.at[3 + k]))
-    own_copy = pltpu.make_async_copy(n_own, n2.at[pl.ds(0, rows_own), :], c_sem.at[1])
-    own_copy.start()
-    own_copy.wait()
-
-    def n_part(k, h):
-        if h is None:
-            return n2.at[pl.ds(k * rows_own, rows_own), :]
-        return n2.at[pl.ds(k * rows_own + h * half, half), :]
-
-    n_rows = links.spread(n_part)
-    next(n_rows)
+    cot_copies.append(pltpu.make_async_copy(n_in, n2, c_sem.at[1]))
     for d in cot_copies:
         d.start()
     for c in range(PRE + 1, chunks):
@@ -697,7 +699,6 @@
         for d in x_landed(PRE):
             d.wait_recv()
         hop_start(PRE, 1)
-    next(n_rows)
 
     def ag_round(r, top):
         for k in range(shards - 1, 0, -1):
@@ -716,9 +717,6 @@
                     hop_wait(c, k - 1)
                 hop_start(c, k)
 
-    for r in range(PRE + 1, shards):
-        ag_round(jnp.int32(r), shards - 1)
-    drain(n_rows)
     for d in cot_copies:
         d.wait()
     for d in pre_copies:
@@ -919,8 +917,9 @@
                 hop_wait(s, shards - 1)
 
             phase_one(s)
-            ag_round(s + shards, shards - 1)
             phase_two(s)
+            for i in range(shards - 3):
+                ag_round(PRE + 1 + s * (shards - 3) + i, shards - 1)
 
         @pl.when(s >= chunks)
         def _():
@@ -941,7 +940,6 @@
     for u in (2 * units - 2, 2 * units - 1):
         at = pl.ds((u % units) * ot, ot)
         pltpu.make_async_copy(ost.at[u % 2], out_out.at[at, :], o_sem.at[u % 2]).wait()
-    links.all_sent()
     for c in range(PRE, chunks):
         for d in x_copies(c, False):
             d.wait_send()
@@ -968,19 +966,15 @@
         fin_copy(c).wait_recv()
 
 
-def mlp_call(shards, ctx, tensor, n_own, cot, cotangent, wg, wu, wd, gu_pre, d_pre):
-    rows_own, width = n_own.shape
-    group = ctx * tensor
-    rows = rows_own * group
+def mlp_call(shards, ctx, tensor, n_all, cot, cotangent, wg, wu, wd, gu_pre, d_pre):
+    rows, width = n_all.shape
+    rows_own = rows // (ctx * tensor)
     d_own = wg.shape[0]
     ff = wg.shape[1] // ctx
     fc = gu_pre.shape[2] // 2
     chunks = ff // fc
     dz = ctx * d_own
     any_spec = pl.BlockSpec(memory_space=pl.ANY)
-    bits_y, bits_x = level_bits(ctx, tensor)
-    halves = 2 ** (len(bits_y) + len(bits_x)) - 1
-    moves = 2 * halves + halves + 1
     stage = 4 * (shards - 2) + 3
     kept = chunks - chunks // 2
     dims = (shards, ctx, tensor, chunks, kept, fc, rows_own, d_own)
@@ -1010,8 +1004,6 @@
             pltpu.VMEM((2, 256, width), BF),
             pltpu.VMEM((3 * fc, d_own), F32),
             pltpu.VMEM((3 * fc, d_own), BF),
-            dma((moves,)),
-            dma((moves,)),
             dma((chunks, 3)),
             dma((chunks, 3)),
             dma((chunks, 3)),
@@ -1033,7 +1025,7 @@
             flops=18 * rows * width * ff, bytes_accessed=100 * 1024 * 1024, transcendentals=rows * ff
         ),
         name="feed_forward",
-    )(n_own, cot, cotangent, wg, wu, wd, gu_pre, d_pre)
+    )(n_all, cot, cotangent, wg, wu, wd, gu_pre, d_pre)
 
 
 def last_kernel(
@@ -1455,6 +1447,7 @@
         keep.wait()
 
     o_steps = None
+    next(dh_rows)
     next(out_steps)
     for i in range(tiles):
         begin = i * QT
@@ -1488,14 +1481,14 @@
         store(i, 2, dv, False)
         store(i, 0, dq[begin : begin + QT, :], True)
         next(late_steps, None)
-        next(out_steps, None)
         if i == 0:
             next(dh_rows, None)
-        elif i == 1:
+        else:
+            next(out_steps, None)
+        if i == 1:
             drain(dh_rows)
             o_steps = grads_o()
-            next(o_steps, None)
-        else:
+        if i >= 1:
             next(o_steps, None)
 
     def back_to_rows(j, carry):

time: 772 us -> 721 us (0.934)
  Pallas kernels: 721 us -> 672 us
    pallas_call x1, Pallas kernels: 214 us -> 180 us  [mlp_call(): pl.pallas_call(functools.partial(mlp_kernel, dims), in_specs=[any_spec] *...]
    pallas_call x1, Pallas kernels: 220 us -> 202 us  [first_call(): pl.pallas_call(functools.partial(first_kernel, dims), in_specs=[smem] * 3...]
where the time goes in v6:
time: 721 us; the launch traced here: 712 us
  Pallas kernels  672 us (93%)
  other arithmetic  20.4 us (3%)
  local copies, waits for them, and re-layouts  17.9 us (2%)
    pallas_call x1, Pallas kernels, last_call(): pl.pallas_call(functools.partial(last_kernel, dims), in_specs=[smem] * 3...  290 us
    pallas_call x1, Pallas kernels, first_call(): pl.pallas_call(functools.partial(first_kernel, dims), in_specs=[smem] * 3...  202 us
    pallas_call x1, Pallas kernels, mlp_call(): pl.pallas_call(functools.partial(mlp_kernel, dims), in_specs=[any_spec] *...  180 us
    unnamed x19, local copies, waits for them, and re-layouts  14.7 us

profile of v6, /device:TPU:0, one launch (start us, length us, event | category | flops | bytes accessed | tf_op | source)
XLA Modules:
  0.0 711.6 jit_solution(7115882749184977066)
XLA Ops:
  1.3 0.7 fusion.11.place_s
  2.0 0.0 copy-start.4
  2.0 0.1 select_reduce_fusion.at_s
  2.1 0.7 stack.9
  2.7 0.7 stack.10
  3.4 0.6 fusion.10.gains_in
  4.0 0.1 convert_bitcast_fusion
  4.1 9.2 %fusion.2 = (f32[2048,128]{1,0:T(8,128)}, f32[2048,128]{1,0:T(8,128)}, f32[2048,128]{1,0:T(8,128)}, f32[2048,128]{1,0:T(8,128)}) fusion(f32[128]{0:T(128)S(1)} %get-tuple-element.109, f32[128]{0:T(128)S(1)} %get-tuple-element.110, f32[2048]{0:T(1024)S(1)} %convert_bitcast_fusion), kind=kLoop, calls=%fused_computation.9 | loop fusion | flops 1048576 | bytes 4203520 | tf_op jit(solution)/shard_map/mul | solution.py:1726
  13.3 201.7 %first.1 = (bf16[2048,2048]{1,0:T(8,128)(2,1)}, bf16[2048,768]{1,0:T(8,128)(2,1)}, bf16[2,2048,1024]{2,1,0:T(8,128)(2,1)}, bf16[2048,2048]{1,0:T(8,128)(2,1)}, b...) custom-call(s32[16]{0:T(128)} %copy-done.4, ...), custom_call_target="tpu_custom_call" | custom-call | flops 8589934592 | bytes 67108864 | tf_op jit(solution)/shard_map/first/pallas_call | solution.py:539
  215.0 179.9 %feed_forward.1 = (bf16[2048,2048]{1,0:T(8,128)(2,1)}, bf16[2048,2048]{1,0:T(8,128)(2,1)}, f32[2,768,256]{2,1,0:T(8,128)}, bf16[2,768,256]{2,1,0:T(8,128)(2,1)},...) custom-call(bf16[2048,2048]{1,0:T(8,128)(2,1)} %get-tuple-element.40.n_in, ...), custom_call_target="tpu_custom_call" | custom-call | flops 77309411328 | bytes 104857600 | tf_op jit(solution)/shard_map/feed_forward/pallas_call | solution.py:982
  394.8 0.0 copy-start.3
  394.8 290.1 %last.1 = (bf16[1024,2048]{1,0:T(8,128)(2,1)}, bf16[1024,2048]{1,0:T(8,128)(2,1)}, f32[256,256]{1,0:T(8,128)}, bf16[256,256]{1,0:T(8,128)(2,1)}, f32[768,256]{1,...) custom-call(s32[16]{0:T(128)} %copy-done.4, ...), custom_call_target="tpu_custom_call" | custom-call | flops 17179869184 | bytes 67108864 | tf_op jit(solution)/shard_map/last/pallas_call | solution.py:1631
  684.9 1.3 fusion.20
  686.3 0.9 convert_element_type.39
  687.2 0.0 copy-start.2
  687.2 1.9 maximum_select_fusion.6
  689.2 1.3 pad_maximum_fusion.1
  690.5 0.1 fusion.18
  690.6 0.1 fusion.19
  690.7 1.0 copy.31
  691.7 1.0 copy.30
  692.8 1.0 copy.29
  693.8 2.1 pad_maximum_fusion
  695.9 0.2 fusion.16
  696.1 0.3 fusion.17
  696.4 1.6 maximum_select_fusion.2
  698.0 0.2 fusion.1
  698.2 1.6 fusion
  699.8 2.9 copy.32
  702.7 1.8 copy.33
  704.5 4.9 copy.37
  709.4 2.0 copy.38
  (14 shorter events, 0.1 us)
Async XLA Ops:
  2.0 11.3 %copy-start.4 = (s32[16]{0:T(128)}, s32[16]{0:T(128)S(1)}, u32[]{:S(2)}) copy-start(s32[16]{0:T(128)S(1)} %fusion.11.place_s) | copy-start | bytes 196
  2.1 11.2 %copy-start.5 = (s32[16]{0:T(128)}, s32[16]{0:T(128)S(1)}, u32[]{:S(2)}) copy-start(s32[16]{0:T(128)S(1)} %select_reduce_fusion.at_s) | copy-start | bytes 196
  394.8 294.3 %copy-start.3 = (bf16[2,768,256]{2,1,0:T(8,128)(2,1)S(1)}, bf16[2,768,256]{2,1,0:T(8,128)(2,1)}, u32[]{:S(2)}) copy-start(bf16[2,768,256]{2,1,0:T(8,128)(2,1)} %get-tuple-element.67) | copy-start | bytes 2359300
  687.2 3.3 copy-start.2
  689.2 1.4 copy-start.1
  704.5 4.9 copy-start

commit v7 on v6

--- a/solution.py
+++ b/solution.py
@@ -247,7 +247,7 @@
 def first_kernel(
     dims, place_s, at_s, live_s, tokens, cotangent, gains_in, wq, wk, wv, w_out, wg, wu, wd, cos_ref, sin_ref,
     n_one_out, w_qkv_out, w_o_out, cot_out, gu_out, d_out, n_all, h_out, gains, qs, ks, vs, os, stats, o_rel,
-    n_one, w_qkv, w_o, qkv_rel, attn_rows, h_own, n_own, x_keep, gu_v, d_v,
+    n_one, w_qkv, w_o, qkv_rel, attn_rows, h_own, n_own, x_keep, gu_v, d_v, cos_v, sin_v,
     send_sems, recv_sems, own_sems,
 ):
     shards, ctx, tensor, fc, own_rows, d_own = dims
@@ -377,6 +377,14 @@
         return carry
 
     next(qkv_chain, None)
+
+    def tables(j, carry):
+        dst = pl.ds(pl.multiple_of(j * BLK, BLK), BLK)
+        cos_v[dst, :] = picked(cos_ref, at_s[j])
+        sin_v[dst, :] = picked(sin_ref, at_s[j])
+        return carry
+
+    lax.fori_loop(0, rows // BLK, tables, 0)
     lax.fori_loop(0, tensor, norm, 0)
     next(tok_rows, None)
     next(qkv_chain, None)
@@ -401,7 +409,7 @@
         per = own_rows // BLK
         for i in range(per):
             where = pl.ds(pl.multiple_of(r * own_rows + i * BLK, BLK), BLK)
-            cos, sin = wide(cos_ref[where, :], cols), wide(sin_ref[where, :], cols)
+            cos, sin = wide(cos_v[where, :], cols), wide(sin_v[where, :], cols)
             part = lin[i * BLK : (i + 1) * BLK, :]
             dst = pl.ds(pl.multiple_of(r * own_rows + i * BLK, BLK), BLK)
             qkv_rel[dst, 0:cols] = turn(part[:, 0:cols], cos, sin).astype(BF)
@@ -568,6 +576,8 @@
             pltpu.VMEM((own_rows, width), BF),
             pltpu.VMEM((PRE, width, 2 * fc), BF),
             pltpu.VMEM((PRE * fc, width), BF),
+            pltpu.VMEM((rows, 128), F32),
+            pltpu.VMEM((rows, 128), F32),
             dma((moves,)),
             dma((moves,)),
             dma((40,)),
@@ -1232,6 +1242,7 @@
         own(h_in.at[:, j * cols : (j + 1) * cols], dq.at[j * own_rows : (j + 1) * own_rows, :]) for j in range(width // cols)
     ]
     load_cot = own(cot_in.at[mine(), :], stage_own)
+    load_left = own(o_rel_in, d_rel.at[:, 0:cols])
     load_o = own(w_o_in, big)
     load_w = own(w_qkv_in, w_qkv)
     core_out = [links.send(out_part.at[block(k), :], o_land.at[k // 2], p.peer_id(1), start=False) for k in odd]
@@ -1245,6 +1256,9 @@
     for m in core_out:
         m.start()
     load_gain.wait()
+    load_left.wait()
+    for k in range(group):
+        left_o[:, k * own_rows : (k + 1) * own_rows] = d_rel[k * own_rows : (k + 1) * own_rows, 0:cols].T
     for _ in sums:
         pass
 
@@ -1272,8 +1286,7 @@
         for j, (_, c) in enumerate(spans):
             dq[j * own_rows + r * per : j * own_rows + (r + 1) * per, :] = d_h[:, c]
     keep_dh = [own(dq.at[a, :], dh_keep.at[:, c]) for a, c in spans]
-    own(dh_low, dh_all.at[block(0), :]).wait()
-    next(late_steps, None)
+    copy_dh = own(dh_low, dh_all.at[block(0), :])
 
     def dh_part(k, h):
         if h is None:
@@ -1282,13 +1295,14 @@
 
     load_o.wait()
     wo_rows = width // tensor
+    lefts = [
+        jnp.concatenate([dh_low[:, (zz * ctx + xx) * d_own : (zz * ctx + xx + 1) * d_own] for zz in range(shards)], axis=1)
+        for xx in range(ctx)
+    ]
     for tt in range(tensor):
         acc = jnp.zeros((own_rows, wo_rows), F32)
         for xx in range(ctx):
-            left = jnp.concatenate(
-                [dh_low[:, (zz * ctx + xx) * d_own : (zz * ctx + xx + 1) * d_own] for zz in range(shards)], axis=1
-            )
-            acc = acc + mm(left, big[xx * width + tt * wo_rows : xx * width + (tt + 1) * wo_rows, :], NT)
+            acc = acc + mm(lefts[xx], big[xx * width + tt * wo_rows : xx * width + (tt + 1) * wo_rows, :], NT)
         stage_own[:, tt * wo_rows : (tt + 1) * wo_rows] = acc.astype(BF)
 
     def heads_of(k):
@@ -1297,9 +1311,9 @@
 
     swaps = [links.send(heads_of(k), go_rel.at[block(k), :], p.peer_id(k)) for k in range(1, group)]
     own_heads = own(heads_of(0), go_rel.at[block(0), :])
+    copy_dh.wait()
     dh_rows = links.spread(dh_part)
     next(dh_rows)
-    load_left = own(o_rel_in, d_rel.at[:, 0:cols])
     load_tok = own(tokens.at[mine(), :], dh_low)
 
     def output():
@@ -1342,6 +1356,7 @@
             m.come()
 
     next(late_steps, None)
+    next(late_steps, None)
     own_heads.wait()
     for m in swaps:
         m.come()
@@ -1355,17 +1370,16 @@
 
     lax.fori_loop(0, rows // BLK, fill, 0)
     load_os = own(os_in, go_rel)
-    load_left.wait()
-    for k in range(group):
-        left_o[:, k * own_rows : (k + 1) * own_rows] = d_rel[k * own_rows : (k + 1) * own_rows, 0:cols].T
     load_os.wait()
     head_row = lax.broadcasted_iota(jnp.int32, (8, cols), 0)
     head_col = lax.broadcasted_iota(jnp.int32, (8, cols), 1) // HDIM
-    pick = jnp.where(head_row == head_col, 1.0, 0.0)
+    pick = jnp.where(head_row == head_col, 1.0, 0.0).astype(BF)
     for i in range(rows // QT):
         part = slice(i * QT, (i + 1) * QT)
         both = go[part, :].astype(F32) * go_rel[part, :].astype(F32)
-        delta[:, part] = lax.dot_general(pick, both, NT, precision=lax.Precision.HIGHEST, preferred_element_type=F32)
+        coarse = both.astype(BF)
+        fine = (both - coarse.astype(F32)).astype(BF)
+        delta[:, part] = mm(pick, coarse, NT) + mm(pick, fine, NT)
     for c in keep_dh:
         c.wait()
     dq[...] = jnp.zeros_like(dq)
@@ -1525,7 +1539,6 @@
         for c in quarters:
             chip[i, :, c] = d_n_one(k, c).astype(BF)
         core.append(links.send(chip.at[i], c_land.at[i], p.peer_id(1)))
-    next(o_steps, None)
     for k in range(group):
         left_w[:, k * own_rows : (k + 1) * own_rows] = d_rel[k * own_rows : (k + 1) * own_rows, :].T
     for c in load_n:
@@ -1539,13 +1552,15 @@
 
     def grad_w(i):
         d = far_first(i)
-        for i in range(3):
-            at = slice(i * cols, (i + 1) * cols)
+        for j in range(3):
+            at = slice(j * cols, (j + 1) * cols)
             g_w[d, at, :] = mm(left_w[at, :], n_block(d)).astype(BF)
 
     grad_w(0)
     next(w_steps)
-    grad_w(1)
+    for i in range(1, shards):
+        grad_w(i)
+    next(o_steps, None)
     for i in range(group // 2):
         core[i].sent()
         done_moves.append(core[i])
@@ -1555,11 +1570,9 @@
     sums = halves(parts_land)
     next(sums)
     next(w_steps, None)
-    for i in range(2, shards):
-        grad_w(i)
-        if i < shards - 1:
-            next(w_steps, None)
-    next(o_steps, None)
+    next(sums)
+    next(w_steps, None)
+    drain(o_steps)
     for _ in sums:
         pass
     for c in load_dh:
@@ -1597,7 +1610,7 @@
         total = total + g_chain[b]
     g_land[0] = total
     own(g_land.at[0, :, pl.ds(pl.multiple_of((z * ctx + x) * d_own, d_own), d_own)], gain_out).wait()
-    drain(o_steps, x_steps, w_steps)
+    drain(x_steps, w_steps)
     for m in links.moves:
         if m not in done_moves:
             m.sent()
@@ -1720,14 +1733,10 @@
     angles = angle_at[:, None] * freqs[None, :]
     cos = jnp.cos(angles)
     sin = jnp.sin(angles) * jnp.where(lane % HDIM < HDIM // 2, -1.0, 1.0)
-    at_pos = (at[:, None] * BLK + jnp.arange(BLK)[None, :]).reshape(-1).astype(F32)
-    angles = at_pos[:, None] * freqs[None, :]
-    cos_rel = jnp.cos(angles)
-    sin_rel = jnp.sin(angles) * jnp.where(lane % HDIM < HDIM // 2, -1.0, 1.0)
     gains = jnp.concatenate([jnp.stack([attn_gain, mlp_gain], axis=0).astype(F32), jnp.zeros((6, d_own), F32)], axis=0)
     n_one, w_qkv, w_o, cot, gu_pre, d_pre, n_two_own, hidden_res, gains, qs, ks, vs, os, stats, o_slot = first_call(
         shards, ctx, tensor, place.astype(jnp.int32), at, seq_len, tokens, cotangent, gains,
-        w_query, w_key, w_value, w_out, w_gate, w_up, w_down, cos_rel, sin_rel,
+        w_query, w_key, w_value, w_out, w_gate, w_up, w_down, cos, sin,
     )
     dn_part, out_part, ff_mine, ff_got, g_late, _ = mlp_call(
         shards, ctx, tensor, n_two_own, cot, cotangent, w_gate, w_up, w_down, gu_pre, d_pre

time: 721 us -> 710 us (0.985)
    unnamed x19 -> x17, local copies, waits for them, and re-layouts: 14.7 us -> 14.6 us
where the time goes in v7:
time: 710 us; the launch traced here: 701 us
  Pallas kernels  665 us (94%)
  local copies, waits for them, and re-layouts  17.9 us (3%)
  other arithmetic  16.4 us (2%)
    pallas_call x1, Pallas kernels, last_call(): pl.pallas_call(functools.partial(last_kernel, dims), in_specs=[smem] * 3...  283 us
    pallas_call x1, Pallas kernels, first_call(): pl.pallas_call(functools.partial(first_kernel, dims), in_specs=[smem] * 3...  202 us
    pallas_call x1, Pallas kernels, mlp_call(): pl.pallas_call(functools.partial(mlp_kernel, dims), in_specs=[any_spec] *...  180 us
    unnamed x17, local copies, waits for them, and re-layouts  14.6 us

profile of v7, /device:TPU:0, one launch (start us, length us, event | category | flops | bytes accessed | tf_op | source)
XLA Modules:
  0.0 701.0 jit_solution(8363212768124315309)
XLA Ops:
  1.3 0.7 fusion.10.place_s
  2.0 0.0 copy-start.4
  2.0 0.6 select_reduce_fusion.at_s
  2.6 0.7 stack.9
  3.2 0.7 stack.10
  3.9 0.6 fusion.9.gains_in
  4.5 4.8 sine_multiply_fusion
  9.3 0.0 copy-done.4
  9.3 201.6 %first.1 = (bf16[2048,2048]{1,0:T(8,128)(2,1)}, bf16[2048,768]{1,0:T(8,128)(2,1)}, bf16[2,2048,1024]{2,1,0:T(8,128)(2,1)}, bf16[2048,2048]{1,0:T(8,128)(2,1)}, b...) custom-call(s32[16]{0:T(128)} %copy-done.4, ...), custom_call_target="tpu_custom_call" | custom-call | flops 8589934592 | bytes 67108864 | tf_op jit(solution)/shard_map/first/pallas_call | solution.py:547
  210.9 179.9 %feed_forward.1 = (bf16[2048,2048]{1,0:T(8,128)(2,1)}, bf16[2048,2048]{1,0:T(8,128)(2,1)}, f32[2,768,256]{2,1,0:T(8,128)}, bf16[2,768,256]{2,1,0:T(8,128)(2,1)},...) custom-call(bf16[2048,2048]{1,0:T(8,128)(2,1)} %get-tuple-element.40.n_in, ...), custom_call_target="tpu_custom_call" | custom-call | flops 77309411328 | bytes 104857600 | tf_op jit(solution)/shard_map/feed_forward/pallas_call | solution.py:992
  390.8 0.0 copy-start.3
  390.8 283.3 %last.1 = (bf16[1024,2048]{1,0:T(8,128)(2,1)}, bf16[1024,2048]{1,0:T(8,128)(2,1)}, f32[256,256]{1,0:T(8,128)}, bf16[256,256]{1,0:T(8,128)(2,1)}, f32[768,256]{1,...) custom-call(s32[16]{0:T(128)} %copy-done.4, ...), custom_call_target="tpu_custom_call" | custom-call | flops 17179869184 | bytes 67108864 | tf_op jit(solution)/shard_map/last/pallas_call | solution.py:1644
  674.1 1.3 fusion.19
  675.4 0.9 convert_element_type.29
  676.3 1.9 maximum_select_fusion.6
  678.3 1.3 pad_maximum_fusion.1
  679.6 0.0 copy-done.2
  679.6 0.1 fusion.17
  679.7 0.1 fusion.18
  679.8 1.0 copy.31
  680.9 1.0 copy.30
  681.9 1.0 copy.29
  682.9 2.1 pad_maximum_fusion
  685.0 0.2 fusion.15
  685.2 0.3 fusion.16
  685.5 1.6 maximum_select_fusion.2
  687.1 0.2 fusion.1
  687.3 1.6 fusion
  688.9 2.9 copy.32
  691.8 1.8 copy.33
  693.6 4.9 copy.37
  698.5 2.0 copy.38
  (10 shorter events, 0.1 us)
Async XLA Ops:
  2.0 7.3 %copy-start.4 = (s32[16]{0:T(128)}, s32[16]{0:T(128)S(1)}, u32[]{:S(2)}) copy-start(s32[16]{0:T(128)S(1)} %fusion.10.place_s) | copy-start | bytes 196
  390.8 287.5 %copy-start.3 = (bf16[2,768,256]{2,1,0:T(8,128)(2,1)S(1)}, bf16[2,768,256]{2,1,0:T(8,128)(2,1)}, u32[]{:S(2)}) copy-start(bf16[2,768,256]{2,1,0:T(8,128)(2,1)} %get-tuple-element.67) | copy-start | bytes 2359300
  676.3 3.3 copy-start.2
  678.3 1.4 copy-start.1
  693.6 4.9 copy-start
